TPU v7x, 32 devices: a whole 2x2x4 slice. The times are simulated.
32 devices in a mesh: row: 4 (over y, core), col: 8 (over z, x).
Axes of the slice: x: 2, y: 2, z: 4, core: 2. Of those that a mesh axis runs over, the one named last changes fastest.
Arguments:
- features: bfloat16 [262144, 400], P(('row', 'col')), may hold values from -110 to 110
- labels: int32 [262144], P(('row', 'col')), may hold values from 0 to 46
- counts: int32 [4, 8], replicated, may hold values from 1 to 8192, as said below
- w_branch: float32 [4, 100, 512], replicated, may hold values from -0.625 to 0.625
- w_mid: float32 [2048, 512], P(('row', 'col')), may hold values from -0.125 to 0.125
- w_out: float32 [512, 47], replicated, may hold values from -0.25 to 0.25
- left_branch: float32 [4, 100, 100], replicated, may hold values from -5.9604645e-08 to 5.9604645e-08
- right_branch: float32 [4, 512, 512], replicated, may hold values from -1.1175871e-08 to 1.1175871e-08
- basis_left_branch: float32 [4, 100, 100], replicated, may hold values from -1 to 1, as said below
- basis_right_branch: float32 [4, 512, 512], replicated, may hold values from -1 to 1, as said below
- first_branch: float32 [4, 100, 512], replicated, may hold values from -0.00012207031 to 0.00012207031
- second_branch: float32 [4, 100, 512], replicated, may hold values from 2.0599366e-11 to 3.3569336e-10
- right_mid: float32 [512, 512], replicated, may hold values from -4.7683716e-06 to 4.7683716e-06
- basis_right_mid: float32 [512, 512], replicated, may hold values from -1 to 1, as said below
- first_mid: float32 [2048, 512], P(('row', 'col')), may hold values from -0.00048828125 to 0.00048828125
- second_mid: float32 [2048, 512], P(('row', 'col')), may hold values from 3.8146972e-10 to 6.1035155e-09
- left_out: float32 [512, 512], replicated, may hold values from -9.536743e-07 to 9.536743e-07
- right_out: float32 [47, 47], replicated, may hold values from -9.536743e-06 to 9.536743e-06
- basis_left_out: float32 [512, 512], replicated, may hold values from -1 to 1, as said below
- basis_right_out: float32 [47, 47], replicated, may hold values from -1 to 1, as said below
- first_out: float32 [512, 47], replicated, may hold values from -0.0014648438 to 0.0014648438
- second_out: float32 [512, 47], replicated, may hold values from 3.4332275e-09 to 5.493164e-08
Outputs:
- logits: float32 [131072, 47], P(('row', 'col'))
- grad_features: bfloat16 [262144, 400], P(('row', 'col'))
- new_left_branch: float32 [4, 100, 100], replicated
- new_right_branch: float32 [4, 512, 512], replicated
- new_first_branch: float32 [4, 100, 512], replicated
- new_second_branch: float32 [4, 100, 512], replicated
- new_w_branch: float32 [4, 100, 512], replicated
- low_w_branch: bfloat16 [4, 100, 512], replicated
- new_right_mid: float32 [512, 512], replicated
- new_first_mid: float32 [2048, 512], P(('row', 'col'))
- new_second_mid: float32 [2048, 512], P(('row', 'col'))
- new_w_mid: float32 [2048, 512], P(('row', 'col'))
- low_w_mid: bfloat16 [2048, 512], P(('row', 'col'))
- new_left_out: float32 [512, 512], replicated
- new_right_out: float32 [47, 47], replicated
- new_first_out: float32 [512, 47], replicated
- new_second_out: float32 [512, 47], replicated
- new_w_out: float32 [512, 47], replicated
- low_w_out: bfloat16 [512, 47], replicated
Inputs may be any that keep to these rules, and one draw needn't show every extreme that they name: `counts`: each row sums to 32768; exactly one entry of each row equals 8192. `basis_left_branch`: each matrix is orthogonal. `basis_right_branch`: each matrix is orthogonal. `basis_right_mid`: orthogonal. `basis_left_out`: orthogonal. `basis_right_out`: orthogonal.
All inputs are finite; a program needn't handle non-finite values.
Results may differ from a plain program's by a relative error of at most 0.0089.
Values may be sent and summed in bfloat16 or wider, within the bound.
No kernel may reach another device: no remote copies, remote signals or barrier semaphores. Data moves between devices by JAX's collectives and lax.ppermute only.
A program may use at most 320 MiB of HBM per device.

v0:
```python
import functools

import jax
import jax.numpy as jnp
from jax import lax
from jax.experimental import pallas as pl
from jax.experimental.pallas import tpu as pltpu
from jax.sharding import PartitionSpec as P

OPS = 4
DIN = 100
HID = 512
CLS = 47
AVG = 4096
STEP = 5
CAT = 2048
LANE = 128
CPAD = 48
STRIDE = 96
WINDOW = 112
VALID = 400
HEAD = 512
WIDE = 416
SHARE = 12
BOTH = ("row", "col")

beta_first = 0.5
beta_second = 0.9
beta_factor = 0.95
adam_eps = 1e-08
norm_eps = 1e-05
rate_branch = 0.1
rate_mid = 0.02
rate_out = 0.04
f32 = jnp.float32
bf16 = jnp.bfloat16
VMEM_LIMIT = 60 * 2**20


def dot_on(first_arg, second_arg, first_dim, second_dim, precision=None):
    return lax.dot_general(
        first_arg,
        second_arg,
        (((first_dim,), (second_dim,)), ((), ())),
        precision=precision,
        preferred_element_type=f32,
    )


def params():
    return pltpu.CompilerParams(vmem_limit_bytes=VMEM_LIMIT)


def cost(microseconds):
    return pl.CostEstimate(
        flops=int(microseconds * 1e9), bytes_accessed=1, transcendentals=0
    )


def shape(dims, dtype):
    return jax.ShapeDtypeStruct(dims, dtype)


def fixed(dims):
    return pl.BlockSpec(dims, lambda *_: (0,) * len(dims))


def rows_of(block, width):
    return pl.BlockSpec((block, width), lambda i, *_: (i, 0))


def columns_of(height, block):
    return pl.BlockSpec((height, block), lambda i, *_: (0, i))


def low_f32(values):
    return values.astype(bf16).astype(f32)


def split_low(values):
    high = values.astype(bf16)
    return high, (values - high.astype(f32)).astype(bf16)


def fold_rows(values):
    return jnp.sum(values.reshape(values.shape[0] // 8, 8, values.shape[1]), axis=0)


def add_up(ref):
    value = ref[0]
    for index in range(1, ref.shape[0]):
        value = value + ref[index]
    return value


def own_count(counts):
    return counts[lax.axis_index("row"), lax.axis_index("col")]


def branch_scale(stats, op, all_rows):
    mean = stats[op : op + 1, :] / all_rows
    square = stats[OPS + op : OPS + op + 1, :] / all_rows
    return mean, lax.rsqrt(square - mean * mean + norm_eps)


def unpack_pair(packed):
    parts = HID // LANE
    return [
        jnp.concatenate(
            [packed[index * parts + part : index * parts + part + 1, :] for part in range(parts)],
            axis=1,
        )
        for index in range(2)
    ]


def pack_pair(first, second):
    parts = HID // LANE
    return jnp.concatenate(
        [
            value[:, part * LANE : (part + 1) * LANE]
            for value in (first, second)
            for part in range(parts)
        ],
        axis=0,
    )


def mid_scale(stats_ref, all_rows):
    total, square = unpack_pair(add_up(stats_ref))
    mean = total / all_rows
    return mean, lax.rsqrt(square / all_rows - mean * mean + norm_eps)


def window_rows(x_ref, op):
    return jnp.concatenate(
        [x_ref[op * STRIDE : op * STRIDE + WINDOW, :], x_ref[VALID:WIDE, :]], axis=0
    )


def padded(window):
    return jnp.concatenate([window, jnp.zeros((LANE - WINDOW, HID), bf16)], axis=0)


def gram_product(gram, window):
    high, low = split_low(gram)
    weight = padded(window)
    return jnp.dot(high, weight, preferred_element_type=f32) + jnp.dot(
        low, weight, preferred_element_type=f32
    )


def mask_rows(counts, x_ref, held):
    block = x_ref.shape[1]
    column = pl.program_id(0) * block + lax.broadcasted_iota(jnp.int32, (16, block), 1)
    valid = jnp.where(column < own_count(counts), 1.0, 0.0)
    line = lax.broadcasted_iota(jnp.int32, (16, block), 0)
    held[:VALID, :] = x_ref[...] * valid[0:1, :].astype(bf16)
    held[VALID:, :] = jnp.where(line < 2, valid, 0.0).astype(bf16)


def gather_pieces(refs, held):
    row = lax.axis_index("row")
    size = held.shape[0] // len(refs)
    for index, ref in enumerate(refs):
        at = pl.multiple_of((row ^ index) * size, size)
        held[pl.ds(at, size), :] = ref[...].reshape(size, held.shape[1]).astype(held.dtype)


def gram_body(counts, x_ref, w_ref, window_ref, gram_ref, stats_ref, xa_ref):
    step = pl.program_id(0)

    @pl.when(step == 0)
    def _():
        gram_ref[...] = jnp.zeros_like(gram_ref)
        for op in range(OPS):
            shift = op * (DIN - STRIDE)
            parts = [low_f32(w_ref[:, op, :])]
            if shift:
                parts.insert(0, jnp.zeros((shift, HID), f32))
            if WINDOW - DIN - shift:
                parts.append(jnp.zeros((WINDOW - DIN - shift, HID), f32))
            window_ref[op] = jnp.concatenate(parts, axis=0).astype(bf16)

    mask_rows(counts, x_ref, xa_ref)
    for op in range(0, OPS, 2):
        rows = jnp.concatenate([window_rows(xa_ref, op), window_rows(xa_ref, op + 1)], axis=0)
        both = dot_on(rows, rows, 1, 1)
        gram_ref[op] += both[:LANE, :LANE]
        gram_ref[op + 1] += both[LANE:, LANE:]

    @pl.when(step == pl.num_programs(0) - 1)
    def _():
        for op in range(OPS):
            turned = gram_product(gram_ref[op], window_ref[op])
            stats_ref[op : op + 1, :] = turned[WINDOW : WINDOW + 1, :]
            stats_ref[OPS + op : OPS + op + 1, :] = jnp.sum(
                window_ref[op].astype(f32) * turned[:WINDOW, :], axis=0, keepdims=True
            )


def gram_call(counts, features, w_branch, block):
    total = features.shape[1]
    return pl.pallas_call(
        gram_body,
        grid_spec=pltpu.PrefetchScalarGridSpec(
            num_scalar_prefetch=1,
            grid=(total // block,),
            in_specs=[columns_of(VALID, block), fixed((DIN, OPS, HID))],
            out_specs=[
                fixed((OPS, WINDOW, HID)),
                fixed((OPS, LANE, LANE)),
                fixed((2 * OPS, HID)),
            ],
            scratch_shapes=[pltpu.VMEM((WIDE, block), bf16)],
        ),
        out_shape=[
            shape((OPS, WINDOW, HID), bf16),
            shape((OPS, LANE, LANE), f32),
            shape((2 * OPS, HID), f32),
        ],
        compiler_params=params(),
        cost_estimate=cost(6),
        name="row_moments",
    )(counts, features, w_branch)


def forward_body(all_rows, count, counts, *refs):
    x_ref, stats_ref, window_ref = refs[:3]
    pieces = refs[3 : 3 + count]
    pre_ref, joined_ref, slope_ref, wm_ref, out_ref, wide, total, xa_ref = refs[3 + count :]
    step = pl.program_id(0)

    @pl.when(step == 0)
    def _():
        total[...] = jnp.zeros_like(total)
        gather_pieces(pieces, wm_ref)
        stats = add_up(stats_ref)
        line = lax.broadcasted_iota(jnp.int32, (LANE - WINDOW, HID), 0)
        for op in range(OPS):
            mean, scale = branch_scale(stats, op, all_rows)
            half = 0.5 * scale
            high, low = split_low(window_ref[op].astype(f32) * half)
            base = -mean * half
            base_high = low_f32(base)
            wide[op, :WINDOW, :] = high
            wide[op, WINDOW:LANE, :] = jnp.where(
                line == 0, base_high, jnp.where(line == 1, base - base_high, 0.0)
            ).astype(bf16)
            wide[op, LANE : LANE + WINDOW, :] = low
            wide[op, LANE + WINDOW :, :] = jnp.zeros((LANE - WINDOW, HID), bf16)

    mask_rows(counts, x_ref, xa_ref)
    pre = None
    for op in range(OPS):
        rows = window_rows(xa_ref, op).T
        half = jnp.dot(
            jnp.concatenate([rows, rows], axis=1), wide[op], preferred_element_type=f32
        ).astype(bf16)
        first = jnp.tanh(half) + 1.0
        act = half * first
        half_act = act * 0.5
        second = jnp.tanh(half_act) + 1.0
        joined = half_act * second
        slope = (first * ((half - half_act) + 0.5)) * (second * ((act - joined) + 1.0))
        joined_ref[:, op * HID : (op + 1) * HID] = joined
        slope_ref[:, op * HID : (op + 1) * HID] = slope
        term = jnp.dot(
            joined, wm_ref[op * HID : (op + 1) * HID, :], preferred_element_type=f32
        )
        pre = term if pre is None else pre + term
    pre_ref[...] = pre.astype(bf16)
    total[0] += fold_rows(pre)
    total[1] += fold_rows(pre * pre)

    @pl.when(step == pl.num_programs(0) - 1)
    def _():
        packed = pack_pair(
            jnp.sum(total[0], axis=0, keepdims=True), jnp.sum(total[1], axis=0, keepdims=True)
        )
        for index in range(out_ref.shape[0]):
            out_ref[index] = packed


def forward_call(all_rows, devices, counts, features, stats, window, pieces, block):
    total = features.shape[1]
    count = len(pieces)
    return pl.pallas_call(
        functools.partial(forward_body, all_rows, count),
        grid_spec=pltpu.PrefetchScalarGridSpec(
            num_scalar_prefetch=1,
            grid=(total // block,),
            in_specs=[
                columns_of(VALID, block),
                fixed(stats.shape),
                fixed((OPS, WINDOW, HID)),
            ]
            + [fixed(piece.shape) for piece in pieces],
            out_specs=[
                rows_of(block, HID),
                rows_of(block, CAT),
                rows_of(block, CAT),
                fixed((CAT, HID)),
                fixed((devices, 8, LANE)),
            ],
            scratch_shapes=[
                pltpu.VMEM((OPS, 2 * LANE, HID), bf16),
                pltpu.VMEM((2, 8, HID), f32),
                pltpu.VMEM((WIDE, block), bf16),
            ],
        ),
        out_shape=[
            shape((total, HID), bf16),
            shape((total, CAT), bf16),
            shape((total, CAT), bf16),
            shape((CAT, HID), bf16),
            shape((devices, 8, LANE), f32),
        ],
        compiler_params=params(),
        cost_estimate=cost(44),
        name="forward_layers",
    )(counts, features, stats, window, *pieces)


def head_body(
    all_rows,
    counts,
    pre_ref,
    stats_ref,
    wo_ref,
    labels_ref,
    back_ref,
    logits_ref,
    grad_ref,
    sums_ref,
    wo_low,
    norm,
    total,
):
    step = pl.program_id(0)
    block = pre_ref.shape[0]

    @pl.when(step == 0)
    def _():
        total[...] = jnp.zeros_like(total)
        grad_ref[...] = jnp.zeros_like(grad_ref)
        wo_low[...] = jnp.concatenate(
            [wo_ref[...], jnp.zeros((CPAD - CLS, HID), f32)], axis=0
        ).astype(bf16)
        mean, scale = mid_scale(stats_ref, all_rows)
        norm[0:1, :] = 0.5 * scale
        norm[1:2, :] = -0.5 * scale * mean

    kind = lax.broadcasted_iota(jnp.int32, (CPAD, HEAD), 0)
    for start in range(0, block, HEAD):
        rows = slice(start, start + HEAD)
        half = pre_ref[rows, :].astype(f32) * norm[0:1, :] + norm[1:2, :]
        raised = jnp.tanh(half) + 1.0
        hidden = half * raised
        slope = raised * ((half - 0.5 * hidden) + 0.5)
        hidden = hidden.astype(bf16)
        logits = dot_on(wo_low[...], hidden, 1, 1)
        logits_ref[:, rows] = logits.astype(bf16)
        column = step * block + start + lax.broadcasted_iota(jnp.int32, (CPAD, HEAD), 1)
        real = kind < CLS
        top = jnp.max(jnp.where(real, logits, -jnp.inf), axis=0, keepdims=True)
        powers = jnp.where(real, jnp.exp(logits - top), 0.0)
        probs = powers / jnp.sum(powers, axis=0, keepdims=True)
        score = (probs - jnp.where(kind == labels_ref[:, rows], 1.0, 0.0)) / all_rows
        score = jnp.where(column < own_count(counts), score, 0.0).astype(bf16)
        grad_ref[...] += dot_on(score, hidden, 1, 0)
        back = dot_on(score, wo_low[...], 0, 0) * slope
        total[0] += fold_rows(back)
        total[1] += fold_rows(back * half)
        back_ref[rows, :] = back.astype(bf16)

    @pl.when(step == pl.num_programs(0) - 1)
    def _():
        packed = pack_pair(
            jnp.sum(total[0], axis=0, keepdims=True),
            2.0 * jnp.sum(total[1], axis=0, keepdims=True),
        )
        for index in range(sums_ref.shape[0]):
            sums_ref[index] = packed


def head_call(all_rows, counts, pre, stats, w_out, labels, block):
    total = pre.shape[0]
    return pl.pallas_call(
        functools.partial(head_body, all_rows),
        grid_spec=pltpu.PrefetchScalarGridSpec(
            num_scalar_prefetch=1,
            grid=(total // block,),
            in_specs=[
                rows_of(block, HID),
                fixed(stats.shape),
                fixed((CLS, HID)),
                columns_of(1, block),
            ],
            out_specs=[
                rows_of(block, HID),
                columns_of(CPAD, block),
                fixed((CPAD, HID)),
                fixed(stats.shape),
            ],
            scratch_shapes=[
                pltpu.VMEM((CPAD, HID), bf16),
                pltpu.VMEM((8, HID), f32),
                pltpu.VMEM((2, 8, HID), f32),
            ],
        ),
        out_shape=[
            shape((total, HID), bf16),
            shape((CPAD, total), bf16),
            shape((CPAD, HID), f32),
            shape(stats.shape, f32),
        ],
        compiler_params=params(),
        cost_estimate=cost(18),
        name="head",
    )(counts, pre, stats, w_out, labels)


def add_windows(pieces, write):
    for op, piece in enumerate(pieces):
        start = op * STRIDE
        skip = WINDOW - STRIDE if op else 0
        stop = WINDOW if op == OPS - 1 else STRIDE
        if op:
            write(start, pieces[op - 1][STRIDE:WINDOW, :] + piece[:skip, :])
        write(start + skip, piece[skip:stop, :])


def branch_back_body(
    all_rows,
    counts,
    pre_ref,
    back_ref,
    slope_ref,
    x_ref,
    wm_ref,
    window_ref,
    mid_stats_ref,
    sums_ref,
    stats_ref,
    grad_out_ref,
    gram_ref,
    mid_ref,
    part_ref,
    all_ref,
    norm,
    halved,
    grad,
    xa_ref,
):
    step = pl.program_id(0)

    @pl.when(step == 0)
    def _():
        grad[...] = jnp.zeros_like(grad)
        stats = add_up(stats_ref)
        for op in range(OPS):
            halved[op : op + 1, :] = 0.5 * branch_scale(stats, op, all_rows)[1]
        mean, scale = mid_scale(mid_stats_ref, all_rows)
        level, slant = unpack_pair(add_up(sums_ref))
        slant = scale * scale * (slant / all_rows)
        norm[0:1, :] = scale
        norm[1:2, :] = slant
        norm[2:3, :] = mean * slant - scale * (level / all_rows)

    mask_rows(counts, x_ref, xa_ref)
    mid = (
        back_ref[...].astype(f32) * norm[0:1, :]
        - pre_ref[...].astype(f32) * norm[1:2, :]
        + norm[2:3, :]
    ).astype(bf16)
    mid_ref[...] = mid
    pieces = []
    for op in range(OPS):
        span = slice(op * HID, (op + 1) * HID)
        joined_back = dot_on(mid, wm_ref[span, :], 1, 1)
        back = (
            (joined_back * halved[op : op + 1, :]) * slope_ref[:, span].astype(f32)
        ).astype(bf16)
        line = slice(op * LANE, (op + 1) * LANE)
        grad[line, :HID] += dot_on(window_rows(xa_ref, op), back, 1, 0)
        pieces.append(dot_on(window_ref[op], back, 1, 1))

    def write(at, value):
        part_ref[at : at + value.shape[0], :] = value.astype(bf16)

    add_windows(pieces, write)

    @pl.when(step == pl.num_programs(0) - 1)
    def _():
        for op in range(OPS):
            start = op * LANE
            grad[start : start + LANE, HID:] = gram_ref[op]
            grad[start : start + LANE, :HID] = jnp.concatenate(
                [
                    grad[start : start + WINDOW + 1, :HID],
                    grad_out_ref[op * SHARE : (op + 1) * SHARE, :],
                    jnp.zeros((LANE - WINDOW - 1 - SHARE, HID), f32),
                ],
                axis=0,
            )
        size = all_ref.shape[1]
        for index in range(all_ref.shape[0]):
            all_ref[index] = grad[index * size : (index + 1) * size, :].astype(bf16)


def branch_back_call(
    all_rows,
    devices,
    counts,
    pre,
    back,
    slope,
    features,
    mid_low,
    window,
    mid_stats,
    sums,
    stats,
    grad_out,
    gram,
    block,
):
    total = pre.shape[0]
    wide = HID + LANE
    parts = (devices, OPS * LANE // devices, wide)
    return pl.pallas_call(
        functools.partial(branch_back_body, all_rows),
        grid_spec=pltpu.PrefetchScalarGridSpec(
            num_scalar_prefetch=1,
            grid=(total // block,),
            in_specs=[
                rows_of(block, HID),
                rows_of(block, HID),
                rows_of(block, CAT),
                columns_of(VALID, block),
                fixed((CAT, HID)),
                fixed((OPS, WINDOW, HID)),
                fixed(mid_stats.shape),
                fixed(sums.shape),
                fixed(stats.shape),
                fixed((CPAD, HID)),
                fixed((OPS, LANE, LANE)),
            ],
            out_specs=[rows_of(block, HID), columns_of(VALID, block), fixed(parts)],
            scratch_shapes=[
                pltpu.VMEM((8, HID), f32),
                pltpu.VMEM((8, HID), f32),
                pltpu.VMEM((OPS * LANE, wide), f32),
                pltpu.VMEM((WIDE, block), bf16),
            ],
        ),
        out_shape=[shape((total, HID), bf16), shape((VALID, total), bf16), shape(parts, bf16)],
        compiler_params=params(),
        cost_estimate=cost(48),
        name="branch_back",
    )(counts, pre, back, slope, features, mid_low, window, mid_stats, sums, stats, grad_out, gram)


def mid_grad_body(mid_ref, joined_ref, *refs):
    step = pl.program_id(0)
    parts, grad = refs[:-1], refs[-1]

    @pl.when(step == 0)
    def _():
        grad[...] = jnp.zeros_like(grad)

    for op in range(OPS):
        span = slice(op * HID, (op + 1) * HID)
        grad[span, :] += dot_on(joined_ref[:, span], mid_ref[...], 0, 0)

    @pl.when(step == pl.num_programs(0) - 1)
    def _():
        groups = lax.axis_size("row")
        row = lax.axis_index("row")
        core, far = lax.rem(row, 2), row // (groups // 2)
        pairs, size = parts[0].shape[0], parts[0].shape[1]
        for index, part in enumerate(parts):
            which = core if index < 2 else 1 - core
            half = far if index % 2 == 0 else 1 - far
            for pair in range(pairs):
                chunk = 2 * (half * pairs + pair) + which
                part[pair] = grad[pl.ds(pl.multiple_of(chunk * size, size), size), :]


def mid_grad_call(groups, mid, joined, block):
    total = mid.shape[0]
    parted = (groups // 4, CAT // groups, HID)
    return pl.pallas_call(
        mid_grad_body,
        grid=(total // block,),
        in_specs=[rows_of(block, HID), rows_of(block, CAT)],
        out_specs=[fixed(parted)] * 4,
        out_shape=[shape(parted, f32)] * 4,
        scratch_shapes=[pltpu.VMEM((CAT, HID), f32)],
        compiler_params=params(),
        cost_estimate=cost(25),
        name="mid_grad",
    )(mid, joined)


def branch_terms(all_rows, mean, scale, window, raw):
    level = raw[WINDOW : WINDOW + 1, :]
    inner = scale * (
        jnp.sum(window.astype(f32) * raw[:WINDOW, :], axis=0, keepdims=True) - mean * level
    )
    return level / all_rows, scale * (inner / all_rows)


def rows_back_body(
    all_rows,
    counts,
    x_ref,
    part_ref,
    stats_ref,
    window_ref,
    grads,
    out_ref,
    inner,
    base,
):
    step = pl.program_id(0)
    block = x_ref.shape[1]

    @pl.when(step == 0)
    def _():
        stats = add_up(stats_ref)
        for op in range(OPS):
            mean, scale = branch_scale(stats, op, all_rows)
            window = window_ref[op]
            level, slant = branch_terms(
                all_rows, mean, scale, window, grads[op * LANE : (op + 1) * LANE, :HID].astype(f32)
            )
            inner[op] = dot_on((window.astype(f32) * -slant).astype(bf16), window, 1, 1).astype(bf16)
            base[op] = jnp.sum(
                window.astype(f32) * (mean * slant - level), axis=1, keepdims=True
            )

    moved = []
    for op in range(OPS):
        rows = x_ref[op * STRIDE : op * STRIDE + WINDOW, :]
        moved.append(jnp.dot(inner[op], rows, preferred_element_type=f32) + base[op])
    column = step * block + lax.broadcasted_iota(jnp.int32, (1, block), 1)
    valid = column < own_count(counts)

    def write(at, value):
        span = slice(at, at + value.shape[0])
        value = jnp.where(valid, value + part_ref[span, :].astype(f32), 0.0)
        out_ref[span, :] = value.astype(bf16)

    add_windows(moved, write)


def rows_back_call(all_rows, counts, features, part, stats, window, grads, block):
    total = features.shape[1]
    return pl.pallas_call(
        functools.partial(rows_back_body, all_rows),
        grid_spec=pltpu.PrefetchScalarGridSpec(
            num_scalar_prefetch=1,
            grid=(total // block,),
            in_specs=[
                columns_of(VALID, block),
                columns_of(VALID, block),
                fixed(stats.shape),
                fixed((OPS, WINDOW, HID)),
                fixed(grads.shape),
            ],
            out_specs=columns_of(VALID, block),
            scratch_shapes=[
                pltpu.VMEM((OPS, WINDOW, WINDOW), bf16),
                pltpu.VMEM((OPS, WINDOW, 1), f32),
            ],
        ),
        out_shape=shape((VALID, total), bf16),
        compiler_params=params(),
        cost_estimate=cost(8),
        name="rows_back",
    )(counts, features, part, stats, window, grads)


def slots_of(rows, peers):
    return -(-(rows // LANE + 1) // peers)


def first_row(counts, source):
    row = lax.axis_index("row")
    begin = jnp.int32(0)
    for peer in range(counts.shape[1]):
        begin += jnp.where(peer < source, counts[row, peer], 0)
    return begin


def deal_body(counts, logits_ref, out_ref):
    peers = out_ref.shape[0]
    tiles = logits_ref.shape[1] // LANE
    begin = first_row(counts, lax.axis_index("col"))
    count = own_count(counts)
    shift = lax.rem(begin, LANE)
    chunk = begin // LANE
    lane = lax.broadcasted_iota(jnp.int32, (CPAD, LANE), 1)
    empty = jnp.zeros((CPAD, LANE), f32)
    left = empty
    for tile in range(peers * (out_ref.shape[2] // LANE)):
        right = empty
        if tile < tiles:
            piece = logits_ref[:, tile * LANE : (tile + 1) * LANE].astype(f32)
            piece = jnp.where(tile * LANE + lane < count, piece, 0.0)
            right = pltpu.roll(piece, shift, 1)
        slot = tile // peers * LANE
        peer = lax.rem(chunk + tile, peers)
        out_ref[peer, :, slot : slot + LANE] = jnp.where(lane < shift, left, right).astype(bf16)
        left = right


def deal_call(counts, logits, peers):
    total = logits.shape[1]
    dealt = (peers, CPAD, slots_of(total, peers) * LANE)
    return pl.pallas_call(
        deal_body,
        grid_spec=pltpu.PrefetchScalarGridSpec(
            num_scalar_prefetch=1,
            grid=(1,),
            in_specs=[fixed((CPAD, total))],
            out_specs=fixed(dealt),
        ),
        out_shape=shape(dealt, bf16),
        compiler_params=params(),
        cost_estimate=cost(3),
        name="deal_logits",
    )(counts, logits)


def collect_body(counts, dealt_ref, out_ref, held):
    peers, _, width = dealt_ref.shape
    member = lax.axis_index("col")
    held[...] = jnp.zeros_like(held)
    for source in range(peers):
        chunk = first_row(counts, source) // LANE
        ahead = lax.rem(member + peers - lax.rem(chunk, peers), peers)
        at = pl.ds(pl.multiple_of((chunk + ahead) // peers * LANE, LANE), width)
        held[:, at] += dealt_ref[source].astype(f32)
    share = out_ref.shape[2]
    for peer in range(peers):
        out_ref[peer] = held[:, peer * share : (peer + 1) * share].astype(bf16)


def collect_call(counts, dealt):
    peers, height, width = dealt.shape
    collected = (peers, height, AVG // peers)
    return pl.pallas_call(
        collect_body,
        grid_spec=pltpu.PrefetchScalarGridSpec(
            num_scalar_prefetch=1,
            grid=(1,),
            in_specs=[fixed(dealt.shape)],
            out_specs=fixed(collected),
            scratch_shapes=[pltpu.VMEM((height, AVG + LANE + width), f32)],
        ),
        out_shape=shape(collected, bf16),
        compiler_params=params(),
        cost_estimate=cost(3),
        name="collect_logits",
    )(counts, dealt)


def join_body(pieces_ref, out_ref):
    peers, _, share = pieces_ref.shape
    for peer in range(peers):
        for index in range(share // LANE):
            at = (index * peers + peer) * LANE
            piece = pieces_ref[peer, :, index * LANE : (index + 1) * LANE].astype(f32)
            out_ref[:, at : at + LANE] = piece[:CLS, :]


def join_call(pieces):
    return pl.pallas_call(
        join_body,
        out_shape=shape((CLS, AVG), f32),
        compiler_params=params(),
        cost_estimate=cost(2),
        name="join_logits",
    )(pieces)


def moments(turned, first, second):
    new_first = beta_first * first + (1.0 - beta_first) * turned
    new_second = beta_second * second + (1.0 - beta_second) * turned * turned
    direction = (
        new_first
        / (1.0 - beta_first**STEP)
        / (jnp.sqrt(new_second / (1.0 - beta_second**STEP)) + adam_eps)
    )
    return new_first, new_second, direction


def dot_parts(first_arg, second_arg, first_dim, second_dim):
    first_high, first_low = split_low(first_arg)
    second_high, second_low = split_low(second_arg)
    return dot_on(first_high, second_high, first_dim, second_dim) + (
        dot_on(first_high, second_low, first_dim, second_dim)
        + dot_on(first_low, second_high, first_dim, second_dim)
    )


def factor(old, grad, dim):
    low = grad.astype(bf16)
    return beta_factor * old + (1.0 - beta_factor) * dot_on(low, low, dim, dim)


def branch_update_body(
    all_rows,
    stats_ref,
    window_ref,
    grads,
    w_ref,
    left_ref,
    right_ref,
    basis_left_ref,
    basis_right_ref,
    first_ref,
    second_ref,
    new_left_ref,
    new_right_ref,
    new_first_ref,
    new_second_ref,
    new_w_ref,
    low_w_ref,
    grad_out_ref,
):
    step = pl.program_id(0)

    @pl.when(step == 0)
    def _():
        for op in range(OPS):
            at = op * LANE + WINDOW + 1
            grad_out_ref[op * SHARE : (op + 1) * SHARE, :] = grads[at : at + SHARE, :HID].astype(f32)

    for op in range(OPS):

        @pl.when(step == op)
        def _(op=op):
            mean, scale = branch_scale(add_up(stats_ref), op, all_rows)
            window = window_ref[op]
            raw = grads[op * LANE : (op + 1) * LANE, :HID].astype(f32)
            gram = grads[op * LANE : (op + 1) * LANE, HID:].astype(f32)
            level, slant = branch_terms(all_rows, mean, scale, window, raw)
            column = gram[:WINDOW, WINDOW : WINDOW + 1]
            normed = gram_product(gram, window)[:WINDOW, :] - column * mean
            grad = raw[:WINDOW, :] - column * level - normed * slant
            shift = op * (DIN - STRIDE)
            grad = grad[shift : shift + DIN, :]
            new_left_ref[:, op, :] = factor(left_ref[:, op, :], grad, 1)
            new_right_ref[0] = factor(right_ref[0], grad, 0)
            basis_left, basis_right = basis_left_ref[:, op, :], basis_right_ref[0]
            turned = dot_parts(basis_left, grad, 0, 0)
            turned = dot_parts(turned, basis_right, 1, 0)
            new_first, new_second, direction = moments(
                turned, first_ref[:, op, :], second_ref[:, op, :]
            )
            new_first_ref[:, op, :] = new_first
            new_second_ref[:, op, :] = new_second
            back = dot_parts(basis_left, direction, 1, 0)
            back = dot_parts(back, basis_right, 1, 1)
            new_w = w_ref[:, op, :] - rate_branch * back
            new_w_ref[:, op, :] = new_w
            low_w_ref[:, op, :] = new_w.astype(bf16)


def branch_update_call(
    all_rows, stats, window, grads, w, left, right, basis_left, basis_right, first, second
):
    small, wide = fixed((DIN, OPS, DIN)), fixed((DIN, OPS, HID))
    square = pl.BlockSpec((1, HID, HID), lambda k: (k, 0, 0))
    return pl.pallas_call(
        functools.partial(branch_update_body, all_rows),
        grid=(OPS,),
        in_specs=[fixed(stats.shape), fixed((OPS, WINDOW, HID)), fixed(grads.shape)]
        + [wide, small, square, small, square, wide, wide],
        out_specs=[small, square, wide, wide, wide, wide, fixed((CPAD, HID))],
        out_shape=[
            shape((DIN, OPS, DIN), f32),
            shape((OPS, HID, HID), f32),
            shape((DIN, OPS, HID), f32),
            shape((DIN, OPS, HID), f32),
            shape((DIN, OPS, HID), f32),
            shape((DIN, OPS, HID), bf16),
            shape((CPAD, HID), f32),
        ],
        compiler_params=params(),
        cost_estimate=cost(12),
        name="branch_update",
    )(stats, window, grads, w, left, right, basis_left, basis_right, first, second)


def out_update_body(
    grad_ref,
    w_ref,
    left_ref,
    right_ref,
    basis_left_ref,
    basis_right_ref,
    first_ref,
    second_ref,
    new_left_ref,
    new_right_ref,
    new_first_ref,
    new_second_ref,
    new_w_ref,
    low_w_ref,
):
    grad = grad_ref[:CLS, :]
    new_left_ref[...] = factor(left_ref[...], grad, 0)
    new_right_ref[...] = factor(right_ref[...], grad, 1)
    turned = dot_parts(grad, basis_left_ref[...], 1, 0)
    turned = dot_parts(basis_right_ref[...], turned, 0, 0)
    new_first, new_second, direction = moments(turned, first_ref[...], second_ref[...])
    new_first_ref[...] = new_first
    new_second_ref[...] = new_second
    back = dot_parts(direction, basis_left_ref[...], 1, 1)
    back = dot_parts(basis_right_ref[...], back, 1, 0)
    new_w = w_ref[...] - rate_out * back
    new_w_ref[...] = new_w
    low_w_ref[...] = new_w.astype(bf16)


def out_update_call(grad, w, left, right, basis_left, basis_right, first, second):
    return pl.pallas_call(
        out_update_body,
        out_shape=[
            shape((HID, HID), f32),
            shape((CLS, CLS), f32),
            shape((CLS, HID), f32),
            shape((CLS, HID), f32),
            shape((CLS, HID), f32),
            shape((CLS, HID), bf16),
        ],
        compiler_params=params(),
        cost_estimate=cost(4),
        name="out_update",
    )(grad, w, left, right, basis_left, basis_right, first, second)


def mid_update_body(
    grad_ref, w_ref, basis_ref, first_ref, second_ref, new_first_ref, new_second_ref, new_w_ref, low_w_ref
):
    turned = dot_parts(grad_ref[...], basis_ref[...], 1, 0)
    new_first, new_second, direction = moments(turned, first_ref[...], second_ref[...])
    new_first_ref[...] = new_first
    new_second_ref[...] = new_second
    new_w = w_ref[...] - rate_mid * dot_parts(direction, basis_ref[...], 1, 1)
    new_w_ref[...] = new_w
    low_w_ref[...] = new_w.astype(bf16)


def mid_update_call(grad, w, basis, first, second):
    rows = grad.shape[0]
    return pl.pallas_call(
        mid_update_body,
        out_shape=[shape((rows, HID), f32)] * 3 + [shape((rows, HID), bf16)],
        compiler_params=params(),
        cost_estimate=cost(3),
        name="mid_update",
    )(grad, w, basis, first, second)


def mid_gram_body(rows_ref, out_ref):
    rows = rows_ref[...]
    out_ref[...] = dot_on(rows, rows, 0, 0).astype(bf16)


def mid_gram_call(rows):
    return pl.pallas_call(
        mid_gram_body,
        out_shape=shape((HID, HID), bf16),
        compiler_params=params(),
        cost_estimate=cost(2),
        name="mid_gram",
    )(rows)


def after(values, *others):
    return lax.optimization_barrier((values,) + others)[0]


def swap(values, axis, distance):
    peers = lax.axis_size(axis)
    return lax.ppermute(values, axis, [(peer, peer ^ distance) for peer in range(peers)])


def add_all(values):
    while len(values) > 1:
        values = [values[i] + values[i + 1] for i in range(0, len(values), 2)]
    return values[0]


def exchange(values):
    return lax.all_to_all(values, "col", 0, 0, tiled=True)


def spread_out(values, dtype=f32):
    copies = jnp.broadcast_to(values[None], (lax.axis_size("col"),) + values.shape)
    return exchange(copies.astype(dtype))


def far_copies(values):
    pieces = {0: values}
    distance = lax.axis_size("row") // 2
    while distance > 1:
        pieces.update({d ^ distance: swap(v, "row", distance) for d, v in list(pieces.items())})
        distance //= 2
    return pieces


def near_copies(pieces, *others):
    held = lax.optimization_barrier((*[pieces[d] for d in sorted(pieces)], *others))
    pieces = dict(zip(sorted(pieces), held))
    pieces.update({d ^ 1: swap(v, "row", 1) for d, v in list(pieces.items())})
    return [pieces[d] for d in sorted(pieces)], held[len(held) - len(others) :]


def sum_in_row(values):
    return add_all([values] + [swap(values, "row", d) for d in range(1, lax.axis_size("row"))])


def keep_bit(values, distance):
    bit = lax.rem(lax.axis_index("row") // distance, 2)
    pairs = values.reshape((-1, 2) + values.shape[1:])
    kept = lax.dynamic_index_in_dim(pairs, bit, 1, keepdims=False)
    sent = lax.dynamic_index_in_dim(pairs, 1 - bit, 1, keepdims=False)
    return kept, sent


def finish_scatter(values, distance):
    while distance < lax.axis_size("row") // 2:
        kept, sent = keep_bit(values, distance)
        values = kept + swap(sent.astype(bf16), "row", distance).astype(f32)
        distance *= 2
    values = values.reshape((lax.axis_size("col"), -1) + values.shape[2:]).astype(bf16)
    return jnp.sum(exchange(values).astype(f32), axis=0)


def local(
    features,
    labels,
    counts,
    w_branch,
    w_mid,
    w_out,
    left_branch,
    right_branch,
    basis_left_branch,
    basis_right_branch,
    first_branch,
    second_branch,
    right_mid,
    basis_right_mid,
    first_mid,
    second_mid,
    left_out,
    right_out,
    basis_left_out,
    basis_right_out,
    first_out,
    second_out,
):
    groups, peers = lax.axis_size("row"), lax.axis_size("col")
    devices = groups * peers
    all_rows = float(AVG * devices)

    def by_input(values):
        return values.transpose(1, 0, 2)

    turned = features.T
    own_mid = spread_out(w_mid, bf16).reshape(-1, HID)
    window, gram, branch_sums = gram_call(counts, turned, by_input(w_branch), 4096)
    branch_sums = sum_in_row(branch_sums)
    own_mid = after(own_mid, branch_sums)
    pieces = far_copies(own_mid)
    branch_stats = spread_out(branch_sums)
    pieces, (branch_stats,) = near_copies(pieces, branch_stats)
    pre, joined, slope, mid_low, mid_sums = forward_call(
        all_rows, devices, counts, turned, branch_stats, window, pieces, 512
    )
    mid_stats = lax.all_to_all(mid_sums, BOTH, 0, 0, tiled=True)
    back, logits, grad_out, back_sums = head_call(
        all_rows, counts, pre, mid_stats, w_out.T, labels.reshape(1, -1), 2048
    )
    back_stats = lax.all_to_all(back_sums, BOTH, 0, 0, tiled=True)

    dealt = deal_call(counts, logits, peers)
    back_stats, dealt = lax.optimization_barrier((back_stats, dealt))
    dealt = exchange(dealt)
    mid, part, grad_branch = branch_back_call(
        all_rows,
        devices,
        counts,
        pre,
        back,
        slope,
        turned,
        mid_low,
        window,
        mid_stats,
        back_stats,
        branch_stats,
        grad_out,
        gram,
        1024,
    )
    grad_branch, dealt = lax.optimization_barrier((grad_branch, dealt))
    grad_branch = lax.all_to_all(grad_branch, BOTH, 0, 0, tiled=True)
    parts = mid_grad_call(groups, mid, joined, 1024)
    grad_branch, *parts = lax.optimization_barrier((grad_branch, *parts))
    kept, sent = parts[:2], parts[2:]
    grad_branch = jnp.sum(grad_branch.astype(f32), axis=0, keepdims=True).astype(bf16)
    grad_branch = jnp.broadcast_to(grad_branch, (devices,) + grad_branch.shape[1:])
    grad_branch = lax.all_to_all(grad_branch, BOTH, 0, 0, tiled=True)
    near = [swap(part, "row", 1) for part in sent]
    away = (kept[1] + near[1]).astype(bf16)
    far = swap(away, "row", groups // 2)
    collected = collect_call(counts, after(dealt, away))
    far, grad_branch, collected = lax.optimization_barrier((far, grad_branch, collected))
    grad_mid = finish_scatter(kept[0] + near[0] + far.astype(f32), 2)
    grad_branch = grad_branch.reshape(OPS * LANE, HID + LANE)
    grad_features = rows_back_call(
        all_rows, counts, turned, part, branch_stats, window, grad_branch, 4096
    )
    grad_mid, grad_features = lax.optimization_barrier((grad_mid, grad_features))
    all_mid = spread_out(grad_mid, bf16).reshape(-1, HID)
    *branch_parts, grad_out = branch_update_call(
        all_rows,
        branch_stats,
        window,
        grad_branch,
        by_input(w_branch),
        by_input(left_branch),
        right_branch,
        by_input(basis_left_branch),
        basis_right_branch,
        by_input(first_branch),
        by_input(second_branch),
    )
    held = lax.optimization_barrier((all_mid, *branch_parts))
    all_mid, branch_parts = held[0], held[1:]
    mid_gram = mid_gram_call(all_mid)
    collected = exchange(after(collected, mid_gram))
    distance = groups // 2
    others = swap(mid_gram, "row", distance)
    mid_parts = mid_update_call(grad_mid, w_mid, basis_right_mid, first_mid, second_mid)
    out_parts = out_update_call(
        grad_out,
        w_out.T,
        left_out,
        right_out,
        basis_left_out,
        basis_right_out,
        first_out.T,
        second_out.T,
    )
    mid_gram, others, collected, *held = lax.optimization_barrier(
        (mid_gram, others, collected, *mid_parts, *out_parts)
    )
    mid_parts, out_parts = held[:4], held[4:]
    mid_gram = mid_gram.astype(f32) + others.astype(f32)
    while distance > 1:
        distance //= 2
        mid_gram = mid_gram + swap(mid_gram, "row", distance)
    new_right_mid = beta_factor * right_mid + (1.0 - beta_factor) * mid_gram
    new_logits = join_call(collected)
    branch_parts = [
        part if index == 1 else by_input(part) for index, part in enumerate(branch_parts)
    ]
    out_parts = list(out_parts[:2]) + [part.T for part in out_parts[2:]]
    return (new_logits.T, grad_features.T, *branch_parts, new_right_mid, *mid_parts, *out_parts)


def solution(mesh):
    split, rows, whole = P(BOTH, None), P(BOTH), P()
    in_specs = (split, rows, whole, whole, split) + (whole,) * 9 + (split, split) + (whole,) * 6
    out_specs = (split, split) + (whole,) * 7 + (split,) * 4 + (whole,) * 6
    return jax.shard_map(local, mesh=mesh, in_specs=in_specs, out_specs=out_specs, check_vma=False)
```

profile of v0, /device:TPU:0, one launch (start us, length us, event | category | flops | bytes accessed | tf_op | source)
XLA Modules:
  0.0 304.2 jit_solution(16459549353531148781)
XLA Ops:
  2.4 7.3 %all-to-all-start = ((bf16[8,64,512]{2,1,0:T(8,128)(2,1)}), bf16[8,64,512]{2,1,0:T(8,128)(2,1)S(1)}, u32[]{:S(2)}, u32[]{:S(2)}) async-start(bf16[8,64,512]{2,1,0:T(8,128)(2,1)} %broadcast_in_dim.8), calls=%async_computation | async-start | bytes 1048576 | tf_op jit(solution)/shard_map/all_to_all | solution.py:1002
  9.7 7.4 %row_moments.1 = (bf16[4,112,512]{2,1,0:T(8,128)(2,1)}, f32[4,128,128]{2,1,0:T(8,128)}, f32[8,512]{1,0:T(8,128)}) custom-call(s32[4,8]{1,0:T(4,128)} %counts.13, bf16[400,8192]{1,0:T(8,128)(2,1)} %bitcast.29, f32[100,4,512]{2,1,0:T(4,128)} %bitcast.33), custom_call_target="tpu_custom_call" | custom-call | flops 6000000000 | bytes 1 | tf_op jit(solution)/shard_map/row_moments/pallas_call | solution.py:204
  19.0 1.6 collective-permute-done.2
  25.7 11.0 %all_to_all.50.refs_1_.stats_ref = f32[8,8,512]{2,1,0:T(8,128)} all-to-all(f32[8,8,512]{2,1,0:T(8,128)S(1)} %broadcast_in_dim.9), channel_id=1, replica_groups=mesh['row'=4,'col'=8] {'col'}, dimensions={0} | all-to-all | bytes 262144 | tf_op jit(solution)/shard_map/all_to_all | solution.py:1002
  40.1 48.7 %forward_layers.1 = (bf16[8192,512]{1,0:T(8,128)(2,1)}, bf16[8192,2048]{1,0:T(8,128)(2,1)}, bf16[8192,2048]{1,0:T(8,128)(2,1)}, bf16[2048,512]{1,0:T(8,128)(2,1)}, f32[32,8,128]{2,1,0:T(8,128)}) custom-call(s32[4,8]{1,0:T(4,128)} %counts.13, bf16[400,8192]{1,0:T(8,128)(2,1)} %bitcast.30, f32[8,8,512]{2,1,0:T(8,128)} %all_to_all.50.refs_1_.stats_ref, ...), custom_call_target="tpu_custom_call" | custom-call | flops 44000002048 | bytes 1 | tf_op jit(solution)/shard_map/forward_layers/pallas_call | solution.py:288
  88.9 12.9 %all_to_all.51.stats_ref.mid_stats_ref = f32[32,8,128]{2,1,0:T(8,128)} all-to-all(f32[32,8,128]{2,1,0:T(8,128)} %get-tuple-element.102), channel_id=1, replica_groups=mesh['row'=4,'col'=8] {'row','col'}, dimensions={0} | all-to-all | bytes 262144 | tf_op jit(solution)/shard_map/all_to_all | solution.py:1089
  101.7 16.4 %head.1 = (bf16[8192,512]{1,0:T(8,128)(2,1)}, bf16[48,8192]{1,0:T(8,128)(2,1)}, f32[48,512]{1,0:T(8,128)}, f32[32,8,128]{2,1,0:T(8,128)}) custom-call(s32[4,8]{1,0:T(4,128)} %counts.13, bf16[8192,512]{1,0:T(8,128)(2,1)} %get-tuple-element.101.pre_ref, f32[32,8,128]{2,1,0:T(8,128)} %all_to_all.51.stats_ref.mid_stats_ref, f32[47,512]{1,0:T(8,128)} %bitcast.39, ...), custom_call_target="tpu_custom_call" | custom-call | flops 17999998976 | bytes 1 | tf_op jit(solution)/shard_map/head/pallas_call | solution.py:389
  118.1 2.6 all-to-all-start.3
  120.7 3.1 %deal_logits.1 = bf16[8,48,1152]{2,1,0:T(8,128)(2,1)} custom-call(s32[4,8]{1,0:T(4,128)} %counts.13, bf16[48,8192]{1,0:T(8,128)(2,1)} %get-tuple-element.107.logits_ref), custom_call_target="tpu_custom_call" | custom-call | flops 3000000000 | bytes 1 | tf_op jit(solution)/shard_map/deal_logits/pallas_call | solution.py:723
  123.8 4.6 %all-to-all-done.3.sums_ref = f32[32,8,128]{2,1,0:T(8,128)S(1)} async-done(((f32[32,8,128]{2,1,0:T(8,128)}), f32[32,8,128]{2,1,0:T(8,128)S(1)}, u32[]{:S(2)}, u32[]{:S(2)}) %all-to-all-start.3) | async-done | bytes 131104 | tf_op jit(solution)/shard_map/all_to_all | solution.py:1093
  128.4 3.7 %all-to-all-start.4 = ((bf16[8,48,1152]{2,1,0:T(8,128)(2,1)}), bf16[8,48,1152]{2,1,0:T(8,128)(2,1)S(1)}, u32[]{:S(2)}, u32[]{:S(2)}) async-start(bf16[8,48,1152]{2,1,0:T(8,128)(2,1)} %deal_logits.1), calls=%async_computation.4 | async-start | bytes 1769472 | tf_op jit(solution)/shard_map/all_to_all | solution.py:1002
  132.2 44.4 %branch_back.1 = (bf16[8192,512]{1,0:T(8,128)(2,1)}, bf16[400,8192]{1,0:T(8,128)(2,1)}, bf16[32,16,640]{2,1,0:T(8,128)(2,1)}) custom-call(s32[4,8]{1,0:T(4,128)} %counts.13, bf16[8192,512]{1,0:T(8,128)(2,1)} %get-tuple-element.101.pre_ref, bf16[8192,512]{1,0:T(8,128)(2,1)} %get-tuple-element.103.back_ref, bf16[8192,2048]{1,0:T(8,128)(2,1)} %get-tuple-element.104.slope_ref, ...), custom_call_target="tpu_custom_call" | custom-call | flops 48000000000 | bytes 1 | tf_op jit(solution)/shard_map/branch_back/pallas_call | solution.py:532
  177.5 5.3 %all-to-all-start.5 = ((bf16[32,16,640]{2,1,0:T(8,128)(2,1)}), bf16[32,16,640]{2,1,0:T(8,128)(2,1)S(1)}, u32[]{:S(2)}, u32[]{:S(2)}) async-start(bf16[32,16,640]{2,1,0:T(8,128)(2,1)} %get-tuple-element.113), calls=%async_computation.5 | async-start | bytes 1310720 | tf_op jit(solution)/shard_map/all_to_all | solution.py:1116
  182.8 24.6 %mid_grad.1 = (f32[1,512,512]{2,1,0:T(8,128)}, f32[1,512,512]{2,1,0:T(8,128)}, f32[1,512,512]{2,1,0:T(8,128)}, f32[1,512,512]{2,1,0:T(8,128)}) custom-call(bf16[8192,512]{1,0:T(8,128)(2,1)} %get-tuple-element.114.mid_ref, bf16[8192,2048]{1,0:T(8,128)(2,1)} %get-tuple-element.115.joined_ref), custom_call_target="tpu_custom_call" | custom-call | flops 24999999488 | bytes 1 | tf_op jit(solution)/shard_map/mid_grad/pallas_call | solution.py:594
  208.7 5.9 %all-to-all-start.6 = ((bf16[32,16,640]{2,1,0:T(8,128)(2,1)}), bf16[32,16,640]{2,1,0:T(8,128)(2,1)}, u32[]{:S(2)}, u32[]{:S(2)}) async-start(bf16[32,16,640]{2,1,0:T(8,128)(2,1)} %broadcast_in_dim.10), calls=%async_computation.6 | async-start | bytes 1310720 | tf_op jit(solution)/shard_map/all_to_all | solution.py:1122
  214.9 2.2 add_convert_fusion.1
  217.1 1.7 collective-permute-start.8
  218.8 2.9 collect_logits.1
  221.7 12.1 %all-to-all-done.6 = bf16[32,16,640]{2,1,0:T(8,128)(2,1)} async-done(((bf16[32,16,640]{2,1,0:T(8,128)(2,1)}), bf16[32,16,640]{2,1,0:T(8,128)(2,1)}, u32[]{:S(2)}, u32[]{:S(2)}) %all-to-all-start.6) | async-done | bytes 655392 | tf_op jit(solution)/shard_map/all_to_all | solution.py:1122
  233.7 2.3 collective-permute-done.8
  237.1 5.3 %all-to-all-start.7 = ((bf16[8,64,512]{2,1,0:T(8,128)(2,1)}), bf16[8,64,512]{2,1,0:T(8,128)(2,1)S(1)}, u32[]{:S(2)}, u32[]{:S(2)}) async-start(bf16[8,64,512]{2,1,0:T(8,128)(2,1)} %bitcast.5), calls=%async_computation.7 | async-start | bytes 1048576 | tf_op jit(solution)/shard_map/all_to_all | solution.py:1002
  242.4 8.8 %rows_back.1 = bf16[400,8192]{1,0:T(8,128)(2,1)} custom-call(s32[4,8]{1,0:T(4,128)} %counts.13, bf16[400,8192]{1,0:T(8,128)(2,1)} %bitcast.32, bf16[400,8192]{1,0:T(8,128)(2,1)} %get-tuple-element.128.part_ref, f32[8,8,512]{2,1,0:T(8,128)} %all_to_all.50.refs_1_.stats_ref, bf16[4,112,512]{2,1,0:T(8,128)(2,1)} %get-tuple-element.98.refs_2_.window_ref, ...), custom_call_target="tpu_custom_call" | custom-call | flops 8000000000 | bytes 1 | tf_op jit(solution)/shard_map/rows_back/pallas_call | solution.py:661
  251.3 5.7 %all-to-all-done.7 = bf16[8,64,512]{2,1,0:T(8,128)(2,1)S(1)} async-done(((bf16[8,64,512]{2,1,0:T(8,128)(2,1)}), bf16[8,64,512]{2,1,0:T(8,128)(2,1)S(1)}, u32[]{:S(2)}, u32[]{:S(2)}) %all-to-all-start.7) | async-done | bytes 524320 | tf_op jit(solution)/shard_map/all_to_all | solution.py:1002
  257.9 3.7 %all-to-all-start.8 = ((bf16[8,64,512]{2,1,0:T(8,128)(2,1)}), bf16[8,64,512]{2,1,0:T(8,128)(2,1)S(1)}, u32[]{:S(2)}, u32[]{:S(2)}) async-start(bf16[8,64,512]{2,1,0:T(8,128)(2,1)} %broadcast_in_dim.11), calls=%async_computation.8 | async-start | bytes 1048576 | tf_op jit(solution)/shard_map/all_to_all | solution.py:1002
  261.6 14.8 %branch_update.1 = (f32[100,4,100]{2,1,0:T(4,128)}, f32[4,512,512]{2,1,0:T(8,128)}, f32[100,4,512]{2,1,0:T(4,128)}, f32[100,4,512]{2,1,0:T(4,128)}, f32[100,4,51...) custom-call(f32[8,8,512]{2,1,0:T(8,128)} %all_to_all.50.refs_1_.stats_ref, ...), custom_call_target="tpu_custom_call" | custom-call | flops 12000000000 | bytes 1 | tf_op jit(solution)/shard_map/branch_update/pallas_call | solution.py:879
  277.3 2.3 mid_gram.1
  279.6 5.9 %all-to-all-start.9 = ((bf16[8,48,512]{2,1,0:T(8,128)(2,1)}), bf16[8,48,512]{2,1,0:T(8,128)(2,1)S(1)}, u32[]{:S(2)}, u32[]{:S(2)}) async-start(bf16[8,48,512]{2,1,0:T(8,128)(2,1)} %collect_logits.1), calls=%async_computation.9 | async-start | bytes 786432 | tf_op jit(solution)/shard_map/all_to_all | solution.py:1002
  286.2 4.0 %out_update.1 = (f32[512,512]{1,0:T(8,128)}, f32[47,47]{1,0:T(8,128)}, f32[47,512]{1,0:T(8,128)}, f32[47,512]{1,0:T(8,128)}, f32[47,512]{1,0:T(8,128)}, /*index=5*/bf16[47,512]{1,0:T(8,128)(2,1)}) custom-call(f32[48,512]{1,0:T(8,128)} %get-tuple-element.144.grad_ref, f32[47,512]{1,0:T(8,128)} %bitcast.40, f32[512,512]{1,0:T(8,128)} %left_ref.1, ...), custom_call_target="tpu_custom_call" | custom-call | flops 4000000000 | bytes 1 | tf_op jit(solution)/shard_map/out_update/pallas_call | solution.py:932
  290.2 3.1 %mid_update.1 = (f32[64,512]{1,0:T(8,128)}, f32[64,512]{1,0:T(8,128)}, f32[64,512]{1,0:T(8,128)}, bf16[64,512]{1,0:T(8,128)(2,1)}) custom-call(f32[64,512]{1,0:T(8,128)} %copy-done.4, f32[64,512]{1,0:T(8,128)} %w_ref.1, f32[512,512]{1,0:T(8,128)} %basis_ref.1, f32[64,512]{1,0:T(8,128)} %first_ref.1, f32[64,512]{1,0:T(8,128)} %second_ref.1), custom_call_target="tpu_custom_call" | custom-call | flops 3000000000 | bytes 1 | tf_op jit(solution)/shard_map/mid_update/pallas_call | solution.py:962
  293.4 5.3 %collective-permute-done.9 = bf16[512,512]{1,0:T(8,128)(2,1)S(1)} collective-permute-done((bf16[512,512]{1,0:T(8,128)(2,1)}, bf16[512,512]{1,0:T(8,128)(2,1)S(1)}, u32[]{:S(2)}, u32[]{:S(2)}) %collective-permute-start.9) | collective-permute-done | bytes 524320 | tf_op jit(solution)/shard_map/ppermute | solution.py:992
  299.4 2.0 join_logits.1
  301.7 2.5 multiply_add_fusion
  (58 shorter events, 19.2 us)
Async XLA Ops:
  2.4 21.7 %all-to-all-start = ((bf16[8,64,512]{2,1,0:T(8,128)(2,1)}), bf16[8,64,512]{2,1,0:T(8,128)(2,1)S(1)}, u32[]{:S(2)}, u32[]{:S(2)}) async-start(bf16[8,64,512]{2,1,0:T(8,128)(2,1)} %broadcast_in_dim.8), calls=%async_computation | async-start | bytes 1048576 | tf_op jit(solution)/shard_map/all_to_all | solution.py:1002
  17.1 3.5 %collective-permute-start.2 = (f32[8,512]{1,0:T(8,128)}, f32[8,512]{1,0:T(8,128)S(1)}, u32[]{:S(2)}, u32[]{:S(2)}) collective-permute-start(f32[8,512]{1,0:T(8,128)} %get-tuple-element.95), channel_id=1, source_target_pairs={{0,24},{8,16},{16,8},{24,0},{1,25},{9,17},{17,9},{25,1},{2,26},{10... | collective-permute-start | bytes 49160 | tf_op jit(solution)/shard_map/ppermute | solution.py:992
  17.8 4.1 %collective-permute-start.1 = (f32[8,512]{1,0:T(8,128)}, f32[8,512]{1,0:T(8,128)S(1)}, u32[]{:S(2)}, u32[]{:S(2)}) collective-permute-start(f32[8,512]{1,0:T(8,128)} %get-tuple-element.95), channel_id=1, source_target_pairs={{0,16},{8,24},{16,0},{24,8},{1,17},{9,25},{17,1},{25,9},{2,18},{10... | collective-permute-start | bytes 49160 | tf_op jit(solution)/shard_map/ppermute | solution.py:992
  18.7 3.2 %collective-permute-start = (f32[8,512]{1,0:T(8,128)}, f32[8,512]{1,0:T(8,128)S(1)}, u32[]{:S(2)}, u32[]{:S(2)}) collective-permute-start(f32[8,512]{1,0:T(8,128)} %get-tuple-element.95), channel_id=1, source_target_pairs={{0,8},{8,0},{16,24},{24,16},{1,9},{9,1},{17,25},{25,17},{2,10},{10... | collective-permute-start | bytes 49160 | tf_op jit(solution)/shard_map/ppermute | solution.py:992
  24.2 15.2 %copy-start.5 = (bf16[8,64,512]{2,1,0:T(8,128)(2,1)}, bf16[8,64,512]{2,1,0:T(8,128)(2,1)S(1)}, u32[]{:S(2)}) copy-start(bf16[8,64,512]{2,1,0:T(8,128)(2,1)S(1)} %all-to-all-done) | copy-start | bytes 1572868
  24.2 12.5 %collective-permute-start.3 = (bf16[512,512]{1,0:T(8,128)(2,1)S(1)}, bf16[512,512]{1,0:T(8,128)(2,1)S(1)}, u32[]{:S(2)}, u32[]{:S(2)}) collective-permute-start(bf16[512,512]{1,0:T(8,128)(2,1)S(1)} %bitcast.25), channel_id=1, source_target_pairs={{0,16},{8,24},{16,0},{24,8},{1,17},{9,25},{17,1},{25,9},{2,18},{10... | collective-permute-start | bytes 1572872 | tf_op jit(solution)/shard_map/ppermute | solution.py:992
  36.7 2.7 copy-start.9
  36.7 1.9 collective-permute-start.4
  36.7 2.7 collective-permute-start.5
  38.6 0.8 copy-start.10
  39.4 0.8 copy-start.11
  118.1 10.3 %all-to-all-start.3 = ((f32[32,8,128]{2,1,0:T(8,128)}), f32[32,8,128]{2,1,0:T(8,128)S(1)}, u32[]{:S(2)}, u32[]{:S(2)}) async-start(f32[32,8,128]{2,1,0:T(8,128)} %get-tuple-element.106), calls=%async_computation.3 | async-start | bytes 262144 | tf_op jit(solution)/shard_map/all_to_all | solution.py:1093
  128.4 3.7 %copy-start.8 = (f32[32,8,128]{2,1,0:T(8,128)}, f32[32,8,128]{2,1,0:T(8,128)S(1)}, u32[]{:S(2)}) copy-start(f32[32,8,128]{2,1,0:T(8,128)S(1)} %all-to-all-done.3.sums_ref) | copy-start | bytes 393220
  128.4 48.2 %all-to-all-start.4 = ((bf16[8,48,1152]{2,1,0:T(8,128)(2,1)}), bf16[8,48,1152]{2,1,0:T(8,128)(2,1)S(1)}, u32[]{:S(2)}, u32[]{:S(2)}) async-start(bf16[8,48,1152]{2,1,0:T(8,128)(2,1)} %deal_logits.1), calls=%async_computation.4 | async-start | bytes 1769472 | tf_op jit(solution)/shard_map/all_to_all | solution.py:1002
  176.6 0.9 copy-start.3
  177.5 29.9 %all-to-all-start.5 = ((bf16[32,16,640]{2,1,0:T(8,128)(2,1)}), bf16[32,16,640]{2,1,0:T(8,128)(2,1)S(1)}, u32[]{:S(2)}, u32[]{:S(2)}) async-start(bf16[32,16,640]{2,1,0:T(8,128)(2,1)} %get-tuple-element.113), calls=%async_computation.5 | async-start | bytes 1310720 | tf_op jit(solution)/shard_map/all_to_all | solution.py:1116
  207.5 7.4 %collective-permute-start.7 = (f32[1,512,512]{2,1,0:T(8,128)}, f32[1,512,512]{2,1,0:T(8,128)S(1)}, u32[]{:S(2)}, u32[]{:S(2)}) collective-permute-start(f32[1,512,512]{2,1,0:T(8,128)} %get-tuple-element.123), channel_id=1, source_target_pairs={{0,8},{8,0},{16,24},{24,16},{1,9},{9,1},{17,25},{25,17},{2,10},{10... | collective-permute-start | bytes 3145736 | tf_op jit(solution)/shard_map/ppermute | solution.py:992
  208.7 25.0 %all-to-all-start.6 = ((bf16[32,16,640]{2,1,0:T(8,128)(2,1)}), bf16[32,16,640]{2,1,0:T(8,128)(2,1)}, u32[]{:S(2)}, u32[]{:S(2)}) async-start(bf16[32,16,640]{2,1,0:T(8,128)(2,1)} %broadcast_in_dim.10), calls=%async_computation.6 | async-start | bytes 1310720 | tf_op jit(solution)/shard_map/all_to_all | solution.py:1122
  214.6 21.5 %copy-start.1 = (f32[1,512,512]{2,1,0:T(8,128)S(1)}, f32[1,512,512]{2,1,0:T(8,128)}, u32[]{:S(2)}) copy-start(f32[1,512,512]{2,1,0:T(8,128)} %get-tuple-element.120) | copy-start | bytes 3145732
  214.6 21.4 %collective-permute-start.6 = (f32[1,512,512]{2,1,0:T(8,128)}, f32[1,512,512]{2,1,0:T(8,128)S(1)}, u32[]{:S(2)}, u32[]{:S(2)}) collective-permute-start(f32[1,512,512]{2,1,0:T(8,128)} %get-tuple-element.121), channel_id=1, source_target_pairs={{0,8},{8,0},{16,24},{24,16},{1,9},{9,1},{17,25},{25,17},{2,10},{10... | collective-permute-start | bytes 3145736 | tf_op jit(solution)/shard_map/ppermute | solution.py:992
  217.1 19.0 %collective-permute-start.8 = (bf16[1,512,512]{2,1,0:T(8,128)(2,1)}, bf16[1,512,512]{2,1,0:T(8,128)(2,1)S(1)}, u32[]{:S(2)}, u32[]{:S(2)}) collective-permute-start(bf16[1,512,512]{2,1,0:T(8,128)(2,1)} %add_convert_fusion.1), channel_id=1, source_target_pairs={{0,16},{8,24},{16,0},{24,8},{1,17},{9,25},{17,1},{25,9},{2,18},{10... | collective-permute-start | bytes 1572872 | tf_op jit(solution)/shard_map/ppermute | solution.py:992
  237.1 19.8 %all-to-all-start.7 = ((bf16[8,64,512]{2,1,0:T(8,128)(2,1)}), bf16[8,64,512]{2,1,0:T(8,128)(2,1)S(1)}, u32[]{:S(2)}, u32[]{:S(2)}) async-start(bf16[8,64,512]{2,1,0:T(8,128)(2,1)} %bitcast.5), calls=%async_computation.7 | async-start | bytes 1048576 | tf_op jit(solution)/shard_map/all_to_all | solution.py:1002
  257.0 19.4 %copy-start.4 = (f32[64,512]{1,0:T(8,128)}, f32[64,512]{1,0:T(8,128)S(1)}, u32[]{:S(2)}) copy-start(f32[64,512]{1,0:T(8,128)S(1)} %convert_reduce_fusion.grad_ref) | copy-start | bytes 393220
  257.9 18.6 %all-to-all-start.8 = ((bf16[8,64,512]{2,1,0:T(8,128)(2,1)}), bf16[8,64,512]{2,1,0:T(8,128)(2,1)S(1)}, u32[]{:S(2)}, u32[]{:S(2)}) async-start(bf16[8,64,512]{2,1,0:T(8,128)(2,1)} %broadcast_in_dim.11), calls=%async_computation.8 | async-start | bytes 1048576 | tf_op jit(solution)/shard_map/all_to_all | solution.py:1002
  276.5 0.8 copy-start.6
  279.6 19.1 %all-to-all-start.9 = ((bf16[8,48,512]{2,1,0:T(8,128)(2,1)}), bf16[8,48,512]{2,1,0:T(8,128)(2,1)S(1)}, u32[]{:S(2)}, u32[]{:S(2)}) async-start(bf16[8,48,512]{2,1,0:T(8,128)(2,1)} %collect_logits.1), calls=%async_computation.9 | async-start | bytes 786432 | tf_op jit(solution)/shard_map/all_to_all | solution.py:1002
  285.5 13.2 %collective-permute-start.9 = (bf16[512,512]{1,0:T(8,128)(2,1)}, bf16[512,512]{1,0:T(8,128)(2,1)S(1)}, u32[]{:S(2)}, u32[]{:S(2)}) collective-permute-start(bf16[512,512]{1,0:T(8,128)(2,1)} %mid_gram.1), channel_id=1, source_target_pairs={{0,16},{8,24},{16,0},{24,8},{1,17},{9,25},{17,1},{25,9},{2,18},{10... | collective-permute-start | bytes 1572872 | tf_op jit(solution)/shard_map/ppermute | solution.py:992
  290.2 8.5 %copy-start = (bf16[512,512]{1,0:T(8,128)(2,1)S(1)}, bf16[512,512]{1,0:T(8,128)(2,1)}, u32[]{:S(2)}) copy-start(bf16[512,512]{1,0:T(8,128)(2,1)} %mid_gram.1) | copy-start | bytes 1572868
  293.4 8.4 %copy-start.2 = (f32[512,512]{1,0:T(8,128)S(1)}, f32[512,512]{1,0:T(8,128)}, u32[]{:S(2)}) copy-start(f32[512,512]{1,0:T(8,128)} %param.34) | copy-start | bytes 3145732
  298.7 0.7 copy-start.7
  298.8 2.9 collective-permute-start.10
where the time goes:
time: 306 us; the launch traced here: 304 us
  Pallas kernels  183 us (60%)
  starting transfers between devices  46.6 us (15%)
  waiting for transfers between devices  37 us (12%)
  blocking collectives  23.8 us (8%)
  other arithmetic  7.8 us (3%)
  local copies, waits for them, and re-layouts  5.59 us (2%)
    pallas_call x1, Pallas kernels, forward_call(): pl.pallas_call(functools.partial(forward_body, all_rows, count), grid_spe...  48.7 us
    pallas_call x1, Pallas kernels, branch_back_call(): pl.pallas_call(functools.partial(branch_back_body, all_rows), grid_spec=p...  44.4 us
    all_to_all x5, starting transfers between devices, exchange(): return lax.all_to_all(values, 'col', 0, 0, tiled=True)  25.9 us
    pallas_call x1, Pallas kernels, mid_grad_call(): pl.pallas_call(mid_grad_body, grid=(total // block,), in_specs=[rows_of(b...  24.6 us
    pallas_call x1, Pallas kernels, head_call(): pl.pallas_call(functools.partial(head_body, all_rows), grid_spec=pltpu.Pr...  16.4 us
    pallas_call x1, Pallas kernels, branch_update_call(): pl.pallas_call(functools.partial(branch_update_body, all_rows), grid=(OPS...  14.8 us
    ppermute x11, waiting for transfers between devices, swap(): lax.ppermute(values, axis, [(peer, peer ^ distance) for peer in range(pee...  13 us
    all_to_all x1, blocking collectives, local(): mid_stats = lax.all_to_all(mid_sums, BOTH, 0, 0, tiled=True)  12.9 us
  transfers between devices with their start and end apart: 19, of which 11 were waited for; matrix products, arithmetic and copies ran while one was open for 1% of the time, Pallas kernels for 38%

commit v1 on v0

--- a/solution.py
+++ b/solution.py
@@ -98,8 +98,8 @@
 
 
 def branch_scale(stats, op, all_rows):
-    mean = stats[op : op + 1, :] / all_rows
-    square = stats[OPS + op : OPS + op + 1, :] / all_rows
+    mean = stats[op : op + 1, :HID] / all_rows
+    square = stats[OPS + op : OPS + op + 1, :HID] / all_rows
     return mean, lax.rsqrt(square - mean * mean + norm_eps)
 
 
@@ -143,11 +143,14 @@
 
 
 def gram_product(gram, window):
-    high, low = split_low(gram)
     weight = padded(window)
-    return jnp.dot(high, weight, preferred_element_type=f32) + jnp.dot(
-        low, weight, preferred_element_type=f32
-    )
+    product = None
+    for _ in range(3):
+        part = gram.astype(bf16)
+        gram = gram - part.astype(f32)
+        term = jnp.dot(part, weight, preferred_element_type=f32)
+        product = term if product is None else product + term
+    return product
 
 
 def mask_rows(counts, x_ref, held):
@@ -157,6 +160,36 @@
     line = lax.broadcasted_iota(jnp.int32, (16, block), 0)
     held[:VALID, :] = x_ref[...] * valid[0:1, :].astype(bf16)
     held[VALID:, :] = jnp.where(line < 2, valid, 0.0).astype(bf16)
+
+
+def doubling_steps():
+    steps = []
+    distance = lax.axis_size("row") // 2
+    while distance > 1:
+        steps.append(("row", distance))
+        distance //= 2
+    distance = lax.axis_size("col") // 2
+    while distance:
+        steps.append(("col", distance))
+        distance //= 2
+    return steps + [("row", 1)]
+
+
+def owned_order(devices):
+    peers = lax.axis_size("col")
+    order = []
+    for device in range(devices):
+        place = {"row": device // peers, "col": device % peers}
+        bits = [place[axis] // distance % 2 for axis, distance in doubling_steps()]
+        order.append(sum(bit << index for index, bit in enumerate(bits)))
+    return order
+
+
+def gather_halves(own_ref, near_ref, held):
+    core = lax.rem(lax.axis_index("row"), 2)
+    size = own_ref.shape[0]
+    held[pl.ds(pl.multiple_of(core * size, size), size), :] = own_ref[...]
+    held[pl.ds(pl.multiple_of((1 - core) * size, size), size), :] = near_ref[...]
 
 
 def gather_pieces(refs, held):
@@ -193,10 +226,12 @@
     def _():
         for op in range(OPS):
             turned = gram_product(gram_ref[op], window_ref[op])
-            stats_ref[op : op + 1, :] = turned[WINDOW : WINDOW + 1, :]
-            stats_ref[OPS + op : OPS + op + 1, :] = jnp.sum(
+            stats_ref[op : op + 1, :HID] = turned[WINDOW : WINDOW + 1, :]
+            stats_ref[OPS + op : OPS + op + 1, :HID] = jnp.sum(
                 window_ref[op].astype(f32) * turned[:WINDOW, :], axis=0, keepdims=True
             )
+            stats_ref[op : op + 1, HID:] = gram_ref[op, WINDOW : WINDOW + 1, :]
+            stats_ref[OPS + op : OPS + op + 1, HID:] = jnp.zeros((1, LANE), f32)
 
 
 def gram_call(counts, features, w_branch, block):
@@ -210,14 +245,14 @@
             out_specs=[
                 fixed((OPS, WINDOW, HID)),
                 fixed((OPS, LANE, LANE)),
-                fixed((2 * OPS, HID)),
+                fixed((2 * OPS, HID + LANE)),
             ],
             scratch_shapes=[pltpu.VMEM((WIDE, block), bf16)],
         ),
         out_shape=[
             shape((OPS, WINDOW, HID), bf16),
             shape((OPS, LANE, LANE), f32),
-            shape((2 * OPS, HID), f32),
+            shape((2 * OPS, HID + LANE), f32),
         ],
         compiler_params=params(),
         cost_estimate=cost(6),
@@ -269,7 +304,7 @@
             joined, wm_ref[op * HID : (op + 1) * HID, :], preferred_element_type=f32
         )
         pre = term if pre is None else pre + term
-    pre_ref[...] = pre.astype(bf16)
+    pre_ref[...] = pre
     total[0] += fold_rows(pre)
     total[1] += fold_rows(pre * pre)
 
@@ -310,7 +345,7 @@
             ],
         ),
         out_shape=[
-            shape((total, HID), bf16),
+            shape((total, HID), f32),
             shape((total, CAT), bf16),
             shape((total, CAT), bf16),
             shape((CAT, HID), bf16),
@@ -354,7 +389,7 @@
     kind = lax.broadcasted_iota(jnp.int32, (CPAD, HEAD), 0)
     for start in range(0, block, HEAD):
         rows = slice(start, start + HEAD)
-        half = pre_ref[rows, :].astype(f32) * norm[0:1, :] + norm[1:2, :]
+        half = pre_ref[rows, :] * norm[0:1, :] + norm[1:2, :]
         raised = jnp.tanh(half) + 1.0
         hidden = half * raised
         slope = raised * ((half - 0.5 * hidden) + 0.5)
@@ -471,7 +506,7 @@
     mask_rows(counts, x_ref, xa_ref)
     mid = (
         back_ref[...].astype(f32) * norm[0:1, :]
-        - pre_ref[...].astype(f32) * norm[1:2, :]
+        - pre_ref[...] * norm[1:2, :]
         + norm[2:3, :]
     ).astype(bf16)
     mid_ref[...] = mid
@@ -493,20 +528,32 @@
 
     @pl.when(step == pl.num_programs(0) - 1)
     def _():
+        means = add_up(stats_ref)[:, HID:] / all_rows
+        means = jnp.where(
+            lax.broadcasted_iota(jnp.int32, means.shape, 1) < WINDOW, means, 0.0
+        )
+        turned = means.T
         for op in range(OPS):
             start = op * LANE
-            grad[start : start + LANE, HID:] = gram_ref[op]
+            gram = gram_ref[op]
+            mean, column = means[op : op + 1, :], turned[:, op : op + 1]
+            sums, count = gram[WINDOW : WINDOW + 1, :], gram[WINDOW:WINDOW + 1, WINDOW : WINDOW + 1]
+            gram = gram - column * (sums - count * mean) - gram[:, WINDOW : WINDOW + 1] * mean
+            grad[start : start + LANE, HID:] = gram
+            level = grad[start + WINDOW : start + WINDOW + 1, :HID]
             grad[start : start + LANE, :HID] = jnp.concatenate(
                 [
-                    grad[start : start + WINDOW + 1, :HID],
+                    grad[start : start + WINDOW, :HID] - column[:WINDOW] * level,
+                    level,
                     grad_out_ref[op * SHARE : (op + 1) * SHARE, :],
                     jnp.zeros((LANE - WINDOW - 1 - SHARE, HID), f32),
                 ],
                 axis=0,
             )
         size = all_ref.shape[1]
-        for index in range(all_ref.shape[0]):
-            all_ref[index] = grad[index * size : (index + 1) * size, :].astype(bf16)
+        for index, block_index in enumerate(owned_order(all_ref.shape[0])):
+            at = block_index * size
+            all_ref[index] = grad[at : at + size, :].astype(bf16)
 
 
 def branch_back_call(
@@ -604,11 +651,9 @@
     )(mid, joined)
 
 
-def branch_terms(all_rows, mean, scale, window, raw):
+def branch_terms(all_rows, scale, window, raw):
     level = raw[WINDOW : WINDOW + 1, :]
-    inner = scale * (
-        jnp.sum(window.astype(f32) * raw[:WINDOW, :], axis=0, keepdims=True) - mean * level
-    )
+    inner = scale * jnp.sum(window.astype(f32) * raw[:WINDOW, :], axis=0, keepdims=True)
     return level / all_rows, scale * (inner / all_rows)
 
 
@@ -619,22 +664,25 @@
     part_ref,
     stats_ref,
     window_ref,
-    grads,
+    own_ref,
+    near_ref,
     out_ref,
     inner,
     base,
+    grads,
 ):
     step = pl.program_id(0)
     block = x_ref.shape[1]
 
     @pl.when(step == 0)
     def _():
+        gather_halves(own_ref, near_ref, grads)
         stats = add_up(stats_ref)
         for op in range(OPS):
             mean, scale = branch_scale(stats, op, all_rows)
             window = window_ref[op]
             level, slant = branch_terms(
-                all_rows, mean, scale, window, grads[op * LANE : (op + 1) * LANE, :HID].astype(f32)
+                all_rows, scale, window, grads[op * LANE : (op + 1) * LANE, :HID].astype(f32)
             )
             inner[op] = dot_on((window.astype(f32) * -slant).astype(bf16), window, 1, 1).astype(bf16)
             base[op] = jnp.sum(
@@ -656,7 +704,7 @@
     add_windows(moved, write)
 
 
-def rows_back_call(all_rows, counts, features, part, stats, window, grads, block):
+def rows_back_call(all_rows, counts, features, part, stats, window, halves, block):
     total = features.shape[1]
     return pl.pallas_call(
         functools.partial(rows_back_body, all_rows),
@@ -668,19 +716,20 @@
                 columns_of(VALID, block),
                 fixed(stats.shape),
                 fixed((OPS, WINDOW, HID)),
-                fixed(grads.shape),
-            ],
+            ]
+            + [fixed(half.shape) for half in halves],
             out_specs=columns_of(VALID, block),
             scratch_shapes=[
                 pltpu.VMEM((OPS, WINDOW, WINDOW), bf16),
                 pltpu.VMEM((OPS, WINDOW, 1), f32),
+                pltpu.VMEM((OPS * LANE, HID + LANE), bf16),
             ],
         ),
         out_shape=shape((VALID, total), bf16),
         compiler_params=params(),
         cost_estimate=cost(8),
         name="rows_back",
-    )(counts, features, part, stats, window, grads)
+    )(counts, features, part, stats, window, *halves)
 
 
 def slots_of(rows, peers):
@@ -816,7 +865,8 @@
     all_rows,
     stats_ref,
     window_ref,
-    grads,
+    own_ref,
+    near_ref,
     w_ref,
     left_ref,
     right_ref,
@@ -831,11 +881,13 @@
     new_w_ref,
     low_w_ref,
     grad_out_ref,
+    grads,
 ):
     step = pl.program_id(0)
 
     @pl.when(step == 0)
     def _():
+        gather_halves(own_ref, near_ref, grads)
         for op in range(OPS):
             at = op * LANE + WINDOW + 1
             grad_out_ref[op * SHARE : (op + 1) * SHARE, :] = grads[at : at + SHARE, :HID].astype(f32)
@@ -847,11 +899,10 @@
             mean, scale = branch_scale(add_up(stats_ref), op, all_rows)
             window = window_ref[op]
             raw = grads[op * LANE : (op + 1) * LANE, :HID].astype(f32)
-            gram = grads[op * LANE : (op + 1) * LANE, HID:].astype(f32)
-            level, slant = branch_terms(all_rows, mean, scale, window, raw)
-            column = gram[:WINDOW, WINDOW : WINDOW + 1]
-            normed = gram_product(gram, window)[:WINDOW, :] - column * mean
-            grad = raw[:WINDOW, :] - column * level - normed * slant
+            gram = grads[op * LANE : (op + 1) * LANE, HID:]
+            level, slant = branch_terms(all_rows, scale, window, raw)
+            normed = jnp.dot(gram, padded(window), preferred_element_type=f32)
+            grad = raw[:WINDOW, :] - normed[:WINDOW, :] * slant
             shift = op * (DIN - STRIDE)
             grad = grad[shift : shift + DIN, :]
             new_left_ref[:, op, :] = factor(left_ref[:, op, :], grad, 1)
@@ -872,14 +923,15 @@
 
 
 def branch_update_call(
-    all_rows, stats, window, grads, w, left, right, basis_left, basis_right, first, second
+    all_rows, stats, window, halves, w, left, right, basis_left, basis_right, first, second
 ):
     small, wide = fixed((DIN, OPS, DIN)), fixed((DIN, OPS, HID))
     square = pl.BlockSpec((1, HID, HID), lambda k: (k, 0, 0))
     return pl.pallas_call(
         functools.partial(branch_update_body, all_rows),
         grid=(OPS,),
-        in_specs=[fixed(stats.shape), fixed((OPS, WINDOW, HID)), fixed(grads.shape)]
+        in_specs=[fixed(stats.shape), fixed((OPS, WINDOW, HID))]
+        + [fixed(half.shape) for half in halves]
         + [wide, small, square, small, square, wide, wide],
         out_specs=[small, square, wide, wide, wide, wide, fixed((CPAD, HID))],
         out_shape=[
@@ -891,10 +943,11 @@
             shape((DIN, OPS, HID), bf16),
             shape((CPAD, HID), f32),
         ],
+        scratch_shapes=[pltpu.VMEM((OPS * LANE, HID + LANE), bf16)],
         compiler_params=params(),
         cost_estimate=cost(12),
         name="branch_update",
-    )(stats, window, grads, w, left, right, basis_left, basis_right, first, second)
+    )(stats, window, *halves, w, left, right, basis_left, basis_right, first, second)
 
 
 def out_update_body(
@@ -968,21 +1021,47 @@
     )(grad, w, basis, first, second)
 
 
+def half_blocks():
+    parts = HID // LANE
+    return [(i, j) for i in range(parts) for j in range(i, parts)]
+
+
 def mid_gram_body(rows_ref, out_ref):
     rows = rows_ref[...]
-    out_ref[...] = dot_on(rows, rows, 0, 0).astype(bf16)
+    gram = dot_on(rows, rows, 0, 0)
+    for index, (i, j) in enumerate(half_blocks()):
+        out_ref[index] = gram[i * LANE : (i + 1) * LANE, j * LANE : (j + 1) * LANE].astype(bf16)
 
 
 def mid_gram_call(rows):
     return pl.pallas_call(
         mid_gram_body,
-        out_shape=shape((HID, HID), bf16),
+        out_shape=shape((len(half_blocks()), LANE, LANE), bf16),
         compiler_params=params(),
         cost_estimate=cost(2),
         name="mid_gram",
     )(rows)
 
 
+def mid_factor_body(right_ref, own_ref, near_ref, out_ref):
+    for index, (i, j) in enumerate(half_blocks()):
+        block = (1.0 - beta_factor) * (own_ref[index] + near_ref[index])
+        rows, columns = slice(i * LANE, (i + 1) * LANE), slice(j * LANE, (j + 1) * LANE)
+        out_ref[rows, columns] = beta_factor * right_ref[rows, columns] + block
+        if i != j:
+            out_ref[columns, rows] = beta_factor * right_ref[columns, rows] + block.T
+
+
+def mid_factor_call(right, own, near):
+    return pl.pallas_call(
+        mid_factor_body,
+        out_shape=shape((HID, HID), f32),
+        compiler_params=params(),
+        cost_estimate=cost(2),
+        name="mid_factor",
+    )(right, own, near)
+
+
 def after(values, *others):
     return lax.optimization_barrier((values,) + others)[0]
 
@@ -990,6 +1069,19 @@
 def swap(values, axis, distance):
     peers = lax.axis_size(axis)
     return lax.ppermute(values, axis, [(peer, peer ^ distance) for peer in range(peers)])
+
+
+def gather_by_doubling(values):
+    steps = doubling_steps()
+    for axis, distance in steps[:-1]:
+        other = swap(values, axis, distance)
+        bit = lax.rem(lax.axis_index(axis) // distance, 2) > 0
+        values = jnp.where(
+            bit,
+            jnp.concatenate([other, values], axis=0),
+            jnp.concatenate([values, other], axis=0),
+        )
+    return values, swap(values, *steps[-1])
 
 
 def add_all(values):
@@ -1117,26 +1209,25 @@
     parts = mid_grad_call(groups, mid, joined, 1024)
     grad_branch, *parts = lax.optimization_barrier((grad_branch, *parts))
     kept, sent = parts[:2], parts[2:]
-    grad_branch = jnp.sum(grad_branch.astype(f32), axis=0, keepdims=True).astype(bf16)
-    grad_branch = jnp.broadcast_to(grad_branch, (devices,) + grad_branch.shape[1:])
-    grad_branch = lax.all_to_all(grad_branch, BOTH, 0, 0, tiled=True)
+    grad_branch = jnp.sum(grad_branch.astype(f32), axis=0).astype(bf16)
     near = [swap(part, "row", 1) for part in sent]
+    halves = [half.reshape(-1, HID + LANE) for half in gather_by_doubling(grad_branch)]
     away = (kept[1] + near[1]).astype(bf16)
     far = swap(away, "row", groups // 2)
-    collected = collect_call(counts, after(dealt, away))
-    far, grad_branch, collected = lax.optimization_barrier((far, grad_branch, collected))
     grad_mid = finish_scatter(kept[0] + near[0] + far.astype(f32), 2)
-    grad_branch = grad_branch.reshape(OPS * LANE, HID + LANE)
     grad_features = rows_back_call(
-        all_rows, counts, turned, part, branch_stats, window, grad_branch, 4096
-    )
-    grad_mid, grad_features = lax.optimization_barrier((grad_mid, grad_features))
+        all_rows, counts, turned, part, branch_stats, window, halves, 4096
+    )
+    collected = collect_call(counts, after(dealt, grad_features))
+    grad_mid, grad_features, collected = lax.optimization_barrier(
+        (grad_mid, grad_features, collected)
+    )
     all_mid = spread_out(grad_mid, bf16).reshape(-1, HID)
     *branch_parts, grad_out = branch_update_call(
         all_rows,
         branch_stats,
         window,
-        grad_branch,
+        halves,
         by_input(w_branch),
         by_input(left_branch),
         right_branch,
@@ -1147,13 +1238,15 @@
     )
     held = lax.optimization_barrier((all_mid, *branch_parts))
     all_mid, branch_parts = held[0], held[1:]
+    collected = exchange(after(collected, all_mid))
     mid_gram = mid_gram_call(all_mid)
-    collected = exchange(after(collected, mid_gram))
     distance = groups // 2
     others = swap(mid_gram, "row", distance)
-    mid_parts = mid_update_call(grad_mid, w_mid, basis_right_mid, first_mid, second_mid)
+    mid_parts = mid_update_call(
+        after(grad_mid, mid_gram), w_mid, basis_right_mid, first_mid, second_mid
+    )
     out_parts = out_update_call(
-        grad_out,
+        after(grad_out, mid_gram),
         w_out.T,
         left_out,
         right_out,
@@ -1162,16 +1255,18 @@
         first_out.T,
         second_out.T,
     )
-    mid_gram, others, collected, *held = lax.optimization_barrier(
-        (mid_gram, others, collected, *mid_parts, *out_parts)
+    mid_gram, others, *held = lax.optimization_barrier(
+        (mid_gram, others, *mid_parts, *out_parts)
     )
     mid_parts, out_parts = held[:4], held[4:]
     mid_gram = mid_gram.astype(f32) + others.astype(f32)
-    while distance > 1:
+    while distance > 2:
         distance //= 2
         mid_gram = mid_gram + swap(mid_gram, "row", distance)
-    new_right_mid = beta_factor * right_mid + (1.0 - beta_factor) * mid_gram
-    new_logits = join_call(collected)
+    others = swap(mid_gram, "row", 1)
+    new_logits = join_call(after(collected, mid_gram))
+    others, new_logits = lax.optimization_barrier((others, new_logits))
+    new_right_mid = mid_factor_call(right_mid, mid_gram, others)
     branch_parts = [
         part if index == 1 else by_input(part) for index, part in enumerate(branch_parts)
     ]

time: 306 us -> 299 us (0.977)
  waiting for transfers between devices: 37 us -> 26.1 us
    all_to_all x2 -> x1, waiting for transfers between devices: 12.1 us -> 0.01 us  [local(): grad_branch = lax.all_to_all(grad_branch, BOTH, 0, 0, tiled=True)]
    ppermute x11 -> x16, starting transfers between devices: 6.94 us -> 15.3 us  [swap(): lax.ppermute(values, axis, [(peer, peer ^ distance) for peer in range(pee...]
    all_to_all x2 -> x1, starting transfers between devices: 11.2 us -> 5.31 us  [local(): grad_branch = lax.all_to_all(grad_branch, BOTH, 0, 0, tiled=True)]
    ppermute x11 -> x16, waiting for transfers between devices: 13 us -> 15.4 us  [swap(): lax.ppermute(values, axis, [(peer, peer ^ distance) for peer in range(pee...]
  transfers between devices with their start and end apart: 19 -> 23, of which waited for: 11 -> 13; matrix products, arithmetic and copies ran while one was open for 1% -> 2% of each run, Pallas kernels for 38% -> 39%
where the time goes in v1:
time: 299 us; the launch traced here: 298 us
  Pallas kernels  186 us (62%)
  starting transfers between devices  48.3 us (16%)
  waiting for transfers between devices  26.1 us (9%)
  blocking collectives  24.6 us (8%)
  local copies, waits for them, and re-layouts  6.52 us (2%)
  other arithmetic  5.72 us (2%)
    pallas_call x1, Pallas kernels, forward_call(): pl.pallas_call(functools.partial(forward_body, all_rows, count), grid_spe...  48.9 us
    pallas_call x1, Pallas kernels, branch_back_call(): pl.pallas_call(functools.partial(branch_back_body, all_rows), grid_spec=p...  44.1 us
    all_to_all x5, starting transfers between devices, exchange(): return lax.all_to_all(values, 'col', 0, 0, tiled=True)  25.1 us
    pallas_call x1, Pallas kernels, mid_grad_call(): pl.pallas_call(mid_grad_body, grid=(total // block,), in_specs=[rows_of(b...  24.6 us
    pallas_call x1, Pallas kernels, head_call(): pl.pallas_call(functools.partial(head_body, all_rows), grid_spec=pltpu.Pr...  16.7 us
    ppermute x16, waiting for transfers between devices, swap(): lax.ppermute(values, axis, [(peer, peer ^ distance) for peer in range(pee...  15.4 us
    ppermute x16, starting transfers between devices, swap(): lax.ppermute(values, axis, [(peer, peer ^ distance) for peer in range(pee...  15.3 us
    pallas_call x1, Pallas kernels, branch_update_call(): pl.pallas_call(functools.partial(branch_update_body, all_rows), grid=(OPS...  14.8 us
  transfers between devices with their start and end apart: 23, of which 13 were waited for; matrix products, arithmetic and copies ran while one was open for 2% of the time, Pallas kernels for 39%

profile of v1, /device:TPU:0, one launch (start us, length us, event | category | flops | bytes accessed | tf_op | source)
XLA Modules:
  0.0 297.7 jit_solution(11789373418744987496)
XLA Ops:
  2.4 7.3 %all-to-all-start = ((bf16[8,64,512]{2,1,0:T(8,128)(2,1)}), bf16[8,64,512]{2,1,0:T(8,128)(2,1)S(1)}, u32[]{:S(2)}, u32[]{:S(2)}) async-start(bf16[8,64,512]{2,1,0:T(8,128)(2,1)} %broadcast_in_dim.6), calls=%async_computation | async-start | bytes 1048576 | tf_op jit(solution)/shard_map/all_to_all | solution.py:1094
  9.7 7.6 %row_moments.1 = (bf16[4,112,512]{2,1,0:T(8,128)(2,1)}, f32[4,128,128]{2,1,0:T(8,128)}, f32[8,640]{1,0:T(8,128)}) custom-call(s32[4,8]{1,0:T(4,128)} %counts.13, bf16[400,8192]{1,0:T(8,128)(2,1)} %bitcast.28, f32[100,4,512]{2,1,0:T(4,128)} %bitcast.32), custom_call_target="tpu_custom_call" | custom-call | flops 6000000000 | bytes 1 | tf_op jit(solution)/shard_map/row_moments/pallas_call | solution.py:239
  19.1 2.1 collective-permute-done.1
  25.7 11.7 %all_to_all.45.refs_1_.stats_ref = f32[8,8,640]{2,1,0:T(8,128)} all-to-all(f32[8,8,640]{2,1,0:T(8,128)S(1)} %broadcast_in_dim.7), channel_id=1, replica_groups=mesh['row'=4,'col'=8] {'col'}, dimensions={0} | all-to-all | bytes 327680 | tf_op jit(solution)/shard_map/all_to_all | solution.py:1094
  40.8 48.9 %forward_layers.1 = (f32[8192,512]{1,0:T(8,128)}, bf16[8192,2048]{1,0:T(8,128)(2,1)}, bf16[8192,2048]{1,0:T(8,128)(2,1)}, bf16[2048,512]{1,0:T(8,128)(2,1)}, f32[32,8,128]{2,1,0:T(8,128)}) custom-call(s32[4,8]{1,0:T(4,128)} %counts.13, bf16[400,8192]{1,0:T(8,128)(2,1)} %bitcast.29, f32[8,8,640]{2,1,0:T(8,128)} %all_to_all.45.refs_1_.stats_ref, ...), custom_call_target="tpu_custom_call" | custom-call | flops 44000002048 | bytes 1 | tf_op jit(solution)/shard_map/forward_layers/pallas_call | solution.py:323
  89.7 12.9 %all_to_all.46.stats_ref.mid_stats_ref = f32[32,8,128]{2,1,0:T(8,128)} all-to-all(f32[32,8,128]{2,1,0:T(8,128)} %get-tuple-element.104), channel_id=1, replica_groups=mesh['row'=4,'col'=8] {'row','col'}, dimensions={0} | all-to-all | bytes 262144 | tf_op jit(solution)/shard_map/all_to_all | solution.py:1181
  102.7 16.7 %head.1 = (bf16[8192,512]{1,0:T(8,128)(2,1)}, bf16[48,8192]{1,0:T(8,128)(2,1)}, f32[48,512]{1,0:T(8,128)}, f32[32,8,128]{2,1,0:T(8,128)}) custom-call(s32[4,8]{1,0:T(4,128)} %counts.13, f32[8192,512]{1,0:T(8,128)} %get-tuple-element.103.pre_ref, f32[32,8,128]{2,1,0:T(8,128)} %all_to_all.46.stats_ref.mid_stats_ref, f32[47,512]{1,0:T(8,128)} %bitcast.38, ...), custom_call_target="tpu_custom_call" | custom-call | flops 17999998976 | bytes 1 | tf_op jit(solution)/shard_map/head/pallas_call | solution.py:424
  119.3 2.6 all-to-all-start.3
  121.9 3.1 %deal_logits.1 = bf16[8,48,1152]{2,1,0:T(8,128)(2,1)} custom-call(s32[4,8]{1,0:T(4,128)} %counts.13, bf16[48,8192]{1,0:T(8,128)(2,1)} %get-tuple-element.109.logits_ref), custom_call_target="tpu_custom_call" | custom-call | flops 3000000000 | bytes 1 | tf_op jit(solution)/shard_map/deal_logits/pallas_call | solution.py:772
  125.0 4.6 %all-to-all-done.3.sums_ref = f32[32,8,128]{2,1,0:T(8,128)S(1)} async-done(((f32[32,8,128]{2,1,0:T(8,128)}), f32[32,8,128]{2,1,0:T(8,128)S(1)}, u32[]{:S(2)}, u32[]{:S(2)}) %all-to-all-start.3) | async-done | bytes 131104 | tf_op jit(solution)/shard_map/all_to_all | solution.py:1185
  129.7 3.7 %all-to-all-start.4 = ((bf16[8,48,1152]{2,1,0:T(8,128)(2,1)}), bf16[8,48,1152]{2,1,0:T(8,128)(2,1)S(1)}, u32[]{:S(2)}, u32[]{:S(2)}) async-start(bf16[8,48,1152]{2,1,0:T(8,128)(2,1)} %deal_logits.1), calls=%async_computation.4 | async-start | bytes 1769472 | tf_op jit(solution)/shard_map/all_to_all | solution.py:1094
  133.4 44.1 %branch_back.1 = (bf16[8192,512]{1,0:T(8,128)(2,1)}, bf16[400,8192]{1,0:T(8,128)(2,1)}, bf16[32,16,640]{2,1,0:T(8,128)(2,1)}) custom-call(s32[4,8]{1,0:T(4,128)} %counts.13, f32[8192,512]{1,0:T(8,128)} %get-tuple-element.103.pre_ref, bf16[8192,512]{1,0:T(8,128)(2,1)} %get-tuple-element.105.back_ref, bf16[8192,2048]{1,0:T(8,128)(2,1)} %get-tuple-element.106.slope_ref, ...), custom_call_target="tpu_custom_call" | custom-call | flops 48000000000 | bytes 1 | tf_op jit(solution)/shard_map/branch_back/pallas_call | solution.py:579
  178.5 5.3 %all-to-all-start.5 = ((bf16[32,16,640]{2,1,0:T(8,128)(2,1)}), bf16[32,16,640]{2,1,0:T(8,128)(2,1)S(1)}, u32[]{:S(2)}, u32[]{:S(2)}) async-start(bf16[32,16,640]{2,1,0:T(8,128)(2,1)} %get-tuple-element.115), calls=%async_computation.5 | async-start | bytes 1310720 | tf_op jit(solution)/shard_map/all_to_all | solution.py:1208
  183.8 24.6 %mid_grad.1 = (f32[1,512,512]{2,1,0:T(8,128)}, f32[1,512,512]{2,1,0:T(8,128)}, f32[1,512,512]{2,1,0:T(8,128)}, f32[1,512,512]{2,1,0:T(8,128)}) custom-call(bf16[8192,512]{1,0:T(8,128)(2,1)} %get-tuple-element.116.mid_ref, bf16[8192,2048]{1,0:T(8,128)(2,1)} %get-tuple-element.117.joined_ref), custom_call_target="tpu_custom_call" | custom-call | flops 24999999488 | bytes 1 | tf_op jit(solution)/shard_map/mid_grad/pallas_call | solution.py:641
  210.9 2.0 collective-permute-done.9
  212.9 2.7 collective-permute-start.10
  220.2 2.9 collective-permute-done.11
  224.7 3.9 %collective-permute-done.12 = bf16[128,640]{1,0:T(8,128)(2,1)S(1)} collective-permute-done((bf16[128,640]{1,0:T(8,128)(2,1)S(1)}, bf16[128,640]{1,0:T(8,128)(2,1)S(1)}, u32[]{:S(2)}, u32[]{:S(2)}) %collective-permute-start.12) | collective-permute-done | bytes 163872 | tf_op jit(solution)/shard_map/ppermute | solution.py:1071
  229.6 2.3 add_convert_fusion
  231.9 4.6 %all-to-all-start.6 = ((bf16[8,64,512]{2,1,0:T(8,128)(2,1)}), bf16[8,64,512]{2,1,0:T(8,128)(2,1)S(1)}, u32[]{:S(2)}, u32[]{:S(2)}) async-start(bf16[8,64,512]{2,1,0:T(8,128)(2,1)} %bitcast.5), calls=%async_computation.6 | async-start | bytes 1048576 | tf_op jit(solution)/shard_map/all_to_all | solution.py:1094
  237.2 8.9 %rows_back.1 = bf16[400,8192]{1,0:T(8,128)(2,1)} custom-call(s32[4,8]{1,0:T(4,128)} %counts.13, bf16[400,8192]{1,0:T(8,128)(2,1)} %bitcast.31, bf16[400,8192]{1,0:T(8,128)(2,1)} %get-tuple-element.126.part_ref, f32[8,8,640]{2,1,0:T(8,128)} %all_to_all.45.refs_1_.stats_ref, bf16[4,112,512]{2,1,0:T(8,128)(2,1)} %get-tuple-element.100.refs_2_.window_ref, ...), custom_call_target="tpu_custom_call" | custom-call | flops 8000000000 | bytes 1 | tf_op jit(solution)/shard_map/rows_back/pallas_call | solution.py:709
  246.1 2.9 collect_logits.1
  249.0 2.7 all-to-all-done.6
  252.6 3.7 %all-to-all-start.7 = ((bf16[8,64,512]{2,1,0:T(8,128)(2,1)}), bf16[8,64,512]{2,1,0:T(8,128)(2,1)S(1)}, u32[]{:S(2)}, u32[]{:S(2)}) async-start(bf16[8,64,512]{2,1,0:T(8,128)(2,1)} %broadcast_in_dim.8), calls=%async_computation.7 | async-start | bytes 1048576 | tf_op jit(solution)/shard_map/all_to_all | solution.py:1094
  256.3 14.8 %branch_update.1 = (f32[100,4,100]{2,1,0:T(4,128)}, f32[4,512,512]{2,1,0:T(8,128)}, f32[100,4,512]{2,1,0:T(4,128)}, f32[100,4,512]{2,1,0:T(4,128)}, f32[100,4,51...) custom-call(f32[8,8,640]{2,1,0:T(8,128)} %all_to_all.45.refs_1_.stats_ref, ...), custom_call_target="tpu_custom_call" | custom-call | flops 12000000000 | bytes 1 | tf_op jit(solution)/shard_map/branch_update/pallas_call | solution.py:930
  271.9 2.2 mid_gram.1
  274.1 5.9 %all-to-all-start.8 = ((bf16[8,48,512]{2,1,0:T(8,128)(2,1)}), bf16[8,48,512]{2,1,0:T(8,128)(2,1)S(1)}, u32[]{:S(2)}, u32[]{:S(2)}) async-start(bf16[8,48,512]{2,1,0:T(8,128)(2,1)} %collect_logits.1), calls=%async_computation.8 | async-start | bytes 786432 | tf_op jit(solution)/shard_map/all_to_all | solution.py:1094
  281.5 4.0 %out_update.1 = (f32[512,512]{1,0:T(8,128)}, f32[47,47]{1,0:T(8,128)}, f32[47,512]{1,0:T(8,128)}, f32[47,512]{1,0:T(8,128)}, f32[47,512]{1,0:T(8,128)}, /*index=5*/bf16[47,512]{1,0:T(8,128)(2,1)}) custom-call(f32[48,512]{1,0:T(8,128)} %get-tuple-element.144.grad_ref, f32[47,512]{1,0:T(8,128)} %bitcast.39, f32[512,512]{1,0:T(8,128)} %left_ref.1, ...), custom_call_target="tpu_custom_call" | custom-call | flops 4000000000 | bytes 1 | tf_op jit(solution)/shard_map/out_update/pallas_call | solution.py:985
  285.4 3.1 %mid_update.1 = (f32[64,512]{1,0:T(8,128)}, f32[64,512]{1,0:T(8,128)}, f32[64,512]{1,0:T(8,128)}, bf16[64,512]{1,0:T(8,128)(2,1)}) custom-call(f32[64,512]{1,0:T(8,128)} %copy-done.2, f32[64,512]{1,0:T(8,128)} %w_ref.1, f32[512,512]{1,0:T(8,128)} %basis_ref.1, f32[64,512]{1,0:T(8,128)} %first_ref.1, f32[64,512]{1,0:T(8,128)} %second_ref.1), custom_call_target="tpu_custom_call" | custom-call | flops 3000000000 | bytes 1 | tf_op jit(solution)/shard_map/mid_update/pallas_call | solution.py:1015
  289.2 2.2 all-to-all-done.8.pieces_ref
  292.1 2.0 join_logits.1
  295.0 2.8 mid_factor.1
  (73 shorter events, 28.2 us)
Async XLA Ops:
  2.4 21.7 %all-to-all-start = ((bf16[8,64,512]{2,1,0:T(8,128)(2,1)}), bf16[8,64,512]{2,1,0:T(8,128)(2,1)S(1)}, u32[]{:S(2)}, u32[]{:S(2)}) async-start(bf16[8,64,512]{2,1,0:T(8,128)(2,1)} %broadcast_in_dim.6), calls=%async_computation | async-start | bytes 1048576 | tf_op jit(solution)/shard_map/all_to_all | solution.py:1094
  17.3 1.9 collective-permute-start
  17.3 4.0 %collective-permute-start.1 = (f32[8,640]{1,0:T(8,128)}, f32[8,640]{1,0:T(8,128)S(1)}, u32[]{:S(2)}, u32[]{:S(2)}) collective-permute-start(f32[8,640]{1,0:T(8,128)} %get-tuple-element.97), channel_id=1, source_target_pairs={{0,16},{8,24},{16,0},{24,8},{1,17},{9,25},{17,1},{25,9},{2,18},{10... | collective-permute-start | bytes 61448 | tf_op jit(solution)/shard_map/ppermute | solution.py:1071
  18.8 3.4 %collective-permute-start.2 = (f32[8,640]{1,0:T(8,128)}, f32[8,640]{1,0:T(8,128)S(1)}, u32[]{:S(2)}, u32[]{:S(2)}) collective-permute-start(f32[8,640]{1,0:T(8,128)} %get-tuple-element.97), channel_id=1, source_target_pairs={{0,24},{8,16},{16,8},{24,0},{1,25},{9,17},{17,9},{25,1},{2,26},{10... | collective-permute-start | bytes 61448 | tf_op jit(solution)/shard_map/ppermute | solution.py:1071
  24.2 15.9 %copy-start.3 = (bf16[8,64,512]{2,1,0:T(8,128)(2,1)}, bf16[8,64,512]{2,1,0:T(8,128)(2,1)S(1)}, u32[]{:S(2)}) copy-start(bf16[8,64,512]{2,1,0:T(8,128)(2,1)S(1)} %all-to-all-done) | copy-start | bytes 1572868
  24.2 13.2 %collective-permute-start.3 = (bf16[512,512]{1,0:T(8,128)(2,1)S(1)}, bf16[512,512]{1,0:T(8,128)(2,1)S(1)}, u32[]{:S(2)}, u32[]{:S(2)}) collective-permute-start(bf16[512,512]{1,0:T(8,128)(2,1)S(1)} %bitcast.24), channel_id=1, source_target_pairs={{0,16},{8,24},{16,0},{24,8},{1,17},{9,25},{17,1},{25,9},{2,18},{10... | collective-permute-start | bytes 1572872 | tf_op jit(solution)/shard_map/ppermute | solution.py:1071
  37.4 2.7 copy-start.10
  37.4 1.9 collective-permute-start.4
  37.4 2.7 collective-permute-start.5
  119.3 10.3 %all-to-all-start.3 = ((f32[32,8,128]{2,1,0:T(8,128)}), f32[32,8,128]{2,1,0:T(8,128)S(1)}, u32[]{:S(2)}, u32[]{:S(2)}) async-start(f32[32,8,128]{2,1,0:T(8,128)} %get-tuple-element.108), calls=%async_computation.3 | async-start | bytes 262144 | tf_op jit(solution)/shard_map/all_to_all | solution.py:1185
  129.7 3.7 %copy-start.8 = (f32[32,8,128]{2,1,0:T(8,128)}, f32[32,8,128]{2,1,0:T(8,128)S(1)}, u32[]{:S(2)}) copy-start(f32[32,8,128]{2,1,0:T(8,128)S(1)} %all-to-all-done.3.sums_ref) | copy-start | bytes 393220
  129.7 47.9 %all-to-all-start.4 = ((bf16[8,48,1152]{2,1,0:T(8,128)(2,1)}), bf16[8,48,1152]{2,1,0:T(8,128)(2,1)S(1)}, u32[]{:S(2)}, u32[]{:S(2)}) async-start(bf16[8,48,1152]{2,1,0:T(8,128)(2,1)} %deal_logits.1), calls=%async_computation.4 | async-start | bytes 1769472 | tf_op jit(solution)/shard_map/all_to_all | solution.py:1094
  177.6 0.9 copy-start
  178.5 29.9 %all-to-all-start.5 = ((bf16[32,16,640]{2,1,0:T(8,128)(2,1)}), bf16[32,16,640]{2,1,0:T(8,128)(2,1)S(1)}, u32[]{:S(2)}, u32[]{:S(2)}) async-start(bf16[32,16,640]{2,1,0:T(8,128)(2,1)} %get-tuple-element.115), calls=%async_computation.5 | async-start | bytes 1310720 | tf_op jit(solution)/shard_map/all_to_all | solution.py:1208
  208.4 7.2 %collective-permute-start.7 = (f32[1,512,512]{2,1,0:T(8,128)}, f32[1,512,512]{2,1,0:T(8,128)S(1)}, u32[]{:S(2)}, u32[]{:S(2)}) collective-permute-start(f32[1,512,512]{2,1,0:T(8,128)} %get-tuple-element.125), channel_id=1, source_target_pairs={{0,8},{8,0},{16,24},{24,16},{1,9},{9,1},{17,25},{25,17},{2,10},{10... | collective-permute-start | bytes 3145736 | tf_op jit(solution)/shard_map/ppermute | solution.py:1071
  208.7 20.0 %collective-permute-start.6 = (f32[1,512,512]{2,1,0:T(8,128)}, f32[1,512,512]{2,1,0:T(8,128)S(1)}, u32[]{:S(2)}, u32[]{:S(2)}) collective-permute-start(f32[1,512,512]{2,1,0:T(8,128)} %get-tuple-element.123), channel_id=1, source_target_pairs={{0,8},{8,0},{16,24},{24,16},{1,9},{9,1},{17,25},{25,17},{2,10},{10... | collective-permute-start | bytes 3145736 | tf_op jit(solution)/shard_map/ppermute | solution.py:1071
  209.0 3.8 %collective-permute-start.9 = (bf16[16,640]{1,0:T(8,128)(2,1)S(1)}, bf16[16,640]{1,0:T(8,128)(2,1)S(1)}, u32[]{:S(2)}, u32[]{:S(2)}) collective-permute-start(bf16[16,640]{1,0:T(8,128)(2,1)S(1)} %reduce_sum.22), channel_id=1, source_target_pairs={{0,16},{8,24},{16,0},{24,8},{1,17},{9,25},{17,1},{25,9},{2,18},{10... | collective-permute-start | bytes 61448 | tf_op jit(solution)/shard_map/ppermute | solution.py:1071
  212.9 5.7 %collective-permute-start.10 = (bf16[32,640]{1,0:T(8,128)(2,1)S(1)}, bf16[32,640]{1,0:T(8,128)(2,1)S(1)}, u32[]{:S(2)}, u32[]{:S(2)}) collective-permute-start(bf16[32,640]{1,0:T(8,128)(2,1)S(1)} %maximum_select_fusion.3), channel_id=1, source_target_pairs={{0,4},{1,5},{2,6},{3,7},{4,0},{5,1},{6,2},{7,3},{8,12},{9,13},{10,... | collective-permute-start | bytes 122888 | tf_op jit(solution)/shard_map/ppermute | solution.py:1071
  217.0 12.6 %collective-permute-start.8 = (bf16[1,512,512]{2,1,0:T(8,128)(2,1)S(1)}, bf16[1,512,512]{2,1,0:T(8,128)(2,1)S(1)}, u32[]{:S(2)}, u32[]{:S(2)}) collective-permute-start(bf16[1,512,512]{2,1,0:T(8,128)(2,1)S(1)} %add_convert_fusion.1), channel_id=1, source_target_pairs={{0,16},{8,24},{16,0},{24,8},{1,17},{9,25},{17,1},{25,9},{2,18},{10... | collective-permute-start | bytes 1572872 | tf_op jit(solution)/shard_map/ppermute | solution.py:1071
  218.6 4.5 %collective-permute-start.11 = (bf16[64,640]{1,0:T(8,128)(2,1)S(1)}, bf16[64,640]{1,0:T(8,128)(2,1)S(1)}, u32[]{:S(2)}, u32[]{:S(2)}) collective-permute-start(bf16[64,640]{1,0:T(8,128)(2,1)S(1)} %maximum_select_fusion.2), channel_id=1, source_target_pairs={{0,2},{1,3},{2,0},{3,1},{4,6},{5,7},{6,4},{7,5},{8,10},{9,11},{10,... | collective-permute-start | bytes 245768 | tf_op jit(solution)/shard_map/ppermute | solution.py:1071
  223.1 5.4 %collective-permute-start.12 = (bf16[128,640]{1,0:T(8,128)(2,1)S(1)}, bf16[128,640]{1,0:T(8,128)(2,1)S(1)}, u32[]{:S(2)}, u32[]{:S(2)}) collective-permute-start(bf16[128,640]{1,0:T(8,128)(2,1)S(1)} %maximum_select_fusion.1), channel_id=1, source_target_pairs={{0,1},{1,0},{2,3},{3,2},{4,5},{5,4},{6,7},{7,6},{8,9},{9,8},{10,11... | collective-permute-start | bytes 491528 | tf_op jit(solution)/shard_map/ppermute | solution.py:1071
  228.6 7.9 %copy-start.7 = (bf16[256,640]{1,0:T(8,128)(2,1)}, bf16[256,640]{1,0:T(8,128)(2,1)S(1)}, u32[]{:S(2)}) copy-start(bf16[256,640]{1,0:T(8,128)(2,1)S(1)} %maximum_select_fusion.own_ref) | copy-start | bytes 983044
  228.6 7.9 %collective-permute-start.13 = (bf16[256,640]{1,0:T(8,128)(2,1)S(1)}, bf16[256,640]{1,0:T(8,128)(2,1)S(1)}, u32[]{:S(2)}, u32[]{:S(2)}) collective-permute-start(bf16[256,640]{1,0:T(8,128)(2,1)S(1)} %maximum_select_fusion.own_ref), channel_id=1, source_target_pairs={{0,8},{8,0},{16,24},{24,16},{1,9},{9,1},{17,25},{25,17},{2,10},{10... | collective-permute-start | bytes 983048 | tf_op jit(solution)/shard_map/ppermute | solution.py:1071
  231.9 19.7 %all-to-all-start.6 = ((bf16[8,64,512]{2,1,0:T(8,128)(2,1)}), bf16[8,64,512]{2,1,0:T(8,128)(2,1)S(1)}, u32[]{:S(2)}, u32[]{:S(2)}) async-start(bf16[8,64,512]{2,1,0:T(8,128)(2,1)} %bitcast.5), calls=%async_computation.6 | async-start | bytes 1048576 | tf_op jit(solution)/shard_map/all_to_all | solution.py:1094
  251.7 19.4 %copy-start.2 = (f32[64,512]{1,0:T(8,128)}, f32[64,512]{1,0:T(8,128)S(1)}, u32[]{:S(2)}) copy-start(f32[64,512]{1,0:T(8,128)S(1)} %convert_reduce_fusion.grad_ref) | copy-start | bytes 393220
  252.6 18.5 %all-to-all-start.7 = ((bf16[8,64,512]{2,1,0:T(8,128)(2,1)}), bf16[8,64,512]{2,1,0:T(8,128)(2,1)S(1)}, u32[]{:S(2)}, u32[]{:S(2)}) async-start(bf16[8,64,512]{2,1,0:T(8,128)(2,1)} %broadcast_in_dim.8), calls=%async_computation.7 | async-start | bytes 1048576 | tf_op jit(solution)/shard_map/all_to_all | solution.py:1094
  274.1 17.3 %all-to-all-start.8 = ((bf16[8,48,512]{2,1,0:T(8,128)(2,1)}), bf16[8,48,512]{2,1,0:T(8,128)(2,1)S(1)}, u32[]{:S(2)}, u32[]{:S(2)}) async-start(bf16[8,48,512]{2,1,0:T(8,128)(2,1)} %collect_logits.1), calls=%async_computation.8 | async-start | bytes 786432 | tf_op jit(solution)/shard_map/all_to_all | solution.py:1094
  280.0 9.0 %collective-permute-start.14 = (bf16[10,128,128]{2,1,0:T(8,128)(2,1)}, bf16[10,128,128]{2,1,0:T(8,128)(2,1)S(1)}, u32[]{:S(2)}, u32[]{:S(2)}) collective-permute-start(bf16[10,128,128]{2,1,0:T(8,128)(2,1)} %mid_gram.1), channel_id=1, source_target_pairs={{0,16},{8,24},{16,0},{24,8},{1,17},{9,25},{17,1},{25,9},{2,18},{10... | collective-permute-start | bytes 983048 | tf_op jit(solution)/shard_map/ppermute | solution.py:1071
  285.4 3.6 %copy-start.6 = (bf16[10,128,128]{2,1,0:T(8,128)(2,1)S(1)}, bf16[10,128,128]{2,1,0:T(8,128)(2,1)}, u32[]{:S(2)}) copy-start(bf16[10,128,128]{2,1,0:T(8,128)(2,1)} %mid_gram.1) | copy-start | bytes 983044
  289.1 5.0 %copy-start.1 = (f32[10,128,128]{2,1,0:T(8,128)}, f32[10,128,128]{2,1,0:T(8,128)S(1)}, u32[]{:S(2)}) copy-start(f32[10,128,128]{2,1,0:T(8,128)S(1)} %convert_add_fusion.own_ref) | copy-start | bytes 1966084
  289.1 5.0 %collective-permute-start.15 = (f32[10,128,128]{2,1,0:T(8,128)S(1)}, f32[10,128,128]{2,1,0:T(8,128)S(1)}, u32[]{:S(2)}, u32[]{:S(2)}) collective-permute-start(f32[10,128,128]{2,1,0:T(8,128)S(1)} %convert_add_fusion.own_ref), channel_id=1, source_target_pairs={{0,8},{8,0},{16,24},{24,16},{1,9},{9,1},{17,25},{25,17},{2,10},{10... | collective-permute-start | bytes 1966088 | tf_op jit(solution)/shard_map/ppermute | solution.py:1071
  294.1 0.9 copy-start.9
  (5 other events, 3.9 us)

commit v2 on v1

--- a/solution.py
+++ b/solution.py
@@ -19,7 +19,8 @@
 STRIDE = 96
 WINDOW = 112
 VALID = 400
-HEAD = 512
+HEAD = 2048
+PART = 256
 WIDE = 416
 SHARE = 12
 BOTH = ("row", "col")
@@ -289,21 +290,22 @@
     pre = None
     for op in range(OPS):
         rows = window_rows(xa_ref, op).T
-        half = jnp.dot(
-            jnp.concatenate([rows, rows], axis=1), wide[op], preferred_element_type=f32
-        ).astype(bf16)
-        first = jnp.tanh(half) + 1.0
-        act = half * first
-        half_act = act * 0.5
-        second = jnp.tanh(half_act) + 1.0
-        joined = half_act * second
-        slope = (first * ((half - half_act) + 0.5)) * (second * ((act - joined) + 1.0))
-        joined_ref[:, op * HID : (op + 1) * HID] = joined
-        slope_ref[:, op * HID : (op + 1) * HID] = slope
-        term = jnp.dot(
-            joined, wm_ref[op * HID : (op + 1) * HID, :], preferred_element_type=f32
-        )
-        pre = term if pre is None else pre + term
+        rows = jnp.concatenate([rows, rows], axis=1)
+        for start in range(0, HID, PART):
+            half = jnp.dot(
+                rows, wide[op, :, start : start + PART], preferred_element_type=f32
+            ).astype(bf16)
+            first = jnp.tanh(half) + 1.0
+            act = half * first
+            half_act = act * 0.5
+            second = jnp.tanh(half_act) + 1.0
+            joined = half_act * second
+            slope = (first * ((half - half_act) + 0.5)) * (second * ((act - joined) + 1.0))
+            span = slice(op * HID + start, op * HID + start + PART)
+            joined_ref[:, span] = joined
+            slope_ref[:, span] = slope
+            term = jnp.dot(joined, wm_ref[span, :], preferred_element_type=f32)
+            pre = term if pre is None else pre + term
     pre_ref[...] = pre
     total[0] += fold_rows(pre)
     total[1] += fold_rows(pre * pre)
@@ -389,12 +391,18 @@
     kind = lax.broadcasted_iota(jnp.int32, (CPAD, HEAD), 0)
     for start in range(0, block, HEAD):
         rows = slice(start, start + HEAD)
-        half = pre_ref[rows, :] * norm[0:1, :] + norm[1:2, :]
-        raised = jnp.tanh(half) + 1.0
-        hidden = half * raised
-        slope = raised * ((half - 0.5 * hidden) + 0.5)
-        hidden = hidden.astype(bf16)
-        logits = dot_on(wo_low[...], hidden, 1, 1)
+        logits = None
+        kept = []
+        for at in range(0, HID, PART):
+            span = slice(at, at + PART)
+            half = pre_ref[rows, span] * norm[0:1, span] + norm[1:2, span]
+            raised = jnp.tanh(half) + 1.0
+            hidden = half * raised
+            slope = raised * ((half - 0.5 * hidden) + 0.5)
+            hidden = hidden.astype(bf16)
+            term = dot_on(wo_low[:, span], hidden, 1, 1)
+            logits = term if logits is None else logits + term
+            kept.append((span, half, hidden, slope))
         logits_ref[:, rows] = logits.astype(bf16)
         column = step * block + start + lax.broadcasted_iota(jnp.int32, (CPAD, HEAD), 1)
         real = kind < CLS
@@ -403,11 +411,12 @@
         probs = powers / jnp.sum(powers, axis=0, keepdims=True)
         score = (probs - jnp.where(kind == labels_ref[:, rows], 1.0, 0.0)) / all_rows
         score = jnp.where(column < own_count(counts), score, 0.0).astype(bf16)
-        grad_ref[...] += dot_on(score, hidden, 1, 0)
-        back = dot_on(score, wo_low[...], 0, 0) * slope
-        total[0] += fold_rows(back)
-        total[1] += fold_rows(back * half)
-        back_ref[rows, :] = back.astype(bf16)
+        for span, half, hidden, slope in kept:
+            grad_ref[:, span] += dot_on(score, hidden, 1, 0)
+            back = dot_on(score, wo_low[:, span], 0, 0) * slope
+            total[0, :, span] += fold_rows(back)
+            total[1, :, span] += fold_rows(back * half)
+            back_ref[rows, span] = back.astype(bf16)
 
     @pl.when(step == pl.num_programs(0) - 1)
     def _():
@@ -1176,7 +1185,7 @@
     branch_stats = spread_out(branch_sums)
     pieces, (branch_stats,) = near_copies(pieces, branch_stats)
     pre, joined, slope, mid_low, mid_sums = forward_call(
-        all_rows, devices, counts, turned, branch_stats, window, pieces, 512
+        all_rows, devices, counts, turned, branch_stats, window, pieces, 1024
     )
     mid_stats = lax.all_to_all(mid_sums, BOTH, 0, 0, tiled=True)
     back, logits, grad_out, back_sums = head_call(

time: 299 us -> 291 us (0.973)
  Pallas kernels: 186 us -> 178 us
    pallas_call x1, Pallas kernels: 48.9 us -> 42.1 us  [forward_call(): pl.pallas_call(functools.partial(forward_body, all_rows, count), grid_spe...]
  transfers between devices with their start and end apart: 23 -> 23, of which waited for: 13 -> 13; matrix products, arithmetic and copies ran while one was open for 2% -> 2% of each run, Pallas kernels for 39% -> 40%
where the time goes in v2:
time: 291 us; the launch traced here: 290 us
  Pallas kernels  178 us (61%)
  starting transfers between devices  48.3 us (17%)
  waiting for transfers between devices  26.1 us (9%)
  blocking collectives  24.6 us (8%)
  local copies, waits for them, and re-layouts  6.52 us (2%)
  other arithmetic  5.72 us (2%)
    pallas_call x1, Pallas kernels, branch_back_call(): pl.pallas_call(functools.partial(branch_back_body, all_rows), grid_spec=p...  44.1 us
    pallas_call x1, Pallas kernels, forward_call(): pl.pallas_call(functools.partial(forward_body, all_rows, count), grid_spe...  42.1 us
    all_to_all x5, starting transfers between devices, exchange(): return lax.all_to_all(values, 'col', 0, 0, tiled=True)  25.1 us
    pallas_call x1, Pallas kernels, mid_grad_call(): pl.pallas_call(mid_grad_body, grid=(total // block,), in_specs=[rows_of(b...  24.6 us
    pallas_call x1, Pallas kernels, head_call(): pl.pallas_call(functools.partial(head_body, all_rows), grid_spec=pltpu.Pr...  15.7 us
    ppermute x16, waiting for transfers between devices, swap(): lax.ppermute(values, axis, [(peer, peer ^ distance) for peer in range(pee...  15.4 us
    ppermute x16, starting transfers between devices, swap(): lax.ppermute(values, axis, [(peer, peer ^ distance) for peer in range(pee...  15.3 us
    pallas_call x1, Pallas kernels, branch_update_call(): pl.pallas_call(functools.partial(branch_update_body, all_rows), grid=(OPS...  14.8 us
  transfers between devices with their start and end apart: 23, of which 13 were waited for; matrix products, arithmetic and copies ran while one was open for 2% of the time, Pallas kernels for 40%

profile of v2, /device:TPU:0, one launch (start us, length us, event | category | flops | bytes accessed | tf_op | source)
XLA Modules:
  0.0 290.0 jit_solution(155316559463630628)
XLA Ops:
  2.4 7.3 %all-to-all-start = ((bf16[8,64,512]{2,1,0:T(8,128)(2,1)}), bf16[8,64,512]{2,1,0:T(8,128)(2,1)S(1)}, u32[]{:S(2)}, u32[]{:S(2)}) async-start(bf16[8,64,512]{2,1,0:T(8,128)(2,1)} %broadcast_in_dim.6), calls=%async_computation | async-start | bytes 1048576 | tf_op jit(solution)/shard_map/all_to_all | solution.py:1103
  9.7 7.6 %row_moments.1 = (bf16[4,112,512]{2,1,0:T(8,128)(2,1)}, f32[4,128,128]{2,1,0:T(8,128)}, f32[8,640]{1,0:T(8,128)}) custom-call(s32[4,8]{1,0:T(4,128)} %counts.13, bf16[400,8192]{1,0:T(8,128)(2,1)} %bitcast.28, f32[100,4,512]{2,1,0:T(4,128)} %bitcast.32), custom_call_target="tpu_custom_call" | custom-call | flops 6000000000 | bytes 1 | tf_op jit(solution)/shard_map/row_moments/pallas_call | solution.py:240
  19.1 2.1 collective-permute-done.1
  25.7 11.7 %all_to_all.45.refs_1_.stats_ref = f32[8,8,640]{2,1,0:T(8,128)} all-to-all(f32[8,8,640]{2,1,0:T(8,128)S(1)} %broadcast_in_dim.7), channel_id=1, replica_groups=mesh['row'=4,'col'=8] {'col'}, dimensions={0} | all-to-all | bytes 327680 | tf_op jit(solution)/shard_map/all_to_all | solution.py:1103
  40.8 42.1 %forward_layers.1 = (f32[8192,512]{1,0:T(8,128)}, bf16[8192,2048]{1,0:T(8,128)(2,1)}, bf16[8192,2048]{1,0:T(8,128)(2,1)}, bf16[2048,512]{1,0:T(8,128)(2,1)}, f32[32,8,128]{2,1,0:T(8,128)}) custom-call(s32[4,8]{1,0:T(4,128)} %counts.13, bf16[400,8192]{1,0:T(8,128)(2,1)} %bitcast.29, f32[8,8,640]{2,1,0:T(8,128)} %all_to_all.45.refs_1_.stats_ref, ...), custom_call_target="tpu_custom_call" | custom-call | flops 44000002048 | bytes 1 | tf_op jit(solution)/shard_map/forward_layers/pallas_call | solution.py:325
  82.9 12.9 %all_to_all.46.stats_ref.mid_stats_ref = f32[32,8,128]{2,1,0:T(8,128)} all-to-all(f32[32,8,128]{2,1,0:T(8,128)} %get-tuple-element.104), channel_id=1, replica_groups=mesh['row'=4,'col'=8] {'row','col'}, dimensions={0} | all-to-all | bytes 262144 | tf_op jit(solution)/shard_map/all_to_all | solution.py:1190
  95.9 15.7 %head.1 = (bf16[8192,512]{1,0:T(8,128)(2,1)}, bf16[48,8192]{1,0:T(8,128)(2,1)}, f32[48,512]{1,0:T(8,128)}, f32[32,8,128]{2,1,0:T(8,128)}) custom-call(s32[4,8]{1,0:T(4,128)} %counts.13, f32[8192,512]{1,0:T(8,128)} %get-tuple-element.103.pre_ref, f32[32,8,128]{2,1,0:T(8,128)} %all_to_all.46.stats_ref.mid_stats_ref, f32[47,512]{1,0:T(8,128)} %bitcast.38, ...), custom_call_target="tpu_custom_call" | custom-call | flops 17999998976 | bytes 1 | tf_op jit(solution)/shard_map/head/pallas_call | solution.py:433
  111.6 2.6 all-to-all-start.3
  114.2 3.1 %deal_logits.1 = bf16[8,48,1152]{2,1,0:T(8,128)(2,1)} custom-call(s32[4,8]{1,0:T(4,128)} %counts.13, bf16[48,8192]{1,0:T(8,128)(2,1)} %get-tuple-element.109.logits_ref), custom_call_target="tpu_custom_call" | custom-call | flops 3000000000 | bytes 1 | tf_op jit(solution)/shard_map/deal_logits/pallas_call | solution.py:781
  117.3 4.6 %all-to-all-done.3.sums_ref = f32[32,8,128]{2,1,0:T(8,128)S(1)} async-done(((f32[32,8,128]{2,1,0:T(8,128)}), f32[32,8,128]{2,1,0:T(8,128)S(1)}, u32[]{:S(2)}, u32[]{:S(2)}) %all-to-all-start.3) | async-done | bytes 131104 | tf_op jit(solution)/shard_map/all_to_all | solution.py:1194
  121.9 3.7 %all-to-all-start.4 = ((bf16[8,48,1152]{2,1,0:T(8,128)(2,1)}), bf16[8,48,1152]{2,1,0:T(8,128)(2,1)S(1)}, u32[]{:S(2)}, u32[]{:S(2)}) async-start(bf16[8,48,1152]{2,1,0:T(8,128)(2,1)} %deal_logits.1), calls=%async_computation.4 | async-start | bytes 1769472 | tf_op jit(solution)/shard_map/all_to_all | solution.py:1103
  125.7 44.1 %branch_back.1 = (bf16[8192,512]{1,0:T(8,128)(2,1)}, bf16[400,8192]{1,0:T(8,128)(2,1)}, bf16[32,16,640]{2,1,0:T(8,128)(2,1)}) custom-call(s32[4,8]{1,0:T(4,128)} %counts.13, f32[8192,512]{1,0:T(8,128)} %get-tuple-element.103.pre_ref, bf16[8192,512]{1,0:T(8,128)(2,1)} %get-tuple-element.105.back_ref, bf16[8192,2048]{1,0:T(8,128)(2,1)} %get-tuple-element.106.slope_ref, ...), custom_call_target="tpu_custom_call" | custom-call | flops 48000000000 | bytes 1 | tf_op jit(solution)/shard_map/branch_back/pallas_call | solution.py:588
  170.7 5.3 %all-to-all-start.5 = ((bf16[32,16,640]{2,1,0:T(8,128)(2,1)}), bf16[32,16,640]{2,1,0:T(8,128)(2,1)S(1)}, u32[]{:S(2)}, u32[]{:S(2)}) async-start(bf16[32,16,640]{2,1,0:T(8,128)(2,1)} %get-tuple-element.115), calls=%async_computation.5 | async-start | bytes 1310720 | tf_op jit(solution)/shard_map/all_to_all | solution.py:1217
  176.1 24.6 %mid_grad.1 = (f32[1,512,512]{2,1,0:T(8,128)}, f32[1,512,512]{2,1,0:T(8,128)}, f32[1,512,512]{2,1,0:T(8,128)}, f32[1,512,512]{2,1,0:T(8,128)}) custom-call(bf16[8192,512]{1,0:T(8,128)(2,1)} %get-tuple-element.116.mid_ref, bf16[8192,2048]{1,0:T(8,128)(2,1)} %get-tuple-element.117.joined_ref), custom_call_target="tpu_custom_call" | custom-call | flops 24999999488 | bytes 1 | tf_op jit(solution)/shard_map/mid_grad/pallas_call | solution.py:650
  203.1 2.0 collective-permute-done.9
  205.2 2.7 collective-permute-start.10
  212.4 2.9 %collective-permute-done.11 = bf16[64,640]{1,0:T(8,128)(2,1)S(1)} collective-permute-done((bf16[64,640]{1,0:T(8,128)(2,1)S(1)}, bf16[64,640]{1,0:T(8,128)(2,1)S(1)}, u32[]{:S(2)}, u32[]{:S(2)}) %collective-permute-start.11) | collective-permute-done | bytes 81952 | tf_op jit(solution)/shard_map/ppermute | solution.py:1080
  216.9 3.9 %collective-permute-done.12 = bf16[128,640]{1,0:T(8,128)(2,1)S(1)} collective-permute-done((bf16[128,640]{1,0:T(8,128)(2,1)S(1)}, bf16[128,640]{1,0:T(8,128)(2,1)S(1)}, u32[]{:S(2)}, u32[]{:S(2)}) %collective-permute-start.12) | collective-permute-done | bytes 163872 | tf_op jit(solution)/shard_map/ppermute | solution.py:1080
  221.9 2.3 add_convert_fusion
  224.2 4.6 %all-to-all-start.6 = ((bf16[8,64,512]{2,1,0:T(8,128)(2,1)}), bf16[8,64,512]{2,1,0:T(8,128)(2,1)S(1)}, u32[]{:S(2)}, u32[]{:S(2)}) async-start(bf16[8,64,512]{2,1,0:T(8,128)(2,1)} %bitcast.5), calls=%async_computation.6 | async-start | bytes 1048576 | tf_op jit(solution)/shard_map/all_to_all | solution.py:1103
  229.5 8.9 %rows_back.1 = bf16[400,8192]{1,0:T(8,128)(2,1)} custom-call(s32[4,8]{1,0:T(4,128)} %counts.13, bf16[400,8192]{1,0:T(8,128)(2,1)} %bitcast.31, bf16[400,8192]{1,0:T(8,128)(2,1)} %get-tuple-element.126.part_ref, f32[8,8,640]{2,1,0:T(8,128)} %all_to_all.45.refs_1_.stats_ref, bf16[4,112,512]{2,1,0:T(8,128)(2,1)} %get-tuple-element.100.refs_2_.window_ref, ...), custom_call_target="tpu_custom_call" | custom-call | flops 8000000000 | bytes 1 | tf_op jit(solution)/shard_map/rows_back/pallas_call | solution.py:718
  238.3 2.9 collect_logits.1
  241.2 2.7 all-to-all-done.6
  244.8 3.7 %all-to-all-start.7 = ((bf16[8,64,512]{2,1,0:T(8,128)(2,1)}), bf16[8,64,512]{2,1,0:T(8,128)(2,1)S(1)}, u32[]{:S(2)}, u32[]{:S(2)}) async-start(bf16[8,64,512]{2,1,0:T(8,128)(2,1)} %broadcast_in_dim.8), calls=%async_computation.7 | async-start | bytes 1048576 | tf_op jit(solution)/shard_map/all_to_all | solution.py:1103
  248.5 14.8 %branch_update.1 = (f32[100,4,100]{2,1,0:T(4,128)}, f32[4,512,512]{2,1,0:T(8,128)}, f32[100,4,512]{2,1,0:T(4,128)}, f32[100,4,512]{2,1,0:T(4,128)}, f32[100,4,51...) custom-call(f32[8,8,640]{2,1,0:T(8,128)} %all_to_all.45.refs_1_.stats_ref, ...), custom_call_target="tpu_custom_call" | custom-call | flops 12000000000 | bytes 1 | tf_op jit(solution)/shard_map/branch_update/pallas_call | solution.py:939
  264.1 2.2 mid_gram.1
  266.4 5.9 %all-to-all-start.8 = ((bf16[8,48,512]{2,1,0:T(8,128)(2,1)}), bf16[8,48,512]{2,1,0:T(8,128)(2,1)S(1)}, u32[]{:S(2)}, u32[]{:S(2)}) async-start(bf16[8,48,512]{2,1,0:T(8,128)(2,1)} %collect_logits.1), calls=%async_computation.8 | async-start | bytes 786432 | tf_op jit(solution)/shard_map/all_to_all | solution.py:1103
  273.7 4.0 %out_update.1 = (f32[512,512]{1,0:T(8,128)}, f32[47,47]{1,0:T(8,128)}, f32[47,512]{1,0:T(8,128)}, f32[47,512]{1,0:T(8,128)}, f32[47,512]{1,0:T(8,128)}, /*index=5*/bf16[47,512]{1,0:T(8,128)(2,1)}) custom-call(f32[48,512]{1,0:T(8,128)} %get-tuple-element.144.grad_ref, f32[47,512]{1,0:T(8,128)} %bitcast.39, f32[512,512]{1,0:T(8,128)} %left_ref.1, ...), custom_call_target="tpu_custom_call" | custom-call | flops 4000000000 | bytes 1 | tf_op jit(solution)/shard_map/out_update/pallas_call | solution.py:994
  277.7 3.1 %mid_update.1 = (f32[64,512]{1,0:T(8,128)}, f32[64,512]{1,0:T(8,128)}, f32[64,512]{1,0:T(8,128)}, bf16[64,512]{1,0:T(8,128)(2,1)}) custom-call(f32[64,512]{1,0:T(8,128)} %copy-done.2, f32[64,512]{1,0:T(8,128)} %w_ref.1, f32[512,512]{1,0:T(8,128)} %basis_ref.1, f32[64,512]{1,0:T(8,128)} %first_ref.1, f32[64,512]{1,0:T(8,128)} %second_ref.1), custom_call_target="tpu_custom_call" | custom-call | flops 3000000000 | bytes 1 | tf_op jit(solution)/shard_map/mid_update/pallas_call | solution.py:1024
  281.5 2.2 all-to-all-done.8.pieces_ref
  284.4 2.0 join_logits.1
  287.2 2.8 mid_factor.1
  (73 shorter events, 28.2 us)
Async XLA Ops:
  2.4 21.7 %all-to-all-start = ((bf16[8,64,512]{2,1,0:T(8,128)(2,1)}), bf16[8,64,512]{2,1,0:T(8,128)(2,1)S(1)}, u32[]{:S(2)}, u32[]{:S(2)}) async-start(bf16[8,64,512]{2,1,0:T(8,128)(2,1)} %broadcast_in_dim.6), calls=%async_computation | async-start | bytes 1048576 | tf_op jit(solution)/shard_map/all_to_all | solution.py:1103
  17.3 1.9 collective-permute-start
  17.3 4.0 %collective-permute-start.1 = (f32[8,640]{1,0:T(8,128)}, f32[8,640]{1,0:T(8,128)S(1)}, u32[]{:S(2)}, u32[]{:S(2)}) collective-permute-start(f32[8,640]{1,0:T(8,128)} %get-tuple-element.97), channel_id=1, source_target_pairs={{0,16},{8,24},{16,0},{24,8},{1,17},{9,25},{17,1},{25,9},{2,18},{10... | collective-permute-start | bytes 61448 | tf_op jit(solution)/shard_map/ppermute | solution.py:1080
  18.8 3.4 %collective-permute-start.2 = (f32[8,640]{1,0:T(8,128)}, f32[8,640]{1,0:T(8,128)S(1)}, u32[]{:S(2)}, u32[]{:S(2)}) collective-permute-start(f32[8,640]{1,0:T(8,128)} %get-tuple-element.97), channel_id=1, source_target_pairs={{0,24},{8,16},{16,8},{24,0},{1,25},{9,17},{17,9},{25,1},{2,26},{10... | collective-permute-start | bytes 61448 | tf_op jit(solution)/shard_map/ppermute | solution.py:1080
  24.2 15.9 %copy-start.3 = (bf16[8,64,512]{2,1,0:T(8,128)(2,1)}, bf16[8,64,512]{2,1,0:T(8,128)(2,1)S(1)}, u32[]{:S(2)}) copy-start(bf16[8,64,512]{2,1,0:T(8,128)(2,1)S(1)} %all-to-all-done) | copy-start | bytes 1572868
  24.2 13.2 %collective-permute-start.3 = (bf16[512,512]{1,0:T(8,128)(2,1)S(1)}, bf16[512,512]{1,0:T(8,128)(2,1)S(1)}, u32[]{:S(2)}, u32[]{:S(2)}) collective-permute-start(bf16[512,512]{1,0:T(8,128)(2,1)S(1)} %bitcast.24), channel_id=1, source_target_pairs={{0,16},{8,24},{16,0},{24,8},{1,17},{9,25},{17,1},{25,9},{2,18},{10... | collective-permute-start | bytes 1572872 | tf_op jit(solution)/shard_map/ppermute | solution.py:1080
  37.4 2.7 copy-start.10
  37.4 1.9 collective-permute-start.4
  37.4 2.7 collective-permute-start.5
  111.6 10.3 %all-to-all-start.3 = ((f32[32,8,128]{2,1,0:T(8,128)}), f32[32,8,128]{2,1,0:T(8,128)S(1)}, u32[]{:S(2)}, u32[]{:S(2)}) async-start(f32[32,8,128]{2,1,0:T(8,128)} %get-tuple-element.108), calls=%async_computation.3 | async-start | bytes 262144 | tf_op jit(solution)/shard_map/all_to_all | solution.py:1194
  121.9 3.7 %copy-start.8 = (f32[32,8,128]{2,1,0:T(8,128)}, f32[32,8,128]{2,1,0:T(8,128)S(1)}, u32[]{:S(2)}) copy-start(f32[32,8,128]{2,1,0:T(8,128)S(1)} %all-to-all-done.3.sums_ref) | copy-start | bytes 393220
  121.9 47.9 %all-to-all-start.4 = ((bf16[8,48,1152]{2,1,0:T(8,128)(2,1)}), bf16[8,48,1152]{2,1,0:T(8,128)(2,1)S(1)}, u32[]{:S(2)}, u32[]{:S(2)}) async-start(bf16[8,48,1152]{2,1,0:T(8,128)(2,1)} %deal_logits.1), calls=%async_computation.4 | async-start | bytes 1769472 | tf_op jit(solution)/shard_map/all_to_all | solution.py:1103
  169.8 0.9 copy-start
  170.7 30.0 %all-to-all-start.5 = ((bf16[32,16,640]{2,1,0:T(8,128)(2,1)}), bf16[32,16,640]{2,1,0:T(8,128)(2,1)S(1)}, u32[]{:S(2)}, u32[]{:S(2)}) async-start(bf16[32,16,640]{2,1,0:T(8,128)(2,1)} %get-tuple-element.115), calls=%async_computation.5 | async-start | bytes 1310720 | tf_op jit(solution)/shard_map/all_to_all | solution.py:1217
  200.7 7.2 %collective-permute-start.7 = (f32[1,512,512]{2,1,0:T(8,128)}, f32[1,512,512]{2,1,0:T(8,128)S(1)}, u32[]{:S(2)}, u32[]{:S(2)}) collective-permute-start(f32[1,512,512]{2,1,0:T(8,128)} %get-tuple-element.125), channel_id=1, source_target_pairs={{0,8},{8,0},{16,24},{24,16},{1,9},{9,1},{17,25},{25,17},{2,10},{10... | collective-permute-start | bytes 3145736 | tf_op jit(solution)/shard_map/ppermute | solution.py:1080
  200.9 20.0 %collective-permute-start.6 = (f32[1,512,512]{2,1,0:T(8,128)}, f32[1,512,512]{2,1,0:T(8,128)S(1)}, u32[]{:S(2)}, u32[]{:S(2)}) collective-permute-start(f32[1,512,512]{2,1,0:T(8,128)} %get-tuple-element.123), channel_id=1, source_target_pairs={{0,8},{8,0},{16,24},{24,16},{1,9},{9,1},{17,25},{25,17},{2,10},{10... | collective-permute-start | bytes 3145736 | tf_op jit(solution)/shard_map/ppermute | solution.py:1080
  201.3 3.8 %collective-permute-start.9 = (bf16[16,640]{1,0:T(8,128)(2,1)S(1)}, bf16[16,640]{1,0:T(8,128)(2,1)S(1)}, u32[]{:S(2)}, u32[]{:S(2)}) collective-permute-start(bf16[16,640]{1,0:T(8,128)(2,1)S(1)} %reduce_sum.22), channel_id=1, source_target_pairs={{0,16},{8,24},{16,0},{24,8},{1,17},{9,25},{17,1},{25,9},{2,18},{10... | collective-permute-start | bytes 61448 | tf_op jit(solution)/shard_map/ppermute | solution.py:1080
  205.2 5.7 %collective-permute-start.10 = (bf16[32,640]{1,0:T(8,128)(2,1)S(1)}, bf16[32,640]{1,0:T(8,128)(2,1)S(1)}, u32[]{:S(2)}, u32[]{:S(2)}) collective-permute-start(bf16[32,640]{1,0:T(8,128)(2,1)S(1)} %maximum_select_fusion.3), channel_id=1, source_target_pairs={{0,4},{1,5},{2,6},{3,7},{4,0},{5,1},{6,2},{7,3},{8,12},{9,13},{10,... | collective-permute-start | bytes 122888 | tf_op jit(solution)/shard_map/ppermute | solution.py:1080
  209.3 12.6 %collective-permute-start.8 = (bf16[1,512,512]{2,1,0:T(8,128)(2,1)S(1)}, bf16[1,512,512]{2,1,0:T(8,128)(2,1)S(1)}, u32[]{:S(2)}, u32[]{:S(2)}) collective-permute-start(bf16[1,512,512]{2,1,0:T(8,128)(2,1)S(1)} %add_convert_fusion.1), channel_id=1, source_target_pairs={{0,16},{8,24},{16,0},{24,8},{1,17},{9,25},{17,1},{25,9},{2,18},{10... | collective-permute-start | bytes 1572872 | tf_op jit(solution)/shard_map/ppermute | solution.py:1080
  210.8 4.5 %collective-permute-start.11 = (bf16[64,640]{1,0:T(8,128)(2,1)S(1)}, bf16[64,640]{1,0:T(8,128)(2,1)S(1)}, u32[]{:S(2)}, u32[]{:S(2)}) collective-permute-start(bf16[64,640]{1,0:T(8,128)(2,1)S(1)} %maximum_select_fusion.2), channel_id=1, source_target_pairs={{0,2},{1,3},{2,0},{3,1},{4,6},{5,7},{6,4},{7,5},{8,10},{9,11},{10,... | collective-permute-start | bytes 245768 | tf_op jit(solution)/shard_map/ppermute | solution.py:1080
  215.4 5.4 %collective-permute-start.12 = (bf16[128,640]{1,0:T(8,128)(2,1)S(1)}, bf16[128,640]{1,0:T(8,128)(2,1)S(1)}, u32[]{:S(2)}, u32[]{:S(2)}) collective-permute-start(bf16[128,640]{1,0:T(8,128)(2,1)S(1)} %maximum_select_fusion.1), channel_id=1, source_target_pairs={{0,1},{1,0},{2,3},{3,2},{4,5},{5,4},{6,7},{7,6},{8,9},{9,8},{10,11... | collective-permute-start | bytes 491528 | tf_op jit(solution)/shard_map/ppermute | solution.py:1080
  220.8 7.9 %copy-start.7 = (bf16[256,640]{1,0:T(8,128)(2,1)}, bf16[256,640]{1,0:T(8,128)(2,1)S(1)}, u32[]{:S(2)}) copy-start(bf16[256,640]{1,0:T(8,128)(2,1)S(1)} %maximum_select_fusion.own_ref) | copy-start | bytes 983044
  220.9 7.9 %collective-permute-start.13 = (bf16[256,640]{1,0:T(8,128)(2,1)S(1)}, bf16[256,640]{1,0:T(8,128)(2,1)S(1)}, u32[]{:S(2)}, u32[]{:S(2)}) collective-permute-start(bf16[256,640]{1,0:T(8,128)(2,1)S(1)} %maximum_select_fusion.own_ref), channel_id=1, source_target_pairs={{0,8},{8,0},{16,24},{24,16},{1,9},{9,1},{17,25},{25,17},{2,10},{10... | collective-permute-start | bytes 983048 | tf_op jit(solution)/shard_map/ppermute | solution.py:1080
  224.2 19.7 %all-to-all-start.6 = ((bf16[8,64,512]{2,1,0:T(8,128)(2,1)}), bf16[8,64,512]{2,1,0:T(8,128)(2,1)S(1)}, u32[]{:S(2)}, u32[]{:S(2)}) async-start(bf16[8,64,512]{2,1,0:T(8,128)(2,1)} %bitcast.5), calls=%async_computation.6 | async-start | bytes 1048576 | tf_op jit(solution)/shard_map/all_to_all | solution.py:1103
  243.9 19.4 %copy-start.2 = (f32[64,512]{1,0:T(8,128)}, f32[64,512]{1,0:T(8,128)S(1)}, u32[]{:S(2)}) copy-start(f32[64,512]{1,0:T(8,128)S(1)} %convert_reduce_fusion.grad_ref) | copy-start | bytes 393220
  244.8 18.5 %all-to-all-start.7 = ((bf16[8,64,512]{2,1,0:T(8,128)(2,1)}), bf16[8,64,512]{2,1,0:T(8,128)(2,1)S(1)}, u32[]{:S(2)}, u32[]{:S(2)}) async-start(bf16[8,64,512]{2,1,0:T(8,128)(2,1)} %broadcast_in_dim.8), calls=%async_computation.7 | async-start | bytes 1048576 | tf_op jit(solution)/shard_map/all_to_all | solution.py:1103
  266.4 17.3 %all-to-all-start.8 = ((bf16[8,48,512]{2,1,0:T(8,128)(2,1)}), bf16[8,48,512]{2,1,0:T(8,128)(2,1)S(1)}, u32[]{:S(2)}, u32[]{:S(2)}) async-start(bf16[8,48,512]{2,1,0:T(8,128)(2,1)} %collect_logits.1), calls=%async_computation.8 | async-start | bytes 786432 | tf_op jit(solution)/shard_map/all_to_all | solution.py:1103
  272.3 9.0 %collective-permute-start.14 = (bf16[10,128,128]{2,1,0:T(8,128)(2,1)}, bf16[10,128,128]{2,1,0:T(8,128)(2,1)S(1)}, u32[]{:S(2)}, u32[]{:S(2)}) collective-permute-start(bf16[10,128,128]{2,1,0:T(8,128)(2,1)} %mid_gram.1), channel_id=1, source_target_pairs={{0,16},{8,24},{16,0},{24,8},{1,17},{9,25},{17,1},{25,9},{2,18},{10... | collective-permute-start | bytes 983048 | tf_op jit(solution)/shard_map/ppermute | solution.py:1080
  277.7 3.6 %copy-start.6 = (bf16[10,128,128]{2,1,0:T(8,128)(2,1)S(1)}, bf16[10,128,128]{2,1,0:T(8,128)(2,1)}, u32[]{:S(2)}) copy-start(bf16[10,128,128]{2,1,0:T(8,128)(2,1)} %mid_gram.1) | copy-start | bytes 983044
  281.4 5.0 %copy-start.1 = (f32[10,128,128]{2,1,0:T(8,128)}, f32[10,128,128]{2,1,0:T(8,128)S(1)}, u32[]{:S(2)}) copy-start(f32[10,128,128]{2,1,0:T(8,128)S(1)} %convert_add_fusion.own_ref) | copy-start | bytes 1966084
  281.4 5.0 %collective-permute-start.15 = (f32[10,128,128]{2,1,0:T(8,128)S(1)}, f32[10,128,128]{2,1,0:T(8,128)S(1)}, u32[]{:S(2)}, u32[]{:S(2)}) collective-permute-start(f32[10,128,128]{2,1,0:T(8,128)S(1)} %convert_add_fusion.own_ref), channel_id=1, source_target_pairs={{0,8},{8,0},{16,24},{24,16},{1,9},{9,1},{17,25},{25,17},{2,10},{10... | collective-permute-start | bytes 1966088 | tf_op jit(solution)/shard_map/ppermute | solution.py:1080
  286.3 0.9 copy-start.9
  (5 other events, 3.9 us)

commit v3 on v2

--- a/solution.py
+++ b/solution.py
@@ -35,7 +35,8 @@
 rate_out = 0.04
 f32 = jnp.float32
 bf16 = jnp.bfloat16
-VMEM_LIMIT = 60 * 2**20
+VMEM_LIMIT = 50 * 2**20
+VMEM_WHOLE = 60 * 2**20
 
 
 def dot_on(first_arg, second_arg, first_dim, second_dim, precision=None):
@@ -48,8 +49,8 @@
     )
 
 
-def params():
-    return pltpu.CompilerParams(vmem_limit_bytes=VMEM_LIMIT)
+def params(limit=VMEM_LIMIT):
+    return pltpu.CompilerParams(vmem_limit_bytes=limit)
 
 
 def cost(microseconds):
@@ -186,11 +187,13 @@
     return order
 
 
-def gather_halves(own_ref, near_ref, held):
+def gather_quarters(refs, held):
     core = lax.rem(lax.axis_index("row"), 2)
-    size = own_ref.shape[0]
-    held[pl.ds(pl.multiple_of(core * size, size), size), :] = own_ref[...]
-    held[pl.ds(pl.multiple_of((1 - core) * size, size), size), :] = near_ref[...]
+    side = lax.rem(lax.axis_index("col"), 2)
+    size = refs[0].shape[0]
+    for index, ref in enumerate(refs):
+        place = (core ^ (index // 2)) * 2 + (side ^ (index % 2))
+        held[pl.ds(pl.multiple_of(place * size, size), size), :] = ref[...]
 
 
 def gather_pieces(refs, held):
@@ -673,19 +676,15 @@
     part_ref,
     stats_ref,
     window_ref,
-    own_ref,
-    near_ref,
-    out_ref,
-    inner,
-    base,
-    grads,
+    *refs,
 ):
+    out_ref, inner, base, grads = refs[4:]
     step = pl.program_id(0)
     block = x_ref.shape[1]
 
     @pl.when(step == 0)
     def _():
-        gather_halves(own_ref, near_ref, grads)
+        gather_quarters(refs[:4], grads)
         stats = add_up(stats_ref)
         for op in range(OPS):
             mean, scale = branch_scale(stats, op, all_rows)
@@ -713,7 +712,7 @@
     add_windows(moved, write)
 
 
-def rows_back_call(all_rows, counts, features, part, stats, window, halves, block):
+def rows_back_call(all_rows, counts, features, part, stats, window, quarters, block):
     total = features.shape[1]
     return pl.pallas_call(
         functools.partial(rows_back_body, all_rows),
@@ -726,7 +725,7 @@
                 fixed(stats.shape),
                 fixed((OPS, WINDOW, HID)),
             ]
-            + [fixed(half.shape) for half in halves],
+            + [fixed(part.shape) for part in quarters],
             out_specs=columns_of(VALID, block),
             scratch_shapes=[
                 pltpu.VMEM((OPS, WINDOW, WINDOW), bf16),
@@ -738,7 +737,7 @@
         compiler_params=params(),
         cost_estimate=cost(8),
         name="rows_back",
-    )(counts, features, part, stats, window, *halves)
+    )(counts, features, part, stats, window, *quarters)
 
 
 def slots_of(rows, peers):
@@ -870,33 +869,29 @@
     return beta_factor * old + (1.0 - beta_factor) * dot_on(low, low, dim, dim)
 
 
-def branch_update_body(
-    all_rows,
-    stats_ref,
-    window_ref,
-    own_ref,
-    near_ref,
-    w_ref,
-    left_ref,
-    right_ref,
-    basis_left_ref,
-    basis_right_ref,
-    first_ref,
-    second_ref,
-    new_left_ref,
-    new_right_ref,
-    new_first_ref,
-    new_second_ref,
-    new_w_ref,
-    low_w_ref,
-    grad_out_ref,
-    grads,
-):
+def branch_update_body(all_rows, stats_ref, window_ref, *refs):
+    (
+        w_ref,
+        left_ref,
+        right_ref,
+        basis_left_ref,
+        basis_right_ref,
+        first_ref,
+        second_ref,
+        new_left_ref,
+        new_right_ref,
+        new_first_ref,
+        new_second_ref,
+        new_w_ref,
+        low_w_ref,
+        grad_out_ref,
+        grads,
+    ) = refs[4:]
     step = pl.program_id(0)
 
     @pl.when(step == 0)
     def _():
-        gather_halves(own_ref, near_ref, grads)
+        gather_quarters(refs[:4], grads)
         for op in range(OPS):
             at = op * LANE + WINDOW + 1
             grad_out_ref[op * SHARE : (op + 1) * SHARE, :] = grads[at : at + SHARE, :HID].astype(f32)
@@ -932,7 +927,7 @@
 
 
 def branch_update_call(
-    all_rows, stats, window, halves, w, left, right, basis_left, basis_right, first, second
+    all_rows, stats, window, quarters, w, left, right, basis_left, basis_right, first, second
 ):
     small, wide = fixed((DIN, OPS, DIN)), fixed((DIN, OPS, HID))
     square = pl.BlockSpec((1, HID, HID), lambda k: (k, 0, 0))
@@ -940,7 +935,7 @@
         functools.partial(branch_update_body, all_rows),
         grid=(OPS,),
         in_specs=[fixed(stats.shape), fixed((OPS, WINDOW, HID))]
-        + [fixed(half.shape) for half in halves]
+        + [fixed(part.shape) for part in quarters]
         + [wide, small, square, small, square, wide, wide],
         out_specs=[small, square, wide, wide, wide, wide, fixed((CPAD, HID))],
         out_shape=[
@@ -953,10 +948,10 @@
             shape((CPAD, HID), f32),
         ],
         scratch_shapes=[pltpu.VMEM((OPS * LANE, HID + LANE), bf16)],
-        compiler_params=params(),
+        compiler_params=params(VMEM_WHOLE),
         cost_estimate=cost(12),
         name="branch_update",
-    )(stats, window, *halves, w, left, right, basis_left, basis_right, first, second)
+    )(stats, window, *quarters, w, left, right, basis_left, basis_right, first, second)
 
 
 def out_update_body(
@@ -1080,17 +1075,47 @@
     return lax.ppermute(values, axis, [(peer, peer ^ distance) for peer in range(peers)])
 
 
-def gather_by_doubling(values):
+def swap_both(values, first, second):
+    groups, peers = lax.axis_size("row"), lax.axis_size("col")
+    away = {"row": 0, "col": 0}
+    for axis, distance in (first, second):
+        away[axis] ^= distance
+    pairs = [
+        (row * peers + col, (row ^ away["row"]) * peers + (col ^ away["col"]))
+        for row in range(groups)
+        for col in range(peers)
+    ]
+    return lax.ppermute(values, BOTH, pairs)
+
+
+def in_order(values, other, step):
+    axis, distance = step
+    bit = lax.rem(lax.axis_index(axis) // distance, 2) > 0
+    return jnp.where(
+        bit,
+        jnp.concatenate([other, values], axis=0),
+        jnp.concatenate([values, other], axis=0),
+    )
+
+
+def gather_by_steps(values):
     steps = doubling_steps()
-    for axis, distance in steps[:-1]:
-        other = swap(values, axis, distance)
-        bit = lax.rem(lax.axis_index(axis) // distance, 2) > 0
-        values = jnp.where(
-            bit,
-            jnp.concatenate([other, values], axis=0),
-            jnp.concatenate([values, other], axis=0),
+    while len(steps) > 3:
+        first, second = steps[:2]
+        steps = steps[2:]
+        near, far, both = (
+            swap(values, *first),
+            swap(values, *second),
+            swap_both(values, first, second),
         )
-    return values, swap(values, *steps[-1])
+        values = in_order(
+            in_order(values, near, first), in_order(far, both, first), second
+        )
+    while len(steps) > 2:
+        values = in_order(values, swap(values, *steps[0]), steps[0])
+        steps = steps[1:]
+    first, second = steps
+    return [values, swap(values, *first), swap(values, *second), swap_both(values, first, second)]
 
 
 def add_all(values):
@@ -1220,12 +1245,12 @@
     kept, sent = parts[:2], parts[2:]
     grad_branch = jnp.sum(grad_branch.astype(f32), axis=0).astype(bf16)
     near = [swap(part, "row", 1) for part in sent]
-    halves = [half.reshape(-1, HID + LANE) for half in gather_by_doubling(grad_branch)]
+    quarters = [part.reshape(-1, HID + LANE) for part in gather_by_steps(grad_branch)]
     away = (kept[1] + near[1]).astype(bf16)
     far = swap(away, "row", groups // 2)
     grad_mid = finish_scatter(kept[0] + near[0] + far.astype(f32), 2)
     grad_features = rows_back_call(
-        all_rows, counts, turned, part, branch_stats, window, halves, 4096
+        all_rows, counts, turned, part, branch_stats, window, quarters, 4096
     )
     collected = collect_call(counts, after(dealt, grad_features))
     grad_mid, grad_features, collected = lax.optimization_barrier(
@@ -1236,7 +1261,7 @@
         all_rows,
         branch_stats,
         window,
-        halves,
+        quarters,
         by_input(w_branch),
         by_input(left_branch),
         right_branch,

time: 291 us -> 281 us (0.966)
  Pallas kernels: 178 us -> 163 us
  local copies, waits for them, and re-layouts: 6.52 us -> 10.9 us
    unnamed x28 -> x54, local copies, waits for them, and re-layouts: 4.83 us -> 9.17 us
  transfers between devices with their start and end apart: 23 -> 25, of which waited for: 13 -> 11; matrix products, arithmetic and copies ran while one was open for 2% -> 2% of each run, Pallas kernels for 40% -> 37%
where the time goes in v3:
time: 281 us; the launch traced here: 279 us
  Pallas kernels  163 us (58%)
  starting transfers between devices  50.9 us (18%)
  blocking collectives  23.9 us (9%)
  waiting for transfers between devices  23.2 us (8%)
  local copies, waits for them, and re-layouts  10.9 us (4%)
  other arithmetic  6.98 us (2%)
    pallas_call x1, Pallas kernels, branch_back_call(): pl.pallas_call(functools.partial(branch_back_body, all_rows), grid_spec=p...  42.9 us
    pallas_call x1, Pallas kernels, forward_call(): pl.pallas_call(functools.partial(forward_body, all_rows, count), grid_spe...  41.1 us
    all_to_all x5, starting transfers between devices, exchange(): return lax.all_to_all(values, 'col', 0, 0, tiled=True)  27 us
    pallas_call x1, Pallas kernels, mid_grad_call(): pl.pallas_call(mid_grad_body, grid=(total // block,), in_specs=[rows_of(b...  23.6 us
    pallas_call x1, Pallas kernels, head_call(): pl.pallas_call(functools.partial(head_body, all_rows), grid_spec=pltpu.Pr...  15.4 us
    pallas_call x1, Pallas kernels, branch_update_call(): pl.pallas_call(functools.partial(branch_update_body, all_rows), grid=(OPS...  14.8 us
    ppermute x16, starting transfers between devices, swap(): lax.ppermute(values, axis, [(peer, peer ^ distance) for peer in range(pee...  13.8 us
    ppermute x16, waiting for transfers between devices, swap(): lax.ppermute(values, axis, [(peer, peer ^ distance) for peer in range(pee...  13.4 us
  transfers between devices with their start and end apart: 25, of which 11 were waited for; matrix products, arithmetic and copies ran while one was open for 2% of the time, Pallas kernels for 37%

profile of v3, /device:TPU:0, one launch (start us, length us, event | category | flops | bytes accessed | tf_op | source)
XLA Modules:
  0.0 279.4 jit_solution(4412998774166383145)
XLA Ops:
  2.4 7.3 %all-to-all-start = ((bf16[8,64,512]{2,1,0:T(8,128)(2,1)}), bf16[8,64,512]{2,1,0:T(8,128)(2,1)S(1)}, u32[]{:S(2)}, u32[]{:S(2)}) async-start(bf16[8,64,512]{2,1,0:T(8,128)(2,1)} %broadcast_in_dim.6), calls=%async_computation | async-start | bytes 1048576 | tf_op jit(solution)/shard_map/all_to_all | solution.py:1128
  11.5 6.4 %row_moments.1 = (bf16[4,112,512]{2,1,0:T(8,128)(2,1)S(1)}, f32[4,128,128]{2,1,0:T(8,128)S(1)}, f32[8,640]{1,0:T(8,128)S(1)}) custom-call(s32[4,8]{1,0:T(4,128)S(1)} %copy-done.21, bf16[400,8192]{1,0:T(8,128)(2,1)} %bitcast.36, f32[100,4,512]{2,1,0:T(4,128)S(1)} %bitcast.29), custom_call_target="tpu_custom_call" | custom-call | flops 6000000000 | bytes 1 | tf_op jit(solution)/shard_map/row_moments/pallas_call | solution.py:243
  18.0 1.6 collective-permute-start.1
  19.9 2.0 collective-permute-done.1
  25.7 11.3 %all_to_all.45.refs_1_.stats_ref = f32[8,8,640]{2,1,0:T(8,128)S(1)} all-to-all(f32[8,8,640]{2,1,0:T(8,128)S(1)} %broadcast_in_dim.7), channel_id=1, replica_groups=mesh['row'=4,'col'=8] {'col'}, dimensions={0} | all-to-all | bytes 327680 | tf_op jit(solution)/shard_map/all_to_all | solution.py:1128
  39.7 41.1 %forward_layers.1 = (f32[8192,512]{1,0:T(8,128)}, bf16[8192,2048]{1,0:T(8,128)(2,1)}, bf16[8192,2048]{1,0:T(8,128)(2,1)}, bf16[2048,512]{1,0:T(8,128)(2,1)}, f32[32,8,128]{2,1,0:T(8,128)S(1)}) custom-call(s32[4,8]{1,0:T(4,128)S(1)} %copy-done.22, bf16[400,8192]{1,0:T(8,128)(2,1)} %bitcast.37, f32[8,8,640]{2,1,0:T(8,128)S(1)} %all_to_all.45.refs_1_.stats_ref, ...), custom_call_target="tpu_custom_call" | custom-call | flops 44000002048 | bytes 1 | tf_op jit(solution)/shard_map/forward_layers/pallas_call | solution.py:328
  80.7 12.6 %all_to_all.46.stats_ref.mid_stats_ref = f32[32,8,128]{2,1,0:T(8,128)S(1)} all-to-all(f32[32,8,128]{2,1,0:T(8,128)S(1)} %get-tuple-element.104), channel_id=1, replica_groups=mesh['row'=4,'col'=8] {'row','col'}, dimensions={0} | all-to-all | bytes 262144 | tf_op jit(solution)/shard_map/all_to_all | solution.py:1215
  93.4 15.4 %head.1 = (bf16[8192,512]{1,0:T(8,128)(2,1)}, bf16[48,8192]{1,0:T(8,128)(2,1)S(1)}, f32[48,512]{1,0:T(8,128)S(1)}, f32[32,8,128]{2,1,0:T(8,128)}) custom-call(s32[4,8]{1,0:T(4,128)S(1)} %copy-done.22, f32[8192,512]{1,0:T(8,128)} %get-tuple-element.103.pre_ref, f32[32,8,128]{2,1,0:T(8,128)S(1)} %all_to_all.46.stats_ref.mid_stats_ref, f32[47,512]{1,0:T(8,128)S(1)} %bitcast.30, ...), custom_call_target="tpu_custom_call" | custom-call | flops 17999998976 | bytes 1 | tf_op jit(solution)/shard_map/head/pallas_call | solution.py:436
  108.8 2.6 all-to-all-start.3
  111.3 1.8 deal_logits.1
  113.2 5.9 %all-to-all-done.3.sums_ref = f32[32,8,128]{2,1,0:T(8,128)S(1)} async-done(((f32[32,8,128]{2,1,0:T(8,128)}), f32[32,8,128]{2,1,0:T(8,128)S(1)}, u32[]{:S(2)}, u32[]{:S(2)}) %all-to-all-start.3) | async-done | bytes 131104 | tf_op jit(solution)/shard_map/all_to_all | solution.py:1219
  119.1 3.7 %all-to-all-start.4 = ((bf16[8,48,1152]{2,1,0:T(8,128)(2,1)}), bf16[8,48,1152]{2,1,0:T(8,128)(2,1)S(1)}, u32[]{:S(2)}, u32[]{:S(2)}) async-start(bf16[8,48,1152]{2,1,0:T(8,128)(2,1)} %deal_logits.1), calls=%async_computation.4 | async-start | bytes 1769472 | tf_op jit(solution)/shard_map/all_to_all | solution.py:1128
  122.8 1.6 copy-done.26
  124.4 42.9 %branch_back.1 = (bf16[8192,512]{1,0:T(8,128)(2,1)}, bf16[400,8192]{1,0:T(8,128)(2,1)}, bf16[32,16,640]{2,1,0:T(8,128)(2,1)}) custom-call(s32[4,8]{1,0:T(4,128)S(1)} %copy-done.22, f32[8192,512]{1,0:T(8,128)} %get-tuple-element.103.pre_ref, bf16[8192,512]{1,0:T(8,128)(2,1)} %get-tuple-element.105.back_ref, bf16[8192,2048]{1,0:T(8,128)(2,1)} %get-tuple-element.106.slope_ref, ...), custom_call_target="tpu_custom_call" | custom-call | flops 48000000000 | bytes 1 | tf_op jit(solution)/shard_map/branch_back/pallas_call | solution.py:591
  167.4 5.4 %all-to-all-start.5 = ((bf16[32,16,640]{2,1,0:T(8,128)(2,1)}), bf16[32,16,640]{2,1,0:T(8,128)(2,1)}, u32[]{:S(2)}, u32[]{:S(2)}) async-start(bf16[32,16,640]{2,1,0:T(8,128)(2,1)} %get-tuple-element.115), calls=%async_computation.5 | async-start | bytes 1310720 | tf_op jit(solution)/shard_map/all_to_all | solution.py:1242
  172.8 23.6 %mid_grad.1 = (f32[1,512,512]{2,1,0:T(8,128)S(1)}, f32[1,512,512]{2,1,0:T(8,128)S(1)}, f32[1,512,512]{2,1,0:T(8,128)S(1)}, f32[1,512,512]{2,1,0:T(8,128)}) custom-call(bf16[8192,512]{1,0:T(8,128)(2,1)} %get-tuple-element.116.mid_ref, bf16[8192,2048]{1,0:T(8,128)(2,1)} %get-tuple-element.117.joined_ref), custom_call_target="tpu_custom_call" | custom-call | flops 24999999488 | bytes 1 | tf_op jit(solution)/shard_map/mid_grad/pallas_call | solution.py:653
  199.1 2.7 collective-permute-start.10
  203.5 2.2 add_convert_fusion.1
  205.7 1.7 collective-permute-start.8
  207.5 1.5 collective-permute-start.12
  209.0 3.0 %collective-permute-done.12 = bf16[64,640]{1,0:T(8,128)(2,1)S(1)} collective-permute-done((bf16[64,640]{1,0:T(8,128)(2,1)S(1)}, bf16[64,640]{1,0:T(8,128)(2,1)S(1)}, u32[]{:S(2)}, u32[]{:S(2)}) %collective-permute-start.12) | collective-permute-done | bytes 81952 | tf_op jit(solution)/shard_map/ppermute | solution.py:1075
  214.3 4.9 %collective-permute-done.8 = bf16[1,512,512]{2,1,0:T(8,128)(2,1)} collective-permute-done((bf16[1,512,512]{2,1,0:T(8,128)(2,1)}, bf16[1,512,512]{2,1,0:T(8,128)(2,1)}, u32[]{:S(2)}, u32[]{:S(2)}) %collective-permute-start.8) | collective-permute-done | bytes 524320 | tf_op jit(solution)/shard_map/ppermute | solution.py:1075
  219.2 2.5 add_convert_fusion
  221.7 5.7 %all-to-all-start.6 = ((bf16[8,64,512]{2,1,0:T(8,128)(2,1)}), bf16[8,64,512]{2,1,0:T(8,128)(2,1)S(1)}, u32[]{:S(2)}, u32[]{:S(2)}) async-start(bf16[8,64,512]{2,1,0:T(8,128)(2,1)} %bitcast.35), calls=%async_computation.6 | async-start | bytes 1048576 | tf_op jit(solution)/shard_map/all_to_all | solution.py:1128
  228.6 8.4 %rows_back.1 = bf16[400,8192]{1,0:T(8,128)(2,1)} custom-call(s32[4,8]{1,0:T(4,128)S(1)} %copy-done.22, bf16[400,8192]{1,0:T(8,128)(2,1)} %bitcast.39, bf16[400,8192]{1,0:T(8,128)(2,1)} %get-tuple-element.126.part_ref, f32[8,8,640]{2,1,0:T(8,128)S(1)} %all_to_all.45.refs_1_.stats_ref, bf16[4,112,512]{2,1,0:T(8,128)(2,1)S(1)} %copy-done.24, ...), custom_call_target="tpu_custom_call" | custom-call | flops 8000000000 | bytes 1 | tf_op jit(solution)/shard_map/rows_back/pallas_call | solution.py:717
  237.0 1.6 collect_logits.1
  238.6 1.9 all-to-all-done.6
  241.4 4.1 %all-to-all-start.7 = ((bf16[8,64,512]{2,1,0:T(8,128)(2,1)}), bf16[8,64,512]{2,1,0:T(8,128)(2,1)S(1)}, u32[]{:S(2)}, u32[]{:S(2)}) async-start(bf16[8,64,512]{2,1,0:T(8,128)(2,1)} %broadcast_in_dim.8), calls=%async_computation.7 | async-start | bytes 1048576 | tf_op jit(solution)/shard_map/all_to_all | solution.py:1128
  245.5 14.8 %branch_update.1 = (f32[100,4,100]{2,1,0:T(4,128)}, f32[4,512,512]{2,1,0:T(8,128)}, f32[100,4,512]{2,1,0:T(4,128)}, f32[100,4,512]{2,1,0:T(4,128)}, f32[100,4,51...) custom-call(f32[8,8,640]{2,1,0:T(8,128)} %copy-done, bf16[4,112,512]{2,1,0:T(8,128)(2,1)} %copy-done.23, ...), custom_call_target="tpu_custom_call" | custom-call | flops 12000000000 | bytes 1 | tf_op jit(solution)/shard_map/branch_update/pallas_call | solution.py:934
  260.8 6.1 %all-to-all-start.8 = ((bf16[8,48,512]{2,1,0:T(8,128)(2,1)}), bf16[8,48,512]{2,1,0:T(8,128)(2,1)S(1)}, u32[]{:S(2)}, u32[]{:S(2)}) async-start(bf16[8,48,512]{2,1,0:T(8,128)(2,1)} %collect_logits.1), calls=%async_computation.8 | async-start | bytes 786432 | tf_op jit(solution)/shard_map/all_to_all | solution.py:1128
  272.0 2.3 out_update.1
  274.3 1.7 mid_update.1
  (103 shorter events, 28.2 us)
Async XLA Ops:
  2.4 21.7 %all-to-all-start = ((bf16[8,64,512]{2,1,0:T(8,128)(2,1)}), bf16[8,64,512]{2,1,0:T(8,128)(2,1)S(1)}, u32[]{:S(2)}, u32[]{:S(2)}) async-start(bf16[8,64,512]{2,1,0:T(8,128)(2,1)} %broadcast_in_dim.6), calls=%async_computation | async-start | bytes 1048576 | tf_op jit(solution)/shard_map/all_to_all | solution.py:1128
  11.5 28.2 %copy-start.22 = (s32[4,8]{1,0:T(4,128)S(1)}, s32[4,8]{1,0:T(4,128)}, u32[]{:S(2)}) copy-start(s32[4,8]{1,0:T(4,128)} %counts.13) | copy-start | bytes 388
  17.9 104.9 %copy-start.23 = (bf16[4,112,512]{2,1,0:T(8,128)(2,1)}, bf16[4,112,512]{2,1,0:T(8,128)(2,1)S(1)}, u32[]{:S(2)}) copy-start(bf16[4,112,512]{2,1,0:T(8,128)(2,1)S(1)} %get-tuple-element.100.refs_2_.window_ref) | copy-start | bytes 1376260
  17.9 1.9 collective-permute-start
  18.0 3.8 %collective-permute-start.1 = (f32[8,640]{1,0:T(8,128)S(1)}, f32[8,640]{1,0:T(8,128)S(1)}, u32[]{:S(2)}, u32[]{:S(2)}) collective-permute-start(f32[8,640]{1,0:T(8,128)S(1)} %get-tuple-element.97), channel_id=1, source_target_pairs={{0,16},{8,24},{16,0},{24,8},{1,17},{9,25},{17,1},{25,9},{2,18},{10... | collective-permute-start | bytes 61448 | tf_op jit(solution)/shard_map/ppermute | solution.py:1075
  19.6 3.2 %collective-permute-start.2 = (f32[8,640]{1,0:T(8,128)S(1)}, f32[8,640]{1,0:T(8,128)S(1)}, u32[]{:S(2)}, u32[]{:S(2)}) collective-permute-start(f32[8,640]{1,0:T(8,128)S(1)} %get-tuple-element.97), channel_id=1, source_target_pairs={{0,24},{8,16},{16,8},{24,0},{1,25},{9,17},{17,9},{25,1},{2,26},{10... | collective-permute-start | bytes 61448 | tf_op jit(solution)/shard_map/ppermute | solution.py:1075
  24.2 12.8 %collective-permute-start.3 = (bf16[512,512]{1,0:T(8,128)(2,1)S(1)}, bf16[512,512]{1,0:T(8,128)(2,1)S(1)}, u32[]{:S(2)}, u32[]{:S(2)}) collective-permute-start(bf16[512,512]{1,0:T(8,128)(2,1)S(1)} %bitcast.24), channel_id=1, source_target_pairs={{0,16},{8,24},{16,0},{24,8},{1,17},{9,25},{17,1},{25,9},{2,18},{10... | collective-permute-start | bytes 1572872 | tf_op jit(solution)/shard_map/ppermute | solution.py:1075
  37.0 190.5 %copy-start = (f32[8,8,640]{2,1,0:T(8,128)}, f32[8,8,640]{2,1,0:T(8,128)S(1)}, u32[]{:S(2)}) copy-start(f32[8,8,640]{2,1,0:T(8,128)S(1)} %all_to_all.45.refs_1_.stats_ref) | copy-start | bytes 491524
  37.0 1.9 collective-permute-start.4
  37.0 2.7 collective-permute-start.5
  39.7 53.7 %copy-start.14 = (f32[512,47]{0,1:T(8,128)S(1)}, f32[512,47]{0,1:T(8,128)}, u32[]{:S(2)}) copy-start(f32[512,47]{0,1:T(8,128)} %param.27) | copy-start | bytes 288772
  39.7 53.7 %copy-start.18 = (s32[8192]{0:T(1024)S(1)}, s32[8192]{0:T(1024)}, u32[]{:S(2)}) copy-start(s32[8192]{0:T(1024)} %param.23) | copy-start | bytes 98308
  108.8 10.3 %all-to-all-start.3 = ((f32[32,8,128]{2,1,0:T(8,128)}), f32[32,8,128]{2,1,0:T(8,128)S(1)}, u32[]{:S(2)}, u32[]{:S(2)}) async-start(f32[32,8,128]{2,1,0:T(8,128)} %get-tuple-element.108), calls=%async_computation.3 | async-start | bytes 262144 | tf_op jit(solution)/shard_map/all_to_all | solution.py:1219
  119.1 48.3 %all-to-all-start.4 = ((bf16[8,48,1152]{2,1,0:T(8,128)(2,1)}), bf16[8,48,1152]{2,1,0:T(8,128)(2,1)S(1)}, u32[]{:S(2)}, u32[]{:S(2)}) async-start(bf16[8,48,1152]{2,1,0:T(8,128)(2,1)} %deal_logits.1), calls=%async_computation.4 | async-start | bytes 1769472 | tf_op jit(solution)/shard_map/all_to_all | solution.py:1128
  167.4 30.0 %all-to-all-start.5 = ((bf16[32,16,640]{2,1,0:T(8,128)(2,1)}), bf16[32,16,640]{2,1,0:T(8,128)(2,1)}, u32[]{:S(2)}, u32[]{:S(2)}) async-start(bf16[32,16,640]{2,1,0:T(8,128)(2,1)} %get-tuple-element.115), calls=%async_computation.5 | async-start | bytes 1310720 | tf_op jit(solution)/shard_map/all_to_all | solution.py:1242
  197.4 6.2 %collective-permute-start.7 = (f32[1,512,512]{2,1,0:T(8,128)}, f32[1,512,512]{2,1,0:T(8,128)}, u32[]{:S(2)}, u32[]{:S(2)}) collective-permute-start(f32[1,512,512]{2,1,0:T(8,128)} %get-tuple-element.125), channel_id=1, source_target_pairs={{0,8},{8,0},{16,24},{24,16},{1,9},{9,1},{17,25},{25,17},{2,10},{10... | collective-permute-start | bytes 3145736 | tf_op jit(solution)/shard_map/ppermute | solution.py:1075
  197.6 16.7 %collective-permute-start.6 = (f32[1,512,512]{2,1,0:T(8,128)}, f32[1,512,512]{2,1,0:T(8,128)}, u32[]{:S(2)}, u32[]{:S(2)}) collective-permute-start(f32[1,512,512]{2,1,0:T(8,128)} %copy-done.7), channel_id=1, source_target_pairs={{0,8},{8,0},{16,24},{24,16},{1,9},{9,1},{17,25},{25,17},{2,10},{10... | collective-permute-start | bytes 3145736 | tf_op jit(solution)/shard_map/ppermute | solution.py:1075
  199.1 8.3 %collective-permute-start.10 = (bf16[16,640]{1,0:T(8,128)(2,1)S(1)}, bf16[16,640]{1,0:T(8,128)(2,1)S(1)}, u32[]{:S(2)}, u32[]{:S(2)}) collective-permute-start(bf16[16,640]{1,0:T(8,128)(2,1)S(1)} %reduce_sum.22), channel_id=1, source_target_pairs={{0,4},{1,5},{2,6},{3,7},{4,0},{5,1},{6,2},{7,3},{8,12},{9,13},{10,... | collective-permute-start | bytes 61448 | tf_op jit(solution)/shard_map/ppermute | solution.py:1075
  201.8 5.7 %collective-permute-start.9 = (bf16[16,640]{1,0:T(8,128)(2,1)S(1)}, bf16[16,640]{1,0:T(8,128)(2,1)S(1)}, u32[]{:S(2)}, u32[]{:S(2)}) collective-permute-start(bf16[16,640]{1,0:T(8,128)(2,1)S(1)} %reduce_sum.22), channel_id=1, source_target_pairs={{0,20},{1,21},{2,22},{3,23},{4,16},{5,17},{6,18},{7,19},{8,28},{9,... | collective-permute-start | bytes 61448 | tf_op jit(solution)/shard_map/ppermute | solution.py:1088
  203.2 4.2 %collective-permute-start.11 = (bf16[16,640]{1,0:T(8,128)(2,1)S(1)}, bf16[16,640]{1,0:T(8,128)(2,1)S(1)}, u32[]{:S(2)}, u32[]{:S(2)}) collective-permute-start(bf16[16,640]{1,0:T(8,128)(2,1)S(1)} %reduce_sum.22), channel_id=1, source_target_pairs={{0,16},{8,24},{16,0},{24,8},{1,17},{9,25},{17,1},{25,9},{2,18},{10... | collective-permute-start | bytes 61448 | tf_op jit(solution)/shard_map/ppermute | solution.py:1075
  205.7 13.5 %collective-permute-start.8 = (bf16[1,512,512]{2,1,0:T(8,128)(2,1)}, bf16[1,512,512]{2,1,0:T(8,128)(2,1)}, u32[]{:S(2)}, u32[]{:S(2)}) collective-permute-start(bf16[1,512,512]{2,1,0:T(8,128)(2,1)} %add_convert_fusion.1), channel_id=1, source_target_pairs={{0,16},{8,24},{16,0},{24,8},{1,17},{9,25},{17,1},{25,9},{2,18},{10... | collective-permute-start | bytes 1572872 | tf_op jit(solution)/shard_map/ppermute | solution.py:1075
  207.5 4.5 %collective-permute-start.12 = (bf16[64,640]{1,0:T(8,128)(2,1)S(1)}, bf16[64,640]{1,0:T(8,128)(2,1)S(1)}, u32[]{:S(2)}, u32[]{:S(2)}) collective-permute-start(bf16[64,640]{1,0:T(8,128)(2,1)S(1)} %maximum_select_fusion.1), channel_id=1, source_target_pairs={{0,2},{1,3},{2,0},{3,1},{4,6},{5,7},{6,4},{7,5},{8,10},{9,11},{10,... | collective-permute-start | bytes 245768 | tf_op jit(solution)/shard_map/ppermute | solution.py:1075
  212.0 24.9 %copy-start.1 = (bf16[128,640]{1,0:T(8,128)(2,1)}, bf16[128,640]{1,0:T(8,128)(2,1)S(1)}, u32[]{:S(2)}) copy-start(bf16[128,640]{1,0:T(8,128)(2,1)S(1)} %maximum_select_fusion.refs_0_) | copy-start | bytes 491524
  212.0 15.3 %collective-permute-start.13 = (bf16[128,640]{1,0:T(8,128)(2,1)S(1)}, bf16[128,640]{1,0:T(8,128)(2,1)S(1)}, u32[]{:S(2)}, u32[]{:S(2)}) collective-permute-start(bf16[128,640]{1,0:T(8,128)(2,1)S(1)} %maximum_select_fusion.refs_0_), channel_id=1, source_target_pairs={{0,1},{1,0},{2,3},{3,2},{4,5},{5,4},{6,7},{7,6},{8,9},{9,8},{10,11... | collective-permute-start | bytes 491528 | tf_op jit(solution)/shard_map/ppermute | solution.py:1075
  213.6 13.8 %collective-permute-start.14 = (bf16[128,640]{1,0:T(8,128)(2,1)S(1)}, bf16[128,640]{1,0:T(8,128)(2,1)S(1)}, u32[]{:S(2)}, u32[]{:S(2)}) collective-permute-start(bf16[128,640]{1,0:T(8,128)(2,1)S(1)} %maximum_select_fusion.refs_0_), channel_id=1, source_target_pairs={{0,8},{8,0},{16,24},{24,16},{1,9},{9,1},{17,25},{25,17},{2,10},{10... | collective-permute-start | bytes 491528 | tf_op jit(solution)/shard_map/ppermute | solution.py:1075
  213.6 13.8 %collective-permute-start.15 = (bf16[128,640]{1,0:T(8,128)(2,1)S(1)}, bf16[128,640]{1,0:T(8,128)(2,1)S(1)}, u32[]{:S(2)}, u32[]{:S(2)}) collective-permute-start(bf16[128,640]{1,0:T(8,128)(2,1)S(1)} %maximum_select_fusion.refs_0_), channel_id=1, source_target_pairs={{0,9},{1,8},{2,11},{3,10},{4,13},{5,12},{6,15},{7,14},{8,1},{9,0},... | collective-permute-start | bytes 491528 | tf_op jit(solution)/shard_map/ppermute | solution.py:1088
  221.7 18.7 %all-to-all-start.6 = ((bf16[8,64,512]{2,1,0:T(8,128)(2,1)}), bf16[8,64,512]{2,1,0:T(8,128)(2,1)S(1)}, u32[]{:S(2)}, u32[]{:S(2)}) async-start(bf16[8,64,512]{2,1,0:T(8,128)(2,1)} %bitcast.35), calls=%async_computation.6 | async-start | bytes 1048576 | tf_op jit(solution)/shard_map/all_to_all | solution.py:1128
  227.4 9.6 %copy-start.9 = (bf16[128,640]{1,0:T(8,128)(2,1)}, bf16[128,640]{1,0:T(8,128)(2,1)S(1)}, u32[]{:S(2)}) copy-start(bf16[128,640]{1,0:T(8,128)(2,1)S(1)} %collective-permute-done.13.refs_1_) | copy-start | bytes 491524
  241.4 19.0 %all-to-all-start.7 = ((bf16[8,64,512]{2,1,0:T(8,128)(2,1)}), bf16[8,64,512]{2,1,0:T(8,128)(2,1)S(1)}, u32[]{:S(2)}, u32[]{:S(2)}) async-start(bf16[8,64,512]{2,1,0:T(8,128)(2,1)} %broadcast_in_dim.8), calls=%async_computation.7 | async-start | bytes 1048576 | tf_op jit(solution)/shard_map/all_to_all | solution.py:1128
  260.8 16.1 %all-to-all-start.8 = ((bf16[8,48,512]{2,1,0:T(8,128)(2,1)}), bf16[8,48,512]{2,1,0:T(8,128)(2,1)S(1)}, u32[]{:S(2)}, u32[]{:S(2)}) async-start(bf16[8,48,512]{2,1,0:T(8,128)(2,1)} %collect_logits.1), calls=%async_computation.8 | async-start | bytes 786432 | tf_op jit(solution)/shard_map/all_to_all | solution.py:1128
  267.0 9.1 %collective-permute-start.16 = (bf16[10,128,128]{2,1,0:T(8,128)(2,1)S(1)}, bf16[10,128,128]{2,1,0:T(8,128)(2,1)S(1)}, u32[]{:S(2)}, u32[]{:S(2)}) collective-permute-start(bf16[10,128,128]{2,1,0:T(8,128)(2,1)S(1)} %mid_gram.1), channel_id=1, source_target_pairs={{0,16},{8,24},{16,0},{24,8},{1,17},{9,25},{17,1},{25,9},{2,18},{10... | collective-permute-start | bytes 983048 | tf_op jit(solution)/shard_map/ppermute | solution.py:1075
  276.1 2.2 collective-permute-start.17
  (20 other events, 72.2 us)

commit v4 on v3

--- a/solution.py
+++ b/solution.py
@@ -166,15 +166,12 @@
 
 def doubling_steps():
     steps = []
-    distance = lax.axis_size("row") // 2
-    while distance > 1:
-        steps.append(("row", distance))
-        distance //= 2
-    distance = lax.axis_size("col") // 2
-    while distance:
-        steps.append(("col", distance))
-        distance //= 2
-    return steps + [("row", 1)]
+    for axis in ("col", "row"):
+        distance = lax.axis_size(axis) // 2
+        while distance > 1:
+            steps.append((axis, distance))
+            distance //= 2
+    return steps + [("col", 1), ("row", 1)]
 
 
 def owned_order(devices):
@@ -1245,10 +1242,12 @@
     kept, sent = parts[:2], parts[2:]
     grad_branch = jnp.sum(grad_branch.astype(f32), axis=0).astype(bf16)
     near = [swap(part, "row", 1) for part in sent]
+    away = (kept[1] + near[1]).astype(bf16)
+    grad_branch, away = lax.optimization_barrier((grad_branch, away))
     quarters = [part.reshape(-1, HID + LANE) for part in gather_by_steps(grad_branch)]
-    away = (kept[1] + near[1]).astype(bf16)
     far = swap(away, "row", groups // 2)
-    grad_mid = finish_scatter(kept[0] + near[0] + far.astype(f32), 2)
+    base = after(kept[0] + near[0], away)
+    grad_mid = finish_scatter(base + far.astype(f32), 2)
     grad_features = rows_back_call(
         all_rows, counts, turned, part, branch_stats, window, quarters, 4096
     )

time: 281 us -> 288 us (1.025)
  waiting for transfers between devices: 23.2 us -> 30.8 us
    all_to_all x5, waiting for transfers between devices: 3.9 us -> 8.08 us  [exchange(): return lax.all_to_all(values, 'col', 0, 0, tiled=True)]
    ppermute x2, waiting for transfers between devices: 0.01 us -> 3.31 us  [swap_both(): return lax.ppermute(values, BOTH, pairs)]
  transfers between devices with their start and end apart: 25 -> 25, of which waited for: 11 -> 12; matrix products, arithmetic and copies ran while one was open for 2% -> 2% of each run, Pallas kernels for 37% -> 37%
where the time goes in v4:
time: 288 us; the launch traced here: 286 us
  Pallas kernels  163 us (57%)
  starting transfers between devices  50.3 us (17%)
  waiting for transfers between devices  30.8 us (11%)
  blocking collectives  23.9 us (8%)
  local copies, waits for them, and re-layouts  9.71 us (3%)
  other arithmetic  7.94 us (3%)
    pallas_call x1, Pallas kernels, branch_back_call(): pl.pallas_call(functools.partial(branch_back_body, all_rows), grid_spec=p...  43 us
    pallas_call x1, Pallas kernels, forward_call(): pl.pallas_call(functools.partial(forward_body, all_rows, count), grid_spe...  41.1 us
    all_to_all x5, starting transfers between devices, exchange(): return lax.all_to_all(values, 'col', 0, 0, tiled=True)  26.4 us
    pallas_call x1, Pallas kernels, mid_grad_call(): pl.pallas_call(mid_grad_body, grid=(total // block,), in_specs=[rows_of(b...  23.6 us
    pallas_call x1, Pallas kernels, head_call(): pl.pallas_call(functools.partial(head_body, all_rows), grid_spec=pltpu.Pr...  15.4 us
    ppermute x16, starting transfers between devices, swap(): lax.ppermute(values, axis, [(peer, peer ^ distance) for peer in range(pee...  15.1 us
    pallas_call x1, Pallas kernels, branch_update_call(): pl.pallas_call(functools.partial(branch_update_body, all_rows), grid=(OPS...  14.8 us
    ppermute x16, waiting for transfers between devices, swap(): lax.ppermute(values, axis, [(peer, peer ^ distance) for peer in range(pee...  13.5 us
  transfers between devices with their start and end apart: 25, of which 12 were waited for; matrix products, arithmetic and copies ran while one was open for 2% of the time, Pallas kernels for 37%

profile of v4, /device:TPU:0, one launch (start us, length us, event | category | flops | bytes accessed | tf_op | source)
XLA Modules:
  0.0 286.2 jit_solution(3525597910037430100)
XLA Ops:
  2.4 7.3 %all-to-all-start = ((bf16[8,64,512]{2,1,0:T(8,128)(2,1)}), bf16[8,64,512]{2,1,0:T(8,128)(2,1)S(1)}, u32[]{:S(2)}, u32[]{:S(2)}) async-start(bf16[8,64,512]{2,1,0:T(8,128)(2,1)} %broadcast_in_dim.6), calls=%async_computation | async-start | bytes 1048576 | tf_op jit(solution)/shard_map/all_to_all | solution.py:1125
  11.5 6.4 %row_moments.1 = (bf16[4,112,512]{2,1,0:T(8,128)(2,1)S(1)}, f32[4,128,128]{2,1,0:T(8,128)S(1)}, f32[8,640]{1,0:T(8,128)S(1)}) custom-call(s32[4,8]{1,0:T(4,128)S(1)} %copy-done.21, bf16[400,8192]{1,0:T(8,128)(2,1)} %bitcast.36, f32[100,4,512]{2,1,0:T(4,128)S(1)} %bitcast.29), custom_call_target="tpu_custom_call" | custom-call | flops 6000000000 | bytes 1 | tf_op jit(solution)/shard_map/row_moments/pallas_call | solution.py:240
  18.0 1.6 collective-permute-start.1
  19.9 2.0 collective-permute-done.1
  25.7 11.3 %all_to_all.45.refs_1_.stats_ref = f32[8,8,640]{2,1,0:T(8,128)S(1)} all-to-all(f32[8,8,640]{2,1,0:T(8,128)S(1)} %broadcast_in_dim.7), channel_id=1, replica_groups=mesh['row'=4,'col'=8] {'col'}, dimensions={0} | all-to-all | bytes 327680 | tf_op jit(solution)/shard_map/all_to_all | solution.py:1125
  39.7 41.1 %forward_layers.1 = (f32[8192,512]{1,0:T(8,128)}, bf16[8192,2048]{1,0:T(8,128)(2,1)}, bf16[8192,2048]{1,0:T(8,128)(2,1)}, bf16[2048,512]{1,0:T(8,128)(2,1)}, f32[32,8,128]{2,1,0:T(8,128)S(1)}) custom-call(s32[4,8]{1,0:T(4,128)S(1)} %copy-done.22, bf16[400,8192]{1,0:T(8,128)(2,1)} %bitcast.37, f32[8,8,640]{2,1,0:T(8,128)S(1)} %all_to_all.45.refs_1_.stats_ref, ...), custom_call_target="tpu_custom_call" | custom-call | flops 44000002048 | bytes 1 | tf_op jit(solution)/shard_map/forward_layers/pallas_call | solution.py:325
  80.7 12.6 %all_to_all.46.stats_ref.mid_stats_ref = f32[32,8,128]{2,1,0:T(8,128)S(1)} all-to-all(f32[32,8,128]{2,1,0:T(8,128)S(1)} %get-tuple-element.107), channel_id=1, replica_groups=mesh['row'=4,'col'=8] {'row','col'}, dimensions={0} | all-to-all | bytes 262144 | tf_op jit(solution)/shard_map/all_to_all | solution.py:1212
  93.4 15.4 %head.1 = (bf16[8192,512]{1,0:T(8,128)(2,1)}, bf16[48,8192]{1,0:T(8,128)(2,1)S(1)}, f32[48,512]{1,0:T(8,128)S(1)}, f32[32,8,128]{2,1,0:T(8,128)}) custom-call(s32[4,8]{1,0:T(4,128)S(1)} %copy-done.22, f32[8192,512]{1,0:T(8,128)} %get-tuple-element.106.pre_ref, f32[32,8,128]{2,1,0:T(8,128)S(1)} %all_to_all.46.stats_ref.mid_stats_ref, f32[47,512]{1,0:T(8,128)S(1)} %bitcast.30, ...), custom_call_target="tpu_custom_call" | custom-call | flops 17999998976 | bytes 1 | tf_op jit(solution)/shard_map/head/pallas_call | solution.py:433
  108.8 2.6 all-to-all-start.3
  111.3 1.8 deal_logits.1
  113.2 5.9 %all-to-all-done.3.sums_ref = f32[32,8,128]{2,1,0:T(8,128)S(1)} async-done(((f32[32,8,128]{2,1,0:T(8,128)}), f32[32,8,128]{2,1,0:T(8,128)S(1)}, u32[]{:S(2)}, u32[]{:S(2)}) %all-to-all-start.3) | async-done | bytes 131104 | tf_op jit(solution)/shard_map/all_to_all | solution.py:1216
  119.1 3.7 %all-to-all-start.4 = ((bf16[8,48,1152]{2,1,0:T(8,128)(2,1)}), bf16[8,48,1152]{2,1,0:T(8,128)(2,1)S(1)}, u32[]{:S(2)}, u32[]{:S(2)}) async-start(bf16[8,48,1152]{2,1,0:T(8,128)(2,1)} %deal_logits.1), calls=%async_computation.4 | async-start | bytes 1769472 | tf_op jit(solution)/shard_map/all_to_all | solution.py:1125
  122.8 1.6 copy-done.26
  124.4 43.0 %branch_back.1 = (bf16[8192,512]{1,0:T(8,128)(2,1)}, bf16[400,8192]{1,0:T(8,128)(2,1)}, bf16[32,16,640]{2,1,0:T(8,128)(2,1)}) custom-call(s32[4,8]{1,0:T(4,128)S(1)} %copy-done.22, f32[8192,512]{1,0:T(8,128)} %get-tuple-element.106.pre_ref, bf16[8192,512]{1,0:T(8,128)(2,1)} %get-tuple-element.108.back_ref, bf16[8192,2048]{1,0:T(8,128)(2,1)} %get-tuple-element.109.slope_ref, ...), custom_call_target="tpu_custom_call" | custom-call | flops 48000000000 | bytes 1 | tf_op jit(solution)/shard_map/branch_back/pallas_call | solution.py:588
  167.4 5.4 %all-to-all-start.5 = ((bf16[32,16,640]{2,1,0:T(8,128)(2,1)}), bf16[32,16,640]{2,1,0:T(8,128)(2,1)}, u32[]{:S(2)}, u32[]{:S(2)}) async-start(bf16[32,16,640]{2,1,0:T(8,128)(2,1)} %get-tuple-element.118), calls=%async_computation.5 | async-start | bytes 1310720 | tf_op jit(solution)/shard_map/all_to_all | solution.py:1239
  172.8 23.6 %mid_grad.1 = (f32[1,512,512]{2,1,0:T(8,128)S(1)}, f32[1,512,512]{2,1,0:T(8,128)S(1)}, f32[1,512,512]{2,1,0:T(8,128)S(1)}, f32[1,512,512]{2,1,0:T(8,128)}) custom-call(bf16[8192,512]{1,0:T(8,128)(2,1)} %get-tuple-element.119.mid_ref, bf16[8192,2048]{1,0:T(8,128)(2,1)} %get-tuple-element.120.joined_ref), custom_call_target="tpu_custom_call" | custom-call | flops 24999999488 | bytes 1 | tf_op jit(solution)/shard_map/mid_grad/pallas_call | solution.py:650
  200.4 2.2 add_convert_fusion.1
  202.6 2.6 collective-permute-start.11
  206.9 1.7 collective-permute-start.8
  208.9 3.3 %collective-permute-done.9 = bf16[16,640]{1,0:T(8,128)(2,1)S(1)} collective-permute-done((bf16[16,640]{1,0:T(8,128)(2,1)S(1)}, bf16[16,640]{1,0:T(8,128)(2,1)S(1)}, u32[]{:S(2)}, u32[]{:S(2)}) %collective-permute-start.9) | collective-permute-done | bytes 20512 | tf_op jit(solution)/shard_map/ppermute | solution.py:1085
  215.3 6.8 %collective-permute-done.12 = bf16[64,640]{1,0:T(8,128)(2,1)S(1)} collective-permute-done((bf16[64,640]{1,0:T(8,128)(2,1)S(1)}, bf16[64,640]{1,0:T(8,128)(2,1)S(1)}, u32[]{:S(2)}, u32[]{:S(2)}) %collective-permute-start.12) | collective-permute-done | bytes 81952 | tf_op jit(solution)/shard_map/ppermute | solution.py:1072
  222.1 1.7 collective-permute-start.13
  224.3 2.0 add_convert_fusion
  226.3 5.7 %all-to-all-start.6 = ((bf16[8,64,512]{2,1,0:T(8,128)(2,1)}), bf16[8,64,512]{2,1,0:T(8,128)(2,1)S(1)}, u32[]{:S(2)}, u32[]{:S(2)}) async-start(bf16[8,64,512]{2,1,0:T(8,128)(2,1)} %bitcast.35), calls=%async_computation.6 | async-start | bytes 1048576 | tf_op jit(solution)/shard_map/all_to_all | solution.py:1125
  232.1 8.4 %rows_back.1 = bf16[400,8192]{1,0:T(8,128)(2,1)} custom-call(s32[4,8]{1,0:T(4,128)S(1)} %copy-done.22, bf16[400,8192]{1,0:T(8,128)(2,1)} %bitcast.39, bf16[400,8192]{1,0:T(8,128)(2,1)} %get-tuple-element.132.part_ref, f32[8,8,640]{2,1,0:T(8,128)S(1)} %all_to_all.45.refs_1_.stats_ref, bf16[4,112,512]{2,1,0:T(8,128)(2,1)S(1)} %copy-done.24, ...), custom_call_target="tpu_custom_call" | custom-call | flops 8000000000 | bytes 1 | tf_op jit(solution)/shard_map/rows_back/pallas_call | solution.py:714
  242.1 4.6 %all-to-all-done.6 = bf16[8,64,512]{2,1,0:T(8,128)(2,1)S(1)} async-done(((bf16[8,64,512]{2,1,0:T(8,128)(2,1)}), bf16[8,64,512]{2,1,0:T(8,128)(2,1)S(1)}, u32[]{:S(2)}, u32[]{:S(2)}) %all-to-all-start.6) | async-done | bytes 524320 | tf_op jit(solution)/shard_map/all_to_all | solution.py:1125
  247.6 3.7 %all-to-all-start.7 = ((bf16[8,64,512]{2,1,0:T(8,128)(2,1)}), bf16[8,64,512]{2,1,0:T(8,128)(2,1)S(1)}, u32[]{:S(2)}, u32[]{:S(2)}) async-start(bf16[8,64,512]{2,1,0:T(8,128)(2,1)} %broadcast_in_dim.8), calls=%async_computation.7 | async-start | bytes 1048576 | tf_op jit(solution)/shard_map/all_to_all | solution.py:1125
  251.4 14.8 %branch_update.1 = (f32[100,4,100]{2,1,0:T(4,128)}, f32[4,512,512]{2,1,0:T(8,128)}, f32[100,4,512]{2,1,0:T(4,128)}, f32[100,4,512]{2,1,0:T(4,128)}, f32[100,4,51...) custom-call(f32[8,8,640]{2,1,0:T(8,128)} %copy-done, bf16[4,112,512]{2,1,0:T(8,128)(2,1)} %copy-done.23, ...), custom_call_target="tpu_custom_call" | custom-call | flops 12000000000 | bytes 1 | tf_op jit(solution)/shard_map/branch_update/pallas_call | solution.py:931
  266.7 6.0 %all-to-all-start.8 = ((bf16[8,48,512]{2,1,0:T(8,128)(2,1)}), bf16[8,48,512]{2,1,0:T(8,128)(2,1)S(1)}, u32[]{:S(2)}, u32[]{:S(2)}) async-start(bf16[8,48,512]{2,1,0:T(8,128)(2,1)} %collect_logits.1), calls=%async_computation.8 | async-start | bytes 786432 | tf_op jit(solution)/shard_map/all_to_all | solution.py:1125
  277.8 2.3 out_update.1
  280.1 1.7 mid_update.1
  282.0 2.1 all-to-all-done.8.pieces_ref
  (104 shorter events, 30.4 us)
Async XLA Ops:
  2.4 21.7 %all-to-all-start = ((bf16[8,64,512]{2,1,0:T(8,128)(2,1)}), bf16[8,64,512]{2,1,0:T(8,128)(2,1)S(1)}, u32[]{:S(2)}, u32[]{:S(2)}) async-start(bf16[8,64,512]{2,1,0:T(8,128)(2,1)} %broadcast_in_dim.6), calls=%async_computation | async-start | bytes 1048576 | tf_op jit(solution)/shard_map/all_to_all | solution.py:1125
  11.5 28.2 %copy-start.22 = (s32[4,8]{1,0:T(4,128)S(1)}, s32[4,8]{1,0:T(4,128)}, u32[]{:S(2)}) copy-start(s32[4,8]{1,0:T(4,128)} %counts.13) | copy-start | bytes 388
  17.9 104.9 %copy-start.23 = (bf16[4,112,512]{2,1,0:T(8,128)(2,1)}, bf16[4,112,512]{2,1,0:T(8,128)(2,1)S(1)}, u32[]{:S(2)}) copy-start(bf16[4,112,512]{2,1,0:T(8,128)(2,1)S(1)} %get-tuple-element.103.refs_2_.window_ref) | copy-start | bytes 1376260
  17.9 1.9 collective-permute-start
  18.0 3.8 %collective-permute-start.1 = (f32[8,640]{1,0:T(8,128)S(1)}, f32[8,640]{1,0:T(8,128)S(1)}, u32[]{:S(2)}, u32[]{:S(2)}) collective-permute-start(f32[8,640]{1,0:T(8,128)S(1)} %get-tuple-element.100), channel_id=1, source_target_pairs={{0,16},{8,24},{16,0},{24,8},{1,17},{9,25},{17,1},{25,9},{2,18},{10... | collective-permute-start | bytes 61448 | tf_op jit(solution)/shard_map/ppermute | solution.py:1072
  19.6 3.2 %collective-permute-start.2 = (f32[8,640]{1,0:T(8,128)S(1)}, f32[8,640]{1,0:T(8,128)S(1)}, u32[]{:S(2)}, u32[]{:S(2)}) collective-permute-start(f32[8,640]{1,0:T(8,128)S(1)} %get-tuple-element.100), channel_id=1, source_target_pairs={{0,24},{8,16},{16,8},{24,0},{1,25},{9,17},{17,9},{25,1},{2,26},{10... | collective-permute-start | bytes 61448 | tf_op jit(solution)/shard_map/ppermute | solution.py:1072
  24.2 12.8 %collective-permute-start.3 = (bf16[512,512]{1,0:T(8,128)(2,1)S(1)}, bf16[512,512]{1,0:T(8,128)(2,1)S(1)}, u32[]{:S(2)}, u32[]{:S(2)}) collective-permute-start(bf16[512,512]{1,0:T(8,128)(2,1)S(1)} %bitcast.24), channel_id=1, source_target_pairs={{0,16},{8,24},{16,0},{24,8},{1,17},{9,25},{17,1},{25,9},{2,18},{10... | collective-permute-start | bytes 1572872 | tf_op jit(solution)/shard_map/ppermute | solution.py:1072
  37.0 195.1 %copy-start = (f32[8,8,640]{2,1,0:T(8,128)}, f32[8,8,640]{2,1,0:T(8,128)S(1)}, u32[]{:S(2)}) copy-start(f32[8,8,640]{2,1,0:T(8,128)S(1)} %all_to_all.45.refs_1_.stats_ref) | copy-start | bytes 491524
  37.0 1.9 collective-permute-start.4
  37.0 2.7 collective-permute-start.5
  39.7 53.7 %copy-start.14 = (f32[512,47]{0,1:T(8,128)S(1)}, f32[512,47]{0,1:T(8,128)}, u32[]{:S(2)}) copy-start(f32[512,47]{0,1:T(8,128)} %param.27) | copy-start | bytes 288772
  39.7 53.7 %copy-start.18 = (s32[8192]{0:T(1024)S(1)}, s32[8192]{0:T(1024)}, u32[]{:S(2)}) copy-start(s32[8192]{0:T(1024)} %param.23) | copy-start | bytes 98308
  108.8 10.3 %all-to-all-start.3 = ((f32[32,8,128]{2,1,0:T(8,128)}), f32[32,8,128]{2,1,0:T(8,128)S(1)}, u32[]{:S(2)}, u32[]{:S(2)}) async-start(f32[32,8,128]{2,1,0:T(8,128)} %get-tuple-element.111), calls=%async_computation.3 | async-start | bytes 262144 | tf_op jit(solution)/shard_map/all_to_all | solution.py:1216
  119.1 48.3 %all-to-all-start.4 = ((bf16[8,48,1152]{2,1,0:T(8,128)(2,1)}), bf16[8,48,1152]{2,1,0:T(8,128)(2,1)S(1)}, u32[]{:S(2)}, u32[]{:S(2)}) async-start(bf16[8,48,1152]{2,1,0:T(8,128)(2,1)} %deal_logits.1), calls=%async_computation.4 | async-start | bytes 1769472 | tf_op jit(solution)/shard_map/all_to_all | solution.py:1125
  167.4 30.0 %all-to-all-start.5 = ((bf16[32,16,640]{2,1,0:T(8,128)(2,1)}), bf16[32,16,640]{2,1,0:T(8,128)(2,1)}, u32[]{:S(2)}, u32[]{:S(2)}) async-start(bf16[32,16,640]{2,1,0:T(8,128)(2,1)} %get-tuple-element.118), calls=%async_computation.5 | async-start | bytes 1310720 | tf_op jit(solution)/shard_map/all_to_all | solution.py:1239
  197.4 3.0 %collective-permute-start.7 = (f32[1,512,512]{2,1,0:T(8,128)}, f32[1,512,512]{2,1,0:T(8,128)}, u32[]{:S(2)}, u32[]{:S(2)}) collective-permute-start(f32[1,512,512]{2,1,0:T(8,128)} %get-tuple-element.129), channel_id=1, source_target_pairs={{0,8},{8,0},{16,24},{24,16},{1,9},{9,1},{17,25},{25,17},{2,10},{10... | collective-permute-start | bytes 3145736 | tf_op jit(solution)/shard_map/ppermute | solution.py:1072
  197.6 16.3 %collective-permute-start.6 = (f32[1,512,512]{2,1,0:T(8,128)}, f32[1,512,512]{2,1,0:T(8,128)}, u32[]{:S(2)}, u32[]{:S(2)}) collective-permute-start(f32[1,512,512]{2,1,0:T(8,128)} %copy-done.7), channel_id=1, source_target_pairs={{0,8},{8,0},{16,24},{24,16},{1,9},{9,1},{17,25},{25,17},{2,10},{10... | collective-permute-start | bytes 3145736 | tf_op jit(solution)/shard_map/ppermute | solution.py:1072
  202.6 29.6 %copy-start.24 = (bf16[4,112,512]{2,1,0:T(8,128)(2,1)S(1)}, bf16[4,112,512]{2,1,0:T(8,128)(2,1)}, u32[]{:S(2)}) copy-start(bf16[4,112,512]{2,1,0:T(8,128)(2,1)} %copy-done.23) | copy-start | bytes 1376260
  202.6 6.1 %collective-permute-start.11 = (bf16[16,640]{1,0:T(8,128)(2,1)S(1)}, bf16[16,640]{1,0:T(8,128)(2,1)S(1)}, u32[]{:S(2)}, u32[]{:S(2)}) collective-permute-start(bf16[16,640]{1,0:T(8,128)(2,1)S(1)} %reduce_sum.21), channel_id=1, source_target_pairs={{0,4},{1,5},{2,6},{3,7},{4,0},{5,1},{6,2},{7,3},{8,12},{9,13},{10,... | collective-permute-start | bytes 61448 | tf_op jit(solution)/shard_map/ppermute | solution.py:1072
  205.2 3.8 %collective-permute-start.10 = (bf16[16,640]{1,0:T(8,128)(2,1)S(1)}, bf16[16,640]{1,0:T(8,128)(2,1)S(1)}, u32[]{:S(2)}, u32[]{:S(2)}) collective-permute-start(bf16[16,640]{1,0:T(8,128)(2,1)S(1)} %reduce_sum.21), channel_id=1, source_target_pairs={{0,2},{1,3},{2,0},{3,1},{4,6},{5,7},{6,4},{7,5},{8,10},{9,11},{10,... | collective-permute-start | bytes 61448 | tf_op jit(solution)/shard_map/ppermute | solution.py:1072
  206.7 5.6 %collective-permute-start.9 = (bf16[16,640]{1,0:T(8,128)(2,1)S(1)}, bf16[16,640]{1,0:T(8,128)(2,1)S(1)}, u32[]{:S(2)}, u32[]{:S(2)}) collective-permute-start(bf16[16,640]{1,0:T(8,128)(2,1)S(1)} %reduce_sum.21), channel_id=1, source_target_pairs={{0,6},{1,7},{2,4},{3,5},{4,2},{5,3},{6,0},{7,1},{8,14},{9,15},{10,... | collective-permute-start | bytes 61448 | tf_op jit(solution)/shard_map/ppermute | solution.py:1085
  206.9 17.4 %collective-permute-start.8 = (bf16[1,512,512]{2,1,0:T(8,128)(2,1)}, bf16[1,512,512]{2,1,0:T(8,128)(2,1)}, u32[]{:S(2)}, u32[]{:S(2)}) collective-permute-start(bf16[1,512,512]{2,1,0:T(8,128)(2,1)} %add_convert_fusion.1), channel_id=1, source_target_pairs={{0,16},{8,24},{16,0},{24,8},{1,17},{9,25},{17,1},{25,9},{2,18},{10... | collective-permute-start | bytes 1572872 | tf_op jit(solution)/shard_map/ppermute | solution.py:1072
  212.3 9.8 %collective-permute-start.12 = (bf16[64,640]{1,0:T(8,128)(2,1)S(1)}, bf16[64,640]{1,0:T(8,128)(2,1)S(1)}, u32[]{:S(2)}, u32[]{:S(2)}) collective-permute-start(bf16[64,640]{1,0:T(8,128)(2,1)S(1)} %maximum_select_fusion.1), channel_id=1, source_target_pairs={{0,16},{8,24},{16,0},{24,8},{1,17},{9,25},{17,1},{25,9},{2,18},{10... | collective-permute-start | bytes 245768 | tf_op jit(solution)/shard_map/ppermute | solution.py:1072
  222.1 18.4 %copy-start.1 = (bf16[128,640]{1,0:T(8,128)(2,1)}, bf16[128,640]{1,0:T(8,128)(2,1)S(1)}, u32[]{:S(2)}) copy-start(bf16[128,640]{1,0:T(8,128)(2,1)S(1)} %maximum_select_fusion.refs_0_) | copy-start | bytes 491524
  222.1 9.9 %collective-permute-start.13 = (bf16[128,640]{1,0:T(8,128)(2,1)S(1)}, bf16[128,640]{1,0:T(8,128)(2,1)S(1)}, u32[]{:S(2)}, u32[]{:S(2)}) collective-permute-start(bf16[128,640]{1,0:T(8,128)(2,1)S(1)} %maximum_select_fusion.refs_0_), channel_id=1, source_target_pairs={{0,1},{1,0},{2,3},{3,2},{4,5},{5,4},{6,7},{7,6},{8,9},{9,8},{10,11... | collective-permute-start | bytes 491528 | tf_op jit(solution)/shard_map/ppermute | solution.py:1072
  223.9 8.2 %collective-permute-start.14 = (bf16[128,640]{1,0:T(8,128)(2,1)S(1)}, bf16[128,640]{1,0:T(8,128)(2,1)S(1)}, u32[]{:S(2)}, u32[]{:S(2)}) collective-permute-start(bf16[128,640]{1,0:T(8,128)(2,1)S(1)} %maximum_select_fusion.refs_0_), channel_id=1, source_target_pairs={{0,8},{8,0},{16,24},{24,16},{1,9},{9,1},{17,25},{25,17},{2,10},{10... | collective-permute-start | bytes 491528 | tf_op jit(solution)/shard_map/ppermute | solution.py:1072
  223.9 8.2 %collective-permute-start.15 = (bf16[128,640]{1,0:T(8,128)(2,1)S(1)}, bf16[128,640]{1,0:T(8,128)(2,1)S(1)}, u32[]{:S(2)}, u32[]{:S(2)}) collective-permute-start(bf16[128,640]{1,0:T(8,128)(2,1)S(1)} %maximum_select_fusion.refs_0_), channel_id=1, source_target_pairs={{0,9},{1,8},{2,11},{3,10},{4,13},{5,12},{6,15},{7,14},{8,1},{9,0},... | collective-permute-start | bytes 491528 | tf_op jit(solution)/shard_map/ppermute | solution.py:1085
  226.3 20.4 %all-to-all-start.6 = ((bf16[8,64,512]{2,1,0:T(8,128)(2,1)}), bf16[8,64,512]{2,1,0:T(8,128)(2,1)S(1)}, u32[]{:S(2)}, u32[]{:S(2)}) async-start(bf16[8,64,512]{2,1,0:T(8,128)(2,1)} %bitcast.35), calls=%async_computation.6 | async-start | bytes 1048576 | tf_op jit(solution)/shard_map/all_to_all | solution.py:1125
  247.6 18.6 %all-to-all-start.7 = ((bf16[8,64,512]{2,1,0:T(8,128)(2,1)}), bf16[8,64,512]{2,1,0:T(8,128)(2,1)S(1)}, u32[]{:S(2)}, u32[]{:S(2)}) async-start(bf16[8,64,512]{2,1,0:T(8,128)(2,1)} %broadcast_in_dim.8), calls=%async_computation.7 | async-start | bytes 1048576 | tf_op jit(solution)/shard_map/all_to_all | solution.py:1125
  266.7 17.4 %all-to-all-start.8 = ((bf16[8,48,512]{2,1,0:T(8,128)(2,1)}), bf16[8,48,512]{2,1,0:T(8,128)(2,1)S(1)}, u32[]{:S(2)}, u32[]{:S(2)}) async-start(bf16[8,48,512]{2,1,0:T(8,128)(2,1)} %collect_logits.1), calls=%async_computation.8 | async-start | bytes 786432 | tf_op jit(solution)/shard_map/all_to_all | solution.py:1125
  272.7 9.1 %collective-permute-start.16 = (bf16[10,128,128]{2,1,0:T(8,128)(2,1)S(1)}, bf16[10,128,128]{2,1,0:T(8,128)(2,1)S(1)}, u32[]{:S(2)}, u32[]{:S(2)}) collective-permute-start(bf16[10,128,128]{2,1,0:T(8,128)(2,1)S(1)} %mid_gram.1), channel_id=1, source_target_pairs={{0,16},{8,24},{16,0},{24,8},{1,17},{9,25},{17,1},{25,9},{2,18},{10... | collective-permute-start | bytes 983048 | tf_op jit(solution)/shard_map/ppermute | solution.py:1072
  281.9 3.2 %collective-permute-start.17 = (f32[10,128,128]{2,1,0:T(8,128)S(1)}, f32[10,128,128]{2,1,0:T(8,128)S(1)}, u32[]{:S(2)}, u32[]{:S(2)}) collective-permute-start(f32[10,128,128]{2,1,0:T(8,128)S(1)} %convert_add_fusion.own_ref), channel_id=1, source_target_pairs={{0,8},{8,0},{16,24},{24,16},{1,9},{9,1},{17,25},{25,17},{2,10},{10... | collective-permute-start | bytes 1966088 | tf_op jit(solution)/shard_map/ppermute | solution.py:1072
  (20 other events, 77.8 us)
